TPU v7x, 32 devices: a whole 2x2x4 slice. The times are simulated.
32 devices in a mesh: tok: 4 (over z), head: 8 (over y, x, core).
Axes of the slice: x: 2, y: 2, z: 4, core: 2. Of those that a mesh axis runs over, the one named last changes fastest.
Arguments:
- block_states: bfloat16 [1024, 2048], P('tok', 'head'), may hold values from -24 to 24
- token_ids: int32 [1024], replicated, may hold values from 0 to 100351
- accept: int32 [1024], P('tok'), may hold values 0 or 1
- cache_lengths: int32 [4], replicated, may hold values from 1 to 3072, as said below
- cache_keys: bfloat16 [4096, 2048], P('tok', 'head'), may hold values from -300 to 300
- cache_values: bfloat16 [4096, 2048], P('tok', 'head'), may hold values from -6 to 6
- w_query: bfloat16 [2048, 2048], P(None, 'head'), may hold values from -0.125 to 0.125
- w_key: bfloat16 [2048, 2048], P(None, 'head'), may hold values from -0.125 to 0.125
- w_value: bfloat16 [2048, 2048], P(None, 'head'), may hold values from -0.125 to 0.125
- w_out: bfloat16 [2048, 2048], P('head'), may hold values from -0.125 to 0.125
- attn_gain: float32 [2048], replicated, may hold values from 0.25 to 1.75
- final_gain: float32 [2048], replicated, may hold values from 0.25 to 1.75
- embed: bfloat16 [100352, 2048], P('tok', 'head'), may hold values from -6 to 6
- lm_head: bfloat16 [100352, 2048], P(('tok', 'head')), may hold values from -0.25 to 0.25
Outputs:
- hiddens: bfloat16 [1024, 2048], P(('tok', 'head'))
- request_norms: float32 [4], replicated
- top_logits: float32 [1024], replicated
Inputs may be any that keep to these rules, and one draw needn't show every extreme that they name: `cache_lengths`: each request has 1 or more cached positions; the counts sum to 4096 and the largest is exactly 3072.
All inputs are finite; a program needn't handle non-finite values. No bound on the sum of `accept` on one device may be relied on, other than what follows from the above.
Results may differ from a plain program's by a relative error of at most 0.0068.
Values may be sent and summed in bfloat16 or wider, within the bound.
No kernel may reach another device: no remote copies, remote signals or barrier semaphores. Data moves between devices by JAX's collectives and lax.ppermute only.
A program may use at most 192 MiB of HBM per device.

v0:
```python
import math

import jax
import jax.numpy as jnp
from jax import lax
from jax.sharding import PartitionSpec as P

HEAD_DIM = 128


EPSILON = 1e-06


def row_norm(values):
    return values * lax.rsqrt(jnp.mean(values * values, axis=-1, keepdims=True) + EPSILON)


def softmax_block(softmax_state, query_heads, key_block, value_block, valid_keys, score_scale):
    running_max, running_sum, running_acc = softmax_state
    scores = (
        jnp.einsum("qhd,khd->hqk", query_heads, key_block, preferred_element_type=jnp.float32)
        * score_scale
    )
    masked = jnp.where(valid_keys[None, None, :], scores, -1e30)
    new_max = jnp.maximum(running_max, jnp.max(masked, axis=-1))
    weights = jnp.where(valid_keys[None, None, :], jnp.exp(masked - new_max[:, :, None]), 0.0)
    factor = jnp.exp(running_max - new_max)
    running_sum = running_sum * factor + jnp.sum(weights, axis=-1)
    running_acc = running_acc * factor[:, :, None] + jnp.einsum(
        "hqk,khd->hqd", weights, value_block.astype(jnp.float32)
    )
    return (new_max, running_sum, running_acc)


def shards(
    block_states,
    token_ids,
    accept,
    cache_lengths,
    cache_keys,
    cache_values,
    w_query,
    w_key,
    w_value,
    w_out,
    attn_gain,
    final_gain,
    embed,
    lm_head,
):
    tok_index = lax.axis_index("tok")
    head_index = lax.axis_index("head")
    tok_count = lax.axis_size("tok")
    head_count = lax.axis_size("head")
    block_rows = block_states.shape[0]
    model_width = w_query.shape[0]
    local_width = w_query.shape[1]
    heads_here = local_width // HEAD_DIM
    share_rows = block_rows // head_count
    key_span = 512
    score_scale = 1.0 / math.sqrt(HEAD_DIM)
    offsets = jnp.cumsum(cache_lengths) - cache_lengths
    zero_rows = jnp.zeros((key_span, local_width), jnp.bfloat16)
    gathered_keys, gathered_values = (
        lax.all_gather(cache_keys, "tok", axis=0, tiled=True),
        lax.all_gather(cache_values, "tok", axis=0, tiled=True),
    )
    gathered_keys = jnp.concatenate([gathered_keys, zero_rows], axis=0)
    gathered_values = jnp.concatenate([gathered_values, zero_rows], axis=0)

    def attention(queries, key_rows, value_rows):
        query_heads = queries.reshape(block_rows, heads_here, HEAD_DIM)
        own_state = softmax_block(
            (
                jnp.full((heads_here, block_rows), -1e30, jnp.float32),
                jnp.zeros((heads_here, block_rows), jnp.float32),
                jnp.zeros((heads_here, block_rows, HEAD_DIM), jnp.float32),
            ),
            query_heads,
            key_rows.reshape(block_rows, heads_here, HEAD_DIM),
            value_rows.reshape(block_rows, heads_here, HEAD_DIM),
            jnp.ones((block_rows,), bool),
            score_scale,
        )
        request_begin = offsets[tok_index]
        request_length = cache_lengths[tok_index]
        block_count = (request_length + key_span - 1) // key_span

        def advance(turn_index, softmax_state):
            key_start = request_begin + turn_index * key_span
            key_block = lax.dynamic_slice_in_dim(gathered_keys, key_start, key_span, 0).reshape(
                key_span, heads_here, HEAD_DIM
            )
            value_block = lax.dynamic_slice_in_dim(gathered_values, key_start, key_span, 0).reshape(
                key_span, heads_here, HEAD_DIM
            )
            valid_keys = (
                turn_index * key_span + jnp.arange(key_span, dtype=jnp.int32) < request_length
            )
            return softmax_block(
                softmax_state, query_heads, key_block, value_block, valid_keys, score_scale
            )

        final_state = lax.fori_loop(0, block_count, advance, own_state)
        running_max, running_sum, running_acc = final_state
        result = running_acc / running_sum[:, :, None]
        return (
            jnp.transpose(result, (1, 0, 2)).reshape(block_rows, local_width).astype(jnp.bfloat16)
        )

    def run_layer(features):
        piece_cols = lax.all_gather(features, "head", axis=1, tiled=True)
        query_acc = jnp.dot(piece_cols, w_query, preferred_element_type=jnp.float32)
        key_acc = jnp.dot(piece_cols, w_key, preferred_element_type=jnp.float32)
        value_acc = jnp.dot(piece_cols, w_value, preferred_element_type=jnp.float32)
        own_rows = lax.dynamic_slice_in_dim(piece_cols, head_index * share_rows, share_rows, 0)
        residual = own_rows
        query_acc, key_acc, value_acc, residual = (query_acc, key_acc, value_acc, residual)
        attended = attention(
            query_acc.astype(jnp.bfloat16),
            key_acc.astype(jnp.bfloat16),
            value_acc.astype(jnp.bfloat16),
        )
        projected = lax.psum_scatter(
            jnp.dot(attended, w_out, preferred_element_type=jnp.float32),
            "head",
            scatter_dimension=0,
            tiled=True,
        )
        return (residual.astype(jnp.float32) + row_norm(projected) * attn_gain).astype(jnp.bfloat16)

    first_pass = run_layer(block_states)
    row_piece = lax.all_gather(first_pass, ("tok", "head"), axis=0, tiled=True)
    piece_rows = row_piece.shape[0]
    widened = row_piece.astype(jnp.float32)
    row_squares = jnp.sum(widened * widened, axis=-1)
    normed = (row_norm(widened) * final_gain).astype(jnp.bfloat16)
    logits = lax.dot_general(
        normed, lm_head, (((1,), (1,)), ((), ())), preferred_element_type=jnp.float32
    )
    best = jnp.max(logits, axis=1)
    owners = jnp.arange(piece_rows, dtype=jnp.int32) // block_rows
    one_hot = (owners[:, None] == jnp.arange(tok_count, dtype=jnp.int32)[None, :]).astype(
        jnp.float32
    )
    square_sums = jnp.dot(row_squares, one_hot, precision=lax.Precision.HIGHEST)
    top_local, square_sums = (best, square_sums)
    top_logits = lax.pmax(top_local, ("tok", "head"))
    request_norms = jnp.sqrt(square_sums / (block_rows * model_width))
    vocab_here = embed.shape[0]
    local_ids = token_ids - tok_index * vocab_here
    inside_vocab = (local_ids >= 0) & (local_ids < vocab_here)
    looked_up = jnp.take(embed, jnp.clip(local_ids, 0, vocab_here - 1), axis=0)
    looked_up = jnp.where(inside_vocab[:, None], looked_up, jnp.zeros_like(looked_up)).astype(
        jnp.float32
    )
    embedded = lax.psum_scatter(
        looked_up.astype(jnp.bfloat16), "tok", scatter_dimension=0, tiled=True
    )
    swapped = jnp.where((accept == 1)[:, None], embedded, block_states)
    hiddens = run_layer(swapped)
    return (hiddens, request_norms, top_logits)


def solution(mesh):
    placed = (
        P("tok", "head"),
        P(),
        P("tok"),
        P(),
        P("tok", "head"),
        P("tok", "head"),
        P(None, "head"),
        P(None, "head"),
        P(None, "head"),
        P("head", None),
        P(),
        P(),
        P("tok", "head"),
        P(("tok", "head"), None),
    )
    return jax.shard_map(
        shards,
        mesh=mesh,
        in_specs=placed,
        out_specs=(P(("tok", "head"), None), P(), P()),
        check_vma=False,
    )
```

profile of v0, /device:TPU:0, one launch (start us, length us, event | category | flops | bytes accessed | tf_op | source)
XLA Modules:
  0.0 413.7 jit_solution(9196764718751126944)
XLA Ops:
  8.1 0.8 compare_and_fusion.1
  8.9 0.7 fusion.34
  9.6 9.9 %gather_fusion = bf16[1024,256]{1,0:T(8,128)(2,1)S(1)} fusion(bf16[25088,256]{1,0:T(8,128)(2,1)} %param.30, s32[1024]{0:T(1024)S(1)} %fusion.34), kind=kCustom, calls=%fused_computation | custom fusion | bytes 1052672 | tf_op jit(solution)/shard_map/jit(_take)/gather | solution.py:153
  19.5 1.2 select_select_fusion
  20.7 0.0 all-gather.12.cloned.1.call-start
  20.7 0.5 all-gather.12.cloned.1.call-update
  21.3 23.9 %reduce-scatter.4.cloned.1.call-done = bf16[256,256]{1,0:T(8,128)(2,1)} async-done(((bf16[1024,256]{1,0:T(8,128)(2,1)}), bf16[256,256]{1,0:T(8,128)(2,1)}) %reduce-scatter.4.cloned.1.call-update) | async-done | bytes 131088 | tf_op jit(solution)/shard_map/reduce_scatter | solution.py:157
  45.2 1.7 broadcast_select_fusion
  46.9 0.0 all-gather.8.cloned.1.call-start
  46.9 1.0 copy.39
  48.0 0.0 all-gather.10.cloned.1.call-start
  48.0 2.1 copy.40
  50.1 0.0 reduce-scatter.6.cloned.1.call-start
  50.2 0.6 dynamic_slice.27
  51.4 0.2 reduce-window.9
  51.6 0.6 dynamic_slice.28
  52.3 1.8 convolution_convert_fusion.2
  54.1 2.1 convolution_convert_fusion.1
  56.2 0.3 fusion.39
  56.5 0.1 copy.47
  56.6 0.1 fusion.27
  56.7 1.8 convolution_convert_fusion
  58.5 0.3 convolution_add_fusion.2
  58.8 16.1 %all-gather.6.cloned.1.call-done = bf16[256,2048]{1,0:T(8,128)(2,1)} async-done(((bf16[256,256]{1,0:T(8,128)(2,1)}), bf16[256,2048]{1,0:T(8,128)(2,1)}) %all-gather.6.cloned.1.call-update) | async-done | bytes 1048592 | tf_op jit(solution)/shard_map/all_gather | solution.py:112
  74.9 2.8 convolution_convert_fusion.5
  77.7 1.7 copy.41
  79.4 2.1 convolution_convert_fusion.4
  81.5 1.2 fusion.40
  82.7 0.1 fusion.26
  82.8 1.8 convolution_convert_fusion.3
  84.6 0.3 convolution_add_fusion.3
  84.9 37.0 %all-gather.8.cloned.1.call-done = bf16[4096,256]{0,1:T(8,128)(2,1)} async-done(((bf16[1024,256]{0,1:T(8,128)(2,1)}), bf16[4096,256]{0,1:T(8,128)(2,1)}) %all-gather.8.cloned.1.call-update) | async-done | bytes 2097168 | tf_op jit(solution)/shard_map/all_gather | solution.py:65
  122.0 3.2 concatenate.6
  125.1 42.8 %all-gather.10.cloned.1.call-done = bf16[4096,256]{0,1:T(8,128)(2,1)} async-done(((bf16[1024,256]{0,1:T(8,128)(2,1)}), bf16[4096,256]{0,1:T(8,128)(2,1)}) %all-gather.10.cloned.1.call-update) | async-done | bytes 2097168 | tf_op jit(solution)/shard_map/all_gather | solution.py:66
  167.9 3.2 concatenate.7
  171.1 3.8 while.28
  171.7 1.3 constant_dynamic-slice_fusion.6
  173.1 0.7 add_compare_fusion.4
  173.8 0.4 fusion.86
  174.1 0.2 fusion.87
  174.4 0.5 convolution_add_fusion.6
  174.9 0.1 copy.42
  175.1 1.8 fusion.41
  177.0 0.0 reduce-scatter.8.cloned.1.call-start
  177.0 4.0 while.29
  177.7 1.3 constant_dynamic-slice_fusion.7
  179.0 0.7 add_compare_fusion.5
  179.7 0.4 fusion.91
  180.0 0.2 fusion.92
  180.3 0.5 convolution_add_fusion.7
  181.0 0.1 copy.48
  181.2 1.8 fusion.42
  183.0 0.0 all-gather.14.cloned.1.call-start
  183.1 52.9 %reduce-scatter.6.cloned.1.call-done = f32[32,2048]{1,0:T(8,128)} async-done(((f32[256,2048]{1,0:T(8,128)}), f32[32,2048]{1,0:T(8,128)}) %reduce-scatter.6.cloned.1.call-update) | async-done | bytes 262160 | tf_op jit(solution)/shard_map/reduce_scatter | solution.py:124
  236.0 1.1 multiply_reduce_fusion.1
  237.1 43.7 %reduce-scatter.8.cloned.1.call-done = f32[32,2048]{1,0:T(8,128)} async-done(((f32[256,2048]{1,0:T(8,128)}), f32[32,2048]{1,0:T(8,128)}) %reduce-scatter.8.cloned.1.call-update) | async-done | bytes 262160 | tf_op jit(solution)/shard_map/reduce_scatter | solution.py:124
  280.8 1.1 multiply_reduce_fusion
  281.9 1.9 add_convert_fusion
  283.9 62.1 %all-gather.14.cloned.1.call-done = bf16[1024,2048]{1,0:T(8,128)(2,1)} async-done(((bf16[32,2048]{1,0:T(8,128)(2,1)}), bf16[1024,2048]{1,0:T(8,128)(2,1)}) %all-gather.14.cloned.1.call-update) | async-done | bytes 4194320 | tf_op jit(solution)/shard_map/all_gather | solution.py:133
  346.0 3.2 fusion.14
  349.3 0.2 copy-done.4
  349.5 16.7 %fusion.21 = f32[1024]{0:T(1024)S(1)} fusion(bf16[3136,2048]{1,0:T(8,128)(2,1)} %param.31, bf16[1024,2048]{1,0:T(8,128)(2,1)S(1)} %copy-done.4, f32[2048]{0:T(1024)S(1)} %copy-done.9, f32[1024]{0:T(1024)S(1)} %add_rsqrt_fusion), kind=kOutput, calls=%fused_computation.39 | convolution fusion | flops 13164936192 | bytes 17055744 | tf_op jit(solution)/shard_map/dot_general | solution.py:138
  366.2 39.2 %pmax.7 = f32[1024]{0:T(1024)} all-reduce(f32[1024]{0:T(1024)S(1)} %fusion.21), channel_id=1, replica_groups=mesh['tok'=4,'head'=8] {'tok','head'}, use_global_device_ids=true, to_apply=%region_20.21 | all-reduce | flops 1024 | bytes 8192 | tf_op jit(solution)/shard_map/pmax | solution.py:148
  405.4 0.9 fusion.25
  (51 shorter events, 0.4 us)
Async XLA Ops:
  8.0 167.1 %copy-start = (bf16[256,2048]{1,0:T(8,128)(2,1)S(1)}, bf16[256,2048]{1,0:T(8,128)(2,1)}, u32[]{:S(2)}) copy-start(bf16[256,2048]{1,0:T(8,128)(2,1)} %param.27) | copy-start | bytes 3145732
  8.0 37.2 %copy-start.7 = (bf16[256,256]{1,0:T(8,128)(2,1)S(1)}, bf16[256,256]{1,0:T(8,128)(2,1)}, u32[]{:S(2)}) copy-start(bf16[256,256]{1,0:T(8,128)(2,1)} %param.18) | copy-start | bytes 393220
  8.0 13.3 %copy-start.10 = (s32[256]{0:T(256)S(1)}, s32[256]{0:T(256)}, u32[]{:S(2)}) copy-start(s32[256]{0:T(256)} %param.20) | copy-start | bytes 3076
  8.0 38.9 %copy-start.6 = (bf16[1024,256]{1,0:T(8,128)(2,1)S(1)}, bf16[1024,256]{1,0:T(8,128)(2,1)}, u32[]{:S(2)}) copy-start(bf16[1024,256]{1,0:T(8,128)(2,1)} %param.22) | copy-start | bytes 1572868
  8.0 37.1 %reduce-scatter.4.cloned.1.call-start = ((), (), s32[]{:S(2)}) async-start(), calls=%async_computation.3 | async-start | bytes 655360 | tf_op jit(solution)/shard_map/reduce_scatter | solution.py:157
  9.6 40.6 %copy-start.11 = (s32[4]{0:T(128)S(1)}, s32[4]{0:T(128)}, u32[]{:S(2)}) copy-start(s32[4]{0:T(128)} %param.21) | copy-start | bytes 52
  9.6 42.6 %copy-start.5 = (bf16[2048,256]{1,0:T(8,128)(2,1)S(1)}, bf16[2048,256]{1,0:T(8,128)(2,1)}, u32[]{:S(2)}) copy-start(bf16[2048,256]{1,0:T(8,128)(2,1)} %param.24) | copy-start | bytes 3145732
  20.7 31.6 %all-gather.12.cloned.1.call-start = ((), (), s32[]{:S(2)}) async-start(), calls=%async_computation.8 | async-start | bytes 1179648 | tf_op jit(solution)/shard_map/all_gather | solution.py:112
  21.2 53.7 %all-gather.6.cloned.1.call-start = ((), (), s32[]{:S(2)}) async-start(), calls=%async_computation.4 | async-start | bytes 1179648 | tf_op jit(solution)/shard_map/all_gather | solution.py:112
  46.9 75.1 %all-gather.8.cloned.1.call-start = ((), (), s32[]{:S(2)}) async-start(), calls=%async_computation.5 | async-start | bytes 2621440 | tf_op jit(solution)/shard_map/all_gather | solution.py:65
  48.0 120.0 %all-gather.10.cloned.1.call-start = ((), (), s32[]{:S(2)}) async-start(), calls=%async_computation.6 | async-start | bytes 2621440 | tf_op jit(solution)/shard_map/all_gather | solution.py:66
  50.1 185.9 %reduce-scatter.6.cloned.1.call-start = ((), (), s32[]{:S(2)}) async-start(), calls=%async_computation.7 | async-start | bytes 2359296 | tf_op jit(solution)/shard_map/reduce_scatter | solution.py:124
  52.3 4.4 %copy-start.1 = (bf16[256,2048]{1,0:T(8,128)(2,1)S(1)}, bf16[256,2048]{1,0:T(8,128)(2,1)}, u32[]{:S(2)}) copy-start(bf16[256,2048]{1,0:T(8,128)(2,1)} %all-gather.12.cloned.1.call-done) | copy-start | bytes 3145732
  74.9 7.9 %copy-start.2 = (bf16[256,2048]{1,0:T(8,128)(2,1)S(1)}, bf16[256,2048]{1,0:T(8,128)(2,1)}, u32[]{:S(2)}) copy-start(bf16[256,2048]{1,0:T(8,128)(2,1)} %all-gather.6.cloned.1.call-done) | copy-start | bytes 3145732
  84.9 86.2 %copy-start.3 = (bf16[256,2,128]{2,0,1:T(8,128)(2,1)S(1)}, bf16[256,2,128]{2,0,1:T(8,128)(2,1)}, u32[]{:S(2)}) copy-start(bf16[256,2,128]{2,0,1:T(8,128)(2,1)} %copy.41) | copy-start | bytes 393220
  177.0 103.9 %reduce-scatter.8.cloned.1.call-start = ((), (), s32[]{:S(2)}) async-start(), calls=%async_computation.9 | async-start | bytes 2359296 | tf_op jit(solution)/shard_map/reduce_scatter | solution.py:124
  181.0 100.9 %copy-start.8 = (f32[2048]{0:T(1024)S(1)}, f32[2048]{0:T(1024)}, u32[]{:S(2)}) copy-start(f32[2048]{0:T(1024)} %param.28) | copy-start | bytes 24580
  183.0 166.2 %copy-start.9 = (f32[2048]{0:T(1024)S(1)}, f32[2048]{0:T(1024)}, u32[]{:S(2)}) copy-start(f32[2048]{0:T(1024)} %param.29) | copy-start | bytes 24580
  183.0 163.0 %all-gather.14.cloned.1.call-start = ((), (), s32[]{:S(2)}) async-start(), calls=%async_computation.10 | async-start | bytes 4325376 | tf_op jit(solution)/shard_map/all_gather | solution.py:133
  346.0 3.4 copy-start.4
Sparse Core Ops, SparseCore 0:
  20.8 24.3 reduce-scatter.3
  284.0 61.9 all-gather.13
Sparse Core Ops, SparseCore 1:
  23.0 26.1 all-gather.11
  51.5 23.4 all-gather.5
  76.4 45.5 all-gather.7
  123.5 44.3 all-gather.9
  177.0 58.9 reduce-scatter.5
  239.7 41.1 reduce-scatter.7
where the time goes:
time: 415 us; the launch traced here: 414 us
  waiting for transfers between devices  279 us (67%)
  blocking collectives  39.2 us (9%)
  matrix products  37.5 us (9%)
  local copies, waits for them, and re-layouts  25.5 us (6%)
  between operations  16.5 us (4%)
  other arithmetic  13.8 us (3%)
    reduce_scatter x2, waiting for transfers between devices, run_layer(): lax.psum_scatter(jnp.dot(attended, w_out, preferred_element_type=jnp.floa...  96.7 us
    all_gather x1, waiting for transfers between devices, shards(): row_piece = lax.all_gather(first_pass, ('tok', 'head'), axis=0, tiled=True)  62.1 us
    all_gather x1, waiting for transfers between devices, shards(): lax.all_gather(cache_values, 'tok', axis=0, tiled=True)  42.8 us
    pmax x1, blocking collectives, shards(): top_logits = lax.pmax(top_local, ('tok', 'head'))  39.2 us
    all_gather x1, waiting for transfers between devices, shards(): lax.all_gather(cache_keys, 'tok', axis=0, tiled=True)  37 us
    reduce_scatter x1, waiting for transfers between devices, shards(): lax.psum_scatter(looked_up.astype(jnp.bfloat16), 'tok', scatter_dimension...  23.9 us
    dot_general x1, matrix products, shards(): lax.dot_general(normed, lm_head, (((1,), (1,)), ((), ())), preferred_elem...  16.7 us
    all_gather x2, waiting for transfers between devices, run_layer(): piece_cols = lax.all_gather(features, 'head', axis=1, tiled=True)  16.2 us
  transfers between devices with their start and end apart: 8, of which 7 were waited for; matrix products, arithmetic and copies ran while one was open for 8% of the time, Pallas kernels for 0%

commit v1 on v0

v1 whole, which is shorter than its diff:
```python
import functools
import math

import jax
import jax.numpy as jnp
from jax import lax
from jax.experimental import pallas as pl
from jax.experimental.pallas import tpu as pltpu
from jax.sharding import PartitionSpec as P

HEAD_DIM = 128
EPSILON = 1e-06
LOWEST = -1e30
BF16 = jnp.bfloat16
F32 = jnp.float32

SMEM = pl.BlockSpec(memory_space=pltpu.SMEM)
VMEM = pl.BlockSpec(memory_space=pltpu.VMEM)


def params(mib=48):
    return pltpu.CompilerParams(vmem_limit_bytes=mib * 2**20)


def cost(flops, moved):
    return pl.CostEstimate(flops=flops, bytes_accessed=moved, transcendentals=0)


def xor_pairs(size, mask):
    return [(i, i ^ mask) for i in range(size)]


def project_kernel(place, *refs):
    *pieces, wq, wk, wv, q_out, k_out, v_out, res_out, x = refs
    head = place[1]
    width = pieces[0].shape[1]
    for mask, piece in enumerate(pieces):
        at = pl.multiple_of(jnp.bitwise_xor(head, mask) * width, width)
        x[:, pl.ds(at, width)] = piece[...]
    for w, out in ((wq, q_out), (wk, k_out), (wv, v_out)):
        out[...] = jnp.dot(x[...], w[...], preferred_element_type=F32).astype(BF16)
    share = res_out.shape[0]
    res_out[...] = x[pl.ds(pl.multiple_of(head * share, share), share), :]


def project(place, pieces, wq, wk, wv):
    rows, width = pieces[0].shape
    full = wq.shape[0]
    share = rows // len(pieces)
    tile = jax.ShapeDtypeStruct((rows, width), BF16)
    return pl.pallas_call(
        project_kernel,
        out_shape=(tile, tile, tile, jax.ShapeDtypeStruct((share, full), BF16)),
        in_specs=[SMEM] + [VMEM] * (len(pieces) + 3),
        out_specs=(VMEM,) * 4,
        scratch_shapes=[pltpu.VMEM((rows, full), BF16)],
        compiler_params=params(),
        cost_estimate=cost(6 * rows * full * width, 8 * full * width),
        name="project",
    )(place, *pieces, wq, wk, wv)


def key_range(place, request, chunk_rows, tok_count):
    begin = jnp.int32(0)
    length = jnp.int32(0)
    for i in range(tok_count):
        begin += jnp.where(i < request, place[2 + i], 0)
        length += jnp.where(i == request, place[2 + i], 0)
    begin -= place[0] * chunk_rows
    low = jnp.clip(begin, 0, chunk_rows)
    high = jnp.clip(begin + length, 0, chunk_rows)
    return low, high


def absorb(state, query, keys, values, valid):
    top, acc = state
    factor = math.log2(math.e) / math.sqrt(HEAD_DIM)
    scores = lax.dot_general(query, keys, (((1,), (1,)), ((), ())), preferred_element_type=F32)
    if valid is not None:
        scores = jnp.where(valid, scores, LOWEST)
    new_top = jnp.maximum(top, jnp.max(scores, axis=1, keepdims=True))
    weights = jnp.exp2((scores - new_top) * factor).astype(BF16)
    wide = jnp.concatenate([values, jnp.ones_like(values)], axis=1)
    acc = acc * jnp.exp2((top - new_top) * factor) + jnp.dot(weights, wide, preferred_element_type=F32)
    return new_top, acc


def cached_states(place, request, query, keys, values, tok_count):
    rows, width = query.shape
    chunk_rows = keys.shape[0]
    heads = width // HEAD_DIM
    span = min(512, chunk_rows)
    low, high = key_range(place, request, chunk_rows, tok_count)
    first = low // span
    last = jnp.where(high > low, (high + span - 1) // span, first)

    def step(block, states):
        start = pl.multiple_of(block * span, span)
        spots = start + lax.broadcasted_iota(jnp.int32, (rows, span), 1)
        valid = (spots >= low) & (spots < high)
        out = []
        for j in range(heads):
            cols = slice(j * HEAD_DIM, (j + 1) * HEAD_DIM)
            out.append(
                absorb(states[j], query[:, cols], keys[pl.ds(start, span), cols], values[pl.ds(start, span), cols], valid)
            )
        return tuple(out)

    empty = (jnp.full((rows, 1), LOWEST, F32), jnp.zeros((rows, 2 * HEAD_DIM), F32))
    return lax.fori_loop(first, last, step, (empty,) * heads)


def settle(state):
    top, acc = state
    total = acc[:, HEAD_DIM:]
    some = total > 0.0
    safe = jnp.where(some, total, 1.0)
    log_sum = jnp.where(some, top * (1.0 / math.sqrt(HEAD_DIM)) + jnp.log(safe), LOWEST)
    return acc[:, :HEAD_DIM] / safe, log_sum


def own_kernel(tok_count, place, query, new_keys, new_values, keys, values, mixed_out, log_out):
    states = cached_states(place, place[0], query, keys, values, tok_count)
    for j, state in enumerate(states):
        cols = slice(j * HEAD_DIM, (j + 1) * HEAD_DIM)
        state = absorb(state, query[:, cols], new_keys[:, cols], new_values[:, cols], None)
        mixed, log_sum = settle(state)
        mixed_out[:, cols] = mixed
        log_out[:, cols] = log_sum


def own_part(tok_count, place, query, new_keys, new_values, keys, values):
    rows, width = query.shape
    shape = jax.ShapeDtypeStruct((rows, width), F32)
    return pl.pallas_call(
        functools.partial(own_kernel, tok_count),
        out_shape=(shape, shape),
        in_specs=[SMEM] + [VMEM] * 5,
        out_specs=(VMEM, VMEM),
        compiler_params=params(),
        cost_estimate=cost(4 * rows * width * keys.shape[0], 4 * keys.shape[0] * width),
        name="own_part",
    )(place, query, new_keys, new_values, keys, values)


def away_kernel(tok_count, masks, place, *refs):
    queries, (keys, values), outs = refs[: len(masks)], refs[len(masks) : len(masks) + 2], refs[len(masks) + 2 :]
    for mask, query, out in zip(masks, queries, outs, strict=True):
        rows, width = query.shape
        heads = width // HEAD_DIM
        request = jnp.bitwise_xor(place[0], mask)
        states = cached_states(place, request, query, keys, values, tok_count)
        pieces = []
        for j, state in enumerate(states):
            mixed, log_sum = settle(state)
            out[:rows, j * HEAD_DIM : (j + 1) * HEAD_DIM] = mixed.astype(BF16)
            rest = jnp.transpose(log_sum)[:1, :]
            for _ in range(3):
                piece = rest.astype(BF16).astype(F32)
                pieces.append(piece)
                rest = rest - piece
        at = lax.broadcasted_iota(jnp.int32, (16, rows), 0)
        tail = jnp.zeros((16, rows), F32)
        for i, piece in enumerate(pieces):
            tail = jnp.where(at == i, piece, tail)
        out[rows:, :] = tail.astype(BF16)


def away_parts(tok_count, masks, place, queries, keys, values):
    rows, width = queries[0].shape
    message = jax.ShapeDtypeStruct((rows + 16, width), BF16)
    return pl.pallas_call(
        functools.partial(away_kernel, tok_count, masks),
        out_shape=(message,) * len(masks),
        in_specs=[SMEM] + [VMEM] * (len(masks) + 2),
        out_specs=(VMEM,) * len(masks),
        compiler_params=params(),
        cost_estimate=cost(4 * rows * width * keys.shape[0], 4 * keys.shape[0] * width),
        name="away_parts",
    )(place, *queries, keys, values)


def combine_kernel(share, place, mixed, logs, *refs):
    *messages, keep_out, send_out, whole = refs
    rows, width = mixed.shape
    tails = [message[rows:, :].astype(F32) for message in messages]
    for j in range(width // HEAD_DIM):
        cols = slice(j * HEAD_DIM, (j + 1) * HEAD_DIM)
        parts = [(mixed[:, cols], logs[:, cols])]
        for message, tail in zip(messages, tails, strict=True):
            row = tail[3 * j : 3 * j + 1] + tail[3 * j + 1 : 3 * j + 2] + tail[3 * j + 2 : 3 * j + 3]
            log_sum = jnp.transpose(jnp.broadcast_to(row, (HEAD_DIM, rows)))
            parts.append((message[:rows, cols].astype(F32), log_sum))
        top = functools.reduce(jnp.maximum, [log_sum for _, log_sum in parts])
        total, acc = 0.0, 0.0
        for part, log_sum in parts:
            weight = jnp.exp(log_sum - top)
            total += weight
            acc += weight * part
        whole[:, cols] = (acc / total).astype(BF16)
    head = place[1]
    core = jnp.bitwise_and(head, 1)
    for slot in range(keep_out.shape[0] // share):
        pair = jnp.bitwise_xor(head, 2 * slot) - core
        at = pl.multiple_of((pair + core) * share, share)
        other = pl.multiple_of((pair + 1 - core) * share, share)
        keep_out[slot * share : (slot + 1) * share, :] = whole[pl.ds(at, share), :]
        send_out[slot * share : (slot + 1) * share, :] = whole[pl.ds(other, share), :]


def combine(share, place, mixed, logs, messages):
    rows, width = mixed.shape
    half = jax.ShapeDtypeStruct((rows // 2, width), BF16)
    return pl.pallas_call(
        functools.partial(combine_kernel, share),
        out_shape=(half, half),
        in_specs=[SMEM] + [VMEM] * (len(messages) + 2),
        out_specs=(VMEM, VMEM),
        scratch_shapes=[pltpu.VMEM((rows, width), BF16)],
        compiler_params=params(),
        cost_estimate=cost(rows * width * 40, rows * width * 16),
        name="combine",
    )(place, mixed, logs, *messages)


def out_kernel(keep, other, w_keep, w_other, *outs):
    share = outs[0].shape[0]
    total = jnp.dot(keep[...], w_keep[...], preferred_element_type=F32)
    total += jnp.dot(other[...], w_other[...], preferred_element_type=F32)
    for slot, out in enumerate(outs):
        out[...] = total[slot * share : (slot + 1) * share].astype(out.dtype)


def out_project(share, keep, other, w_keep, w_other):
    half, width = keep.shape
    full = w_keep.shape[1]
    return pl.pallas_call(
        out_kernel,
        out_shape=tuple(jax.ShapeDtypeStruct((share, full), F32 if s == 0 else BF16) for s in range(half // share)),
        in_specs=[VMEM] * 4,
        out_specs=(VMEM,) * (half // share),
        compiler_params=params(),
        cost_estimate=cost(4 * half * width * full, 4 * width * full),
        name="out_project",
    )(keep, other, w_keep, w_other)


def finish_kernel(last, own, *refs):
    *others, residual, attn_gain, final_gain, first_out = refs[: len(refs) - (0 if last else 2)]
    total = own[...]
    for other in others:
        total += other[...].astype(F32)
    scale = lax.rsqrt(jnp.mean(total * total, axis=1, keepdims=True) + EPSILON)
    first = (residual[...].astype(F32) + total * scale * attn_gain[...]).astype(BF16)
    first_out[...] = first
    if not last:
        normed_out, square_out = refs[-2:]
        wide = first.astype(F32)
        squares = jnp.sum(wide * wide, axis=1, keepdims=True)
        scale = lax.rsqrt(squares / wide.shape[1] + EPSILON)
        normed_out[...] = (wide * scale * final_gain[...]).astype(BF16)
        square_out[...] = jnp.broadcast_to(jnp.sum(squares, axis=0, keepdims=True), square_out.shape)


def finish(last, own, others, residual, attn_gain, final_gain):
    state = jax.ShapeDtypeStruct(residual.shape, BF16)
    outs = (state,) if last else (state, state, jax.ShapeDtypeStruct((1, 128), F32))
    return pl.pallas_call(
        functools.partial(finish_kernel, last),
        out_shape=outs,
        in_specs=[VMEM] * (len(others) + 4),
        out_specs=(VMEM,) * len(outs),
        compiler_params=params(),
        cost_estimate=cost(residual.size * 20, residual.size * 12),
        name="finish",
    )(own, *others, residual, attn_gain, final_gain)


def logits_kernel(share, tok_count, place, mine, other, lm_block, best_out, x):
    @pl.when(pl.program_id(0) == 0)
    def _():
        core = jnp.bitwise_and(place[1], 1)
        for flag, piece in enumerate((mine, other)):
            for slot in range(tok_count):
                tok = jnp.bitwise_xor(place[0], slot)
                at = pl.multiple_of((2 * tok + jnp.bitwise_xor(core, flag)) * share, share)
                x[pl.ds(at, share), :] = piece[slot * share : (slot + 1) * share, :]
        best_out[...] = jnp.full(best_out.shape, -jnp.inf, F32)

    logits = lax.dot_general(lm_block[...], x[...], (((1,), (1,)), ((), ())), preferred_element_type=F32)
    best = jnp.max(logits.reshape(logits.shape[0] // 8, 8, logits.shape[1]), axis=0)
    best_out[...] = jnp.maximum(best_out[...], best)


def largest_logits(share, tok_count, place, mine, other, lm_head):
    half, full = mine.shape
    vocab = lm_head.shape[0]
    span = vocab // 7
    return pl.pallas_call(
        functools.partial(logits_kernel, share, tok_count),
        out_shape=jax.ShapeDtypeStruct((8, 2 * half), F32),
        grid=(vocab // span,),
        in_specs=[SMEM, VMEM, VMEM, pl.BlockSpec((span, full), lambda i: (i, 0))],
        out_specs=VMEM,
        scratch_shapes=[pltpu.VMEM((2 * half, full), BF16)],
        compiler_params=params(),
        cost_estimate=cost(4 * half * full * vocab, 2 * full * vocab),
        name="largest_logits",
    )(place, mine, other, lm_head)


def gather_best_kernel(place, square, *refs):
    *bests, out = refs
    chip = place[1] // 2
    out[...] = jnp.zeros(out.shape, F32)
    for slot, best in enumerate(bests):
        out[pl.ds(jnp.bitwise_xor(chip, slot), 1), :] = jnp.max(best[...], axis=0, keepdims=True)
    lanes = lax.broadcasted_iota(jnp.int32, (1, out.shape[1]), 1)
    out[len(bests) : len(bests) + 1, :] = jnp.where(lanes == place[0], square[:, :1], 0.0)


def gather_best(place, square, bests):
    rows = -(-(len(bests) + 1) // 8) * 8
    return pl.pallas_call(
        gather_best_kernel,
        out_shape=jax.ShapeDtypeStruct((rows, bests[0].shape[1]), F32),
        in_specs=[SMEM] + [VMEM] * (1 + len(bests)),
        out_specs=VMEM,
        compiler_params=params(),
        name="gather_best",
    )(place, square, *bests)


def shards(
    block_states,
    token_ids,
    accept,
    cache_lengths,
    cache_keys,
    cache_values,
    w_query,
    w_key,
    w_value,
    w_out,
    attn_gain,
    final_gain,
    embed,
    lm_head,
):
    tok_index = lax.axis_index("tok")
    head_index = lax.axis_index("head")
    tok_count = lax.axis_size("tok")
    head_count = lax.axis_size("head")
    chips = head_count // 2
    block_rows = block_states.shape[0]
    share = block_rows // head_count
    model_width = w_query.shape[0]
    place = jnp.concatenate([jnp.stack([tok_index, head_index]).astype(jnp.int32), cache_lengths])
    gains = (attn_gain.reshape(1, -1), final_gain.reshape(1, -1))
    tok_masks = range(1, tok_count)

    def by_head(value, mask):
        return lax.ppermute(value, "head", xor_pairs(head_count, mask))

    def by_tok(value, mask):
        return lax.ppermute(value, "tok", xor_pairs(tok_count, mask))

    def run_layer(features, last):
        chip_pieces = [features] + [by_head(features, 2 * s) for s in range(1, chips)]
        core_pieces = [by_head(piece, 1) for piece in chip_pieces]
        pieces = [piece for pair in zip(chip_pieces, core_pieces, strict=True) for piece in pair]
        query, key, value, residual = project(place, pieces, w_query, w_key, w_value)
        queries = [by_tok(query, mask) for mask in tok_masks]
        mixed, logs = own_part(tok_count, place, query, key, value, cache_keys, cache_values)
        messages = away_parts(tok_count, tok_masks, place, queries, cache_keys, cache_values)
        messages = [by_tok(message, mask) for mask, message in zip(tok_masks, messages, strict=True)]
        keep, send = combine(share, place, mixed, logs, messages)
        own, *sums = out_project(share, keep, by_head(send, 1), w_out, w_out_other)
        sums = [by_head(total, 2 * s) for s, total in enumerate(sums, 1)]
        return finish(last, own, sums, residual, *gains)

    w_out_other = by_head(w_out, 1)

    _, normed, square = run_layer(block_states, False)

    vocab_here = embed.shape[0]
    local_ids = jnp.clip(token_ids - tok_index * vocab_here, 0, vocab_here - 1).reshape(tok_count, block_rows)
    owners = lax.dynamic_slice_in_dim(token_ids, tok_index * block_rows, block_rows, 0) // vocab_here
    chosen = block_states
    for mask in range(tok_count):
        other = jnp.bitwise_xor(tok_index, mask)
        ids = lax.dynamic_slice_in_dim(local_ids, other, 1, 0)[0]
        found = jnp.take(embed, ids, axis=0, mode="clip")
        if mask:
            found = by_tok(found, mask)
        chosen = jnp.where(((accept == 1) & (owners == other))[:, None], found, chosen)
    (hiddens,) = run_layer(chosen, True)

    column = jnp.concatenate([normed] + [by_tok(normed, mask) for mask in tok_masks], axis=0)
    if chips == 4:
        along_x, along_y = by_head(column, 2), by_head(column, 4)
        half = column.shape[0] // 2
        across = jnp.concatenate([by_head(along_y[:half], 2), by_head(along_x[half:], 4)], axis=0)
        columns = [column, along_x, along_y, across]
    else:
        columns = [column] + [by_head(column, 2 * s) for s in range(1, chips)]
    bests = [largest_logits(share, tok_count, place, piece, by_head(piece, 1), lm_head) for piece in columns]
    best = gather_best(place, square, bests)
    is_max = lax.broadcasted_iota(jnp.int32, best.shape, 0) < chips
    for axis, size in (("head", head_count), ("tok", tok_count)):
        mask = 1
        while mask < size:
            other = lax.ppermute(best, axis, xor_pairs(size, mask))
            best = jnp.where(is_max, jnp.maximum(best, other), best + other)
            mask *= 2
    top_logits = best[:chips].reshape(chips, tok_count, 2, share).transpose(1, 0, 2, 3).reshape(-1)
    request_norms = jnp.sqrt(best[chips, :tok_count] / (block_rows * model_width))
    return (hiddens, request_norms, top_logits)


def solution(mesh):
    placed = (
        P("tok", "head"),
        P(),
        P("tok"),
        P(),
        P("tok", "head"),
        P("tok", "head"),
        P(None, "head"),
        P(None, "head"),
        P(None, "head"),
        P("head", None),
        P(),
        P(),
        P("tok", "head"),
        P(("tok", "head"), None),
    )
    return jax.shard_map(
        shards,
        mesh=mesh,
        in_specs=placed,
        out_specs=(P(("tok", "head"), None), P(), P()),
        check_vma=False,
    )
```

time: 415 us -> 213 us (0.51)
  waiting for transfers between devices: 279 us -> 50.2 us
  Pallas kernels: 0 us -> 56.6 us
  starting transfers between devices: 0.34 us -> 54.8 us
  blocking collectives: 39.2 us -> 0 us
  matrix products: 37.5 us -> 0 us
  local copies, waits for them, and re-layouts: 25.5 us -> 44 us
  between operations: 16.5 us -> 1.14 us
  other arithmetic: 13.8 us -> 5.46 us
    all_gather x5 -> x0, waiting for transfers between devices: 158 us -> none  [the longest x1 62.1 us: shards(): row_piece = lax.all_gather(first_pass, ('tok', 'head'), axis=0, tiled=True)]
    reduce_scatter x3 -> x0, waiting for transfers between devices: 121 us -> none  [the longest x2 96.7 us: run_layer(): lax.psum_scatter(jnp.dot(attended, w_out, preferred_element_type=jnp.floa...]
    pallas_call x0 -> x17, Pallas kernels: none -> 56.6 us  [the longest x4 36.3 us: largest_logits(): pl.pallas_call(functools.partial(logits_kernel, share, tok_count), out_sh...]
    ppermute x0 -> x54, starting transfers between devices: none -> 54.8 us  [the longest x18 27.9 us: by_tok(): return lax.ppermute(value, 'tok', xor_pairs(tok_count, mask))]
    ppermute x0 -> x54, waiting for transfers between devices: none -> 50.2 us  [the longest x18 33.5 us: by_tok(): return lax.ppermute(value, 'tok', xor_pairs(tok_count, mask))]
    pmax x1 -> x0, blocking collectives: 39.2 us -> none  [shards(): top_logits = lax.pmax(top_local, ('tok', 'head'))]
    dot_general x18 -> x0, matrix products: 37.5 us -> none  [the longest x1 16.7 us: shards(): lax.dot_general(normed, lm_head, (((1,), (1,)), ((), ())), preferred_elem...]
    gather x1 -> x4, local copies, waits for them, and re-layouts: 9.85 us -> 31 us  [shards(): found = jnp.take(embed, ids, axis=0, mode='clip')]
  transfers between devices with their start and end apart: 8 -> 54, of which waited for: 7 -> 16; matrix products, arithmetic and copies ran while one was open for 8% -> 17% of each run, Pallas kernels for 0% -> 27%
where the time goes in v1:
time: 213 us; the launch traced here: 212 us
  Pallas kernels  56.6 us (27%)
  starting transfers between devices  54.8 us (26%)
  waiting for transfers between devices  50.2 us (24%)
  local copies, waits for them, and re-layouts  44 us (21%)
  other arithmetic  5.46 us (3%)
    pallas_call x4, Pallas kernels, largest_logits(): pl.pallas_call(functools.partial(logits_kernel, share, tok_count), out_sh...  36.3 us
    ppermute x18, waiting for transfers between devices, by_tok(): return lax.ppermute(value, 'tok', xor_pairs(tok_count, mask))  33.5 us
    gather x4, local copies, waits for them, and re-layouts, shards(): found = jnp.take(embed, ids, axis=0, mode='clip')  31 us
    ppermute x18, starting transfers between devices, by_tok(): return lax.ppermute(value, 'tok', xor_pairs(tok_count, mask))  27.9 us
    ppermute x31, starting transfers between devices, by_head(): return lax.ppermute(value, 'head', xor_pairs(head_count, mask))  22.4 us
    ppermute x31, waiting for transfers between devices, by_head(): return lax.ppermute(value, 'head', xor_pairs(head_count, mask))  16.8 us
    unnamed x48, local copies, waits for them, and re-layouts  12.1 us
    pallas_call x2, Pallas kernels, away_parts(): pl.pallas_call(functools.partial(away_kernel, tok_count, masks), out_shap...  7.5 us
  transfers between devices with their start and end apart: 54, of which 16 were waited for; matrix products, arithmetic and copies ran while one was open for 17% of the time, Pallas kernels for 27%

profile of v1, /device:TPU:0, one launch (start us, length us, event | category | flops | bytes accessed | tf_op | source)
XLA Modules:
  0.0 212.2 jit_solution(12315438696500344117)
XLA Ops:
  1.1 2.6 %collective-permute-start.22 = (bf16[256,256]{1,0:T(8,128)(2,1)}, bf16[256,256]{1,0:T(8,128)(2,1)S(1)}, u32[]{:S(2)}, u32[]{:S(2)}) collective-permute-start(bf16[256,256]{1,0:T(8,128)(2,1)} %refs_0_.1), channel_id=1, source_target_pairs={{0,2},{1,3},{2,0},{3,1},{4,6},{5,7},{6,4},{7,5},{8,10},{9,11},{10,... | collective-permute-start | bytes 393224 | tf_op jit(solution)/shard_map/ppermute | solution.py:363
  3.7 1.5 collective-permute-start.24
  5.3 2.8 %collective-permute-done.22.refs_2_ = bf16[256,256]{1,0:T(8,128)(2,1)S(1)} collective-permute-done((bf16[256,256]{1,0:T(8,128)(2,1)}, bf16[256,256]{1,0:T(8,128)(2,1)S(1)}, u32[]{:S(2)}, u32[]{:S(2)}) %collective-permute-start.22) | collective-permute-done | bytes 131104 | tf_op jit(solution)/shard_map/ppermute | solution.py:363
  8.1 4.2 %collective-permute-done.24.refs_4_ = bf16[256,256]{1,0:T(8,128)(2,1)S(1)} collective-permute-done((bf16[256,256]{1,0:T(8,128)(2,1)}, bf16[256,256]{1,0:T(8,128)(2,1)S(1)}, u32[]{:S(2)}, u32[]{:S(2)}) %collective-permute-start.24) | collective-permute-done | bytes 131104 | tf_op jit(solution)/shard_map/ppermute | solution.py:363
  13.8 1.2 copy-done.6
  15.1 1.2 copy-done.8
  16.3 1.2 copy-done.10
  18.4 1.7 project.3
  20.1 1.6 collective-permute-start.28
  21.7 2.6 %collective-permute-start.29 = (bf16[256,256]{1,0:T(8,128)(2,1)S(1)}, bf16[256,256]{1,0:T(8,128)(2,1)S(1)}, u32[]{:S(2)}, u32[]{:S(2)}) collective-permute-start(bf16[256,256]{1,0:T(8,128)(2,1)S(1)} %get-tuple-element.50.query), channel_id=1, source_target_pairs={{0,16},{8,24},{16,0},{24,8},{1,17},{9,25},{17,1},{25,9},{2,18},{10... | collective-permute-start | bytes 393224 | tf_op jit(solution)/shard_map/ppermute | solution.py:366
  25.2 2.8 %collective-permute-done.28.refs_0_ = bf16[256,256]{1,0:T(8,128)(2,1)S(1)} collective-permute-done((bf16[256,256]{1,0:T(8,128)(2,1)S(1)}, bf16[256,256]{1,0:T(8,128)(2,1)S(1)}, u32[]{:S(2)}, u32[]{:S(2)}) %collective-permute-start.28) | collective-permute-done | bytes 131104 | tf_op jit(solution)/shard_map/ppermute | solution.py:366
  28.0 6.7 %collective-permute-done.29.refs_1_ = bf16[256,256]{1,0:T(8,128)(2,1)S(1)} collective-permute-done((bf16[256,256]{1,0:T(8,128)(2,1)S(1)}, bf16[256,256]{1,0:T(8,128)(2,1)S(1)}, u32[]{:S(2)}, u32[]{:S(2)}) %collective-permute-start.29) | collective-permute-done | bytes 131104 | tf_op jit(solution)/shard_map/ppermute | solution.py:366
  34.7 1.0 copy-done
  35.7 1.0 copy-done.3
  36.7 3.7 %away_parts.3 = (bf16[272,256]{1,0:T(8,128)(2,1)S(1)}, bf16[272,256]{1,0:T(8,128)(2,1)S(1)}, bf16[272,256]{1,0:T(8,128)(2,1)S(1)}) custom-call(s32[6]{0:T(128)S(1)} %pad_add_fusion.place, bf16[256,256]{1,0:T(8,128)(2,1)S(1)} %collective-permute-done.28.refs_0_, bf16[256,256]{1,0:T(8,128)(2,1)S(1)} %collective-permute-done.29.refs_1_, ...), custom_call_target="tpu_custom_call" | custom-call | flops 268435456 | bytes 1048576 | tf_op jit(solution)/shard_map/away_parts/pallas_call | solution.py:172
  40.5 1.6 collective-permute-start.31
  42.1 2.8 %collective-permute-start.33 = (bf16[272,256]{1,0:T(8,128)(2,1)S(1)}, bf16[272,256]{1,0:T(8,128)(2,1)S(1)}, u32[]{:S(2)}, u32[]{:S(2)}) collective-permute-start(bf16[272,256]{1,0:T(8,128)(2,1)S(1)} %get-tuple-element.57), channel_id=1, source_target_pairs={{0,24},{8,16},{16,8},{24,0},{1,25},{9,17},{17,9},{25,1},{2,26},{10... | collective-permute-start | bytes 417800 | tf_op jit(solution)/shard_map/ppermute | solution.py:366
  44.9 7.9 %gather_fusion = bf16[256,256]{1,0:T(8,128)(2,1)} fusion(bf16[25088,256]{1,0:T(8,128)(2,1)} %param.26, s32[1024]{0:T(1024)S(1)} %pad_clamp_fusion.3), kind=kCustom, calls=%fused_computation | custom fusion | bytes 263168 | tf_op jit(solution)/shard_map/jit(_take)/gather | solution.py:393
  53.9 1.0 copy-done.1
  54.9 1.0 copy-done.4
  56.0 2.2 %own_part.3 = (f32[256,256]{1,0:T(8,128)S(1)}, f32[256,256]{1,0:T(8,128)S(1)}) custom-call(s32[6]{0:T(128)S(1)} %pad_add_fusion.place, bf16[256,256]{1,0:T(8,128)(2,1)S(1)} %get-tuple-element.50.query, bf16[256,256]{1,0:T(8,128)(2,1)S(1)} %get-tuple-element.51.new_keys, bf16[256,256]{1,0:T(8,128)(2,1)S(1)} %get-tuple-element.52.new_values, ...), custom_call_target="tpu_custom_call" | custom-call | flops 268435456 | bytes 1048576 | tf_op jit(solution)/shard_map/own_part/pallas_call | solution.py:135
  58.2 1.0 combine.3
  59.3 7.9 %gather_fusion.1 = bf16[256,256]{1,0:T(8,128)(2,1)} fusion(bf16[25088,256]{1,0:T(8,128)(2,1)} %param.26, s32[1024]{0:T(1024)S(1)} %get-tuple-element.78), kind=kCustom, calls=%fused_computation.1 | custom fusion | bytes 263168 | tf_op jit(solution)/shard_map/jit(_take)/gather | solution.py:393
  67.3 2.7 %collective-permute-start.1 = (bf16[256,256]{1,0:T(8,128)(2,1)}, bf16[256,256]{1,0:T(8,128)(2,1)}, u32[]{:S(2)}, u32[]{:S(2)}) collective-permute-start(bf16[256,256]{1,0:T(8,128)(2,1)} %gather_fusion.1), channel_id=1, source_target_pairs={{0,16},{8,24},{16,0},{24,8},{1,17},{9,25},{17,1},{25,9},{2,18},{10... | collective-permute-start | bytes 393224 | tf_op jit(solution)/shard_map/ppermute | solution.py:366
  70.0 1.2 copy-done.12
  72.5 1.3 collective-permute-start.36
  73.8 1.4 collective-permute-start.37
  75.2 1.3 compare_and_fusion.3
  76.5 1.6 collective-permute-done.35.refs_0_
  78.1 1.4 collective-permute-done.36.refs_1_
  79.5 1.6 collective-permute-done.37.refs_2_
  83.3 1.5 collective-permute-start.38
  84.8 1.3 collective-permute-start.39
  86.1 1.6 collective-permute-start.40
  87.7 1.5 collective-permute-done.38
  89.2 7.6 %collective-permute-done.39 = bf16[32,2048]{1,0:T(8,128)(2,1)S(1)} collective-permute-done((bf16[32,2048]{1,0:T(8,128)(2,1)S(1)}, bf16[32,2048]{1,0:T(8,128)(2,1)S(1)}, u32[]{:S(2)}, u32[]{:S(2)}) %collective-permute-start.39) | collective-permute-done | bytes 131104 | tf_op jit(solution)/shard_map/ppermute | solution.py:366
  97.5 1.4 collective-permute-start.44
  99.5 7.9 %gather_fusion.2 = bf16[256,256]{1,0:T(8,128)(2,1)} fusion(bf16[25088,256]{1,0:T(8,128)(2,1)} %param.26, s32[1024]{0:T(1024)S(1)} %get-tuple-element.77), kind=kCustom, calls=%fused_computation.2 | custom fusion | bytes 263168 | tf_op jit(solution)/shard_map/jit(_take)/gather | solution.py:393
  107.4 2.0 collective-permute-start.2
  109.4 7.3 %gather_fusion.3 = bf16[256,256]{1,0:T(8,128)(2,1)S(1)} fusion(bf16[25088,256]{1,0:T(8,128)(2,1)} %param.26, s32[1024]{0:T(1024)S(1)} %pad_clamp_fusion), kind=kCustom, calls=%fused_computation.3 | custom fusion | bytes 263168 | tf_op jit(solution)/shard_map/jit(_take)/gather | solution.py:393
  117.4 1.3 select_select_fusion.refs_0_
  118.7 1.1 collective-permute-start.4
  119.7 1.5 collective-permute-start.6
  121.7 1.3 collective-permute-start.47
  123.0 9.2 %largest_logits.4.refs_0_ = f32[8,256]{1,0:T(8,128)S(1)} custom-call(s32[6]{0:T(128)S(1)} %pad_add_fusion.place, bf16[128,2048]{1,0:T(8,128)(2,1)S(1)} %constant_dynamic-update-slice_fusion.mine, bf16[128,2048]{1,0:T(8,128)(2,1)S(1)} %collective-permute-done.41.other, bf16[3136,2048]{1,0:T(8,128)(2,1)} %lm_block.7), custom_call_target="tpu_custom_call" | custom-call | flops 3288334336 | bytes 12845056 | tf_op jit(solution)/shard_map/largest_logits/pallas_call | solution.py:299
  132.2 2.0 collective-permute-start.8
  134.9 9.0 %largest_logits.5.refs_1_ = f32[8,256]{1,0:T(8,128)S(1)} custom-call(s32[6]{0:T(128)S(1)} %pad_add_fusion.place, bf16[128,2048]{1,0:T(8,128)(2,1)S(1)} %collective-permute-done.42.mine, bf16[128,2048]{1,0:T(8,128)(2,1)S(1)} %collective-permute-done.43.other, bf16[3136,2048]{1,0:T(8,128)(2,1)} %lm_block.7), custom_call_target="tpu_custom_call" | custom-call | flops 3288334336 | bytes 12845056 | tf_op jit(solution)/shard_map/largest_logits/pallas_call | solution.py:299
  145.0 9.1 %largest_logits.6.refs_2_ = f32[8,256]{1,0:T(8,128)S(1)} custom-call(s32[6]{0:T(128)S(1)} %pad_add_fusion.place, bf16[128,2048]{1,0:T(8,128)(2,1)S(1)} %collective-permute-done.44.mine, bf16[128,2048]{1,0:T(8,128)(2,1)S(1)} %collective-permute-done.45.other, bf16[3136,2048]{1,0:T(8,128)(2,1)} %lm_block.7), custom_call_target="tpu_custom_call" | custom-call | flops 3288334336 | bytes 12845056 | tf_op jit(solution)/shard_map/largest_logits/pallas_call | solution.py:299
  154.2 9.1 %largest_logits.7.refs_3_ = f32[8,256]{1,0:T(8,128)S(1)} custom-call(s32[6]{0:T(128)S(1)} %pad_add_fusion.place, bf16[128,2048]{1,0:T(8,128)(2,1)S(1)} %constant_dynamic-update-slice_fusion.4.mine, bf16[128,2048]{1,0:T(8,128)(2,1)S(1)} %collective-permute-done.48.other, bf16[3136,2048]{1,0:T(8,128)(2,1)} %lm_block.7), custom_call_target="tpu_custom_call" | custom-call | flops 3288334336 | bytes 12845056 | tf_op jit(solution)/shard_map/largest_logits/pallas_call | solution.py:299
  164.0 1.7 project.2
  166.3 1.1 collective-permute-start.11
  167.4 2.6 %collective-permute-start.12 = (bf16[256,256]{1,0:T(8,128)(2,1)S(1)}, bf16[256,256]{1,0:T(8,128)(2,1)S(1)}, u32[]{:S(2)}, u32[]{:S(2)}) collective-permute-start(bf16[256,256]{1,0:T(8,128)(2,1)S(1)} %get-tuple-element.35.query), channel_id=1, source_target_pairs={{0,24},{8,16},{16,8},{24,0},{1,25},{9,17},{17,9},{25,1},{2,26},{10... | collective-permute-start | bytes 393224 | tf_op jit(solution)/shard_map/ppermute | solution.py:366
  170.5 2.5 %collective-permute-done.10.refs_0_ = bf16[256,256]{1,0:T(8,128)(2,1)S(1)} collective-permute-done((bf16[256,256]{1,0:T(8,128)(2,1)S(1)}, bf16[256,256]{1,0:T(8,128)(2,1)S(1)}, u32[]{:S(2)}, u32[]{:S(2)}) %collective-permute-start.10) | collective-permute-done | bytes 131104 | tf_op jit(solution)/shard_map/ppermute | solution.py:366
  173.0 6.2 %collective-permute-done.11.refs_1_ = bf16[256,256]{1,0:T(8,128)(2,1)S(1)} collective-permute-done((bf16[256,256]{1,0:T(8,128)(2,1)S(1)}, bf16[256,256]{1,0:T(8,128)(2,1)S(1)}, u32[]{:S(2)}, u32[]{:S(2)}) %collective-permute-start.11) | collective-permute-done | bytes 131104 | tf_op jit(solution)/shard_map/ppermute | solution.py:366
  179.2 3.8 %away_parts.2 = (bf16[272,256]{1,0:T(8,128)(2,1)S(1)}, bf16[272,256]{1,0:T(8,128)(2,1)S(1)}, bf16[272,256]{1,0:T(8,128)(2,1)S(1)}) custom-call(s32[6]{0:T(128)S(1)} %pad_add_fusion.place, bf16[256,256]{1,0:T(8,128)(2,1)S(1)} %collective-permute-done.10.refs_0_, bf16[256,256]{1,0:T(8,128)(2,1)S(1)} %collective-permute-done.11.refs_1_, ...), custom_call_target="tpu_custom_call" | custom-call | flops 268435456 | bytes 1048576 | tf_op jit(solution)/shard_map/away_parts/pallas_call | solution.py:172
  183.0 1.8 collective-permute-start.13
  184.7 2.6 %collective-permute-start.15 = (bf16[272,256]{1,0:T(8,128)(2,1)S(1)}, bf16[272,256]{1,0:T(8,128)(2,1)S(1)}, u32[]{:S(2)}, u32[]{:S(2)}) collective-permute-start(bf16[272,256]{1,0:T(8,128)(2,1)S(1)} %get-tuple-element.42), channel_id=1, source_target_pairs={{0,24},{8,16},{16,8},{24,0},{1,25},{9,17},{17,9},{25,1},{2,26},{10... | collective-permute-start | bytes 417800 | tf_op jit(solution)/shard_map/ppermute | solution.py:366
  188.0 2.0 own_part.2
  190.1 6.3 %collective-permute-done.14.refs_1_ = bf16[272,256]{1,0:T(8,128)(2,1)S(1)} collective-permute-done((bf16[272,256]{1,0:T(8,128)(2,1)S(1)}, bf16[272,256]{1,0:T(8,128)(2,1)S(1)}, u32[]{:S(2)}, u32[]{:S(2)}) %collective-permute-start.14) | collective-permute-done | bytes 139296 | tf_op jit(solution)/shard_map/ppermute | solution.py:366
  197.5 3.4 %collective-permute-start.52 = (f32[8,256]{1,0:T(8,128)S(1)}, f32[8,256]{1,0:T(8,128)S(1)}, u32[]{:S(2)}, u32[]{:S(2)}) collective-permute-start(f32[8,256]{1,0:T(8,128)S(1)} %add_select_fusion.2), channel_id=1, source_target_pairs={{0,8},{8,0},{16,24},{24,16},{1,9},{9,1},{17,25},{25,17},{2,10},{10... | collective-permute-start | bytes 24584 | tf_op jit(solution)/shard_map/ppermute | solution.py:413
  201.8 1.2 collective-permute-start.19
  203.1 1.9 collective-permute-start.20
  205.2 2.6 %collective-permute-done.18.refs_0_ = bf16[32,2048]{1,0:T(8,128)(2,1)S(1)} collective-permute-done((bf16[32,2048]{1,0:T(8,128)(2,1)S(1)}, bf16[32,2048]{1,0:T(8,128)(2,1)S(1)}, u32[]{:S(2)}, u32[]{:S(2)}) %collective-permute-start.18) | collective-permute-done | bytes 131104 | tf_op jit(solution)/shard_map/ppermute | solution.py:363
  207.8 2.2 %collective-permute-done.19.refs_1_ = bf16[32,2048]{1,0:T(8,128)(2,1)S(1)} collective-permute-done((bf16[32,2048]{1,0:T(8,128)(2,1)S(1)}, bf16[32,2048]{1,0:T(8,128)(2,1)S(1)}, u32[]{:S(2)}, u32[]{:S(2)}) %collective-permute-start.19) | collective-permute-done | bytes 131104 | tf_op jit(solution)/shard_map/ppermute | solution.py:363
  (138 shorter events, 19.6 us)
Async XLA Ops:
  0.6 69.3 %collective-permute-start.17 = (bf16[256,2048]{1,0:T(8,128)(2,1)}, bf16[256,2048]{1,0:T(8,128)(2,1)S(1)}, u32[]{:S(2)}, u32[]{:S(2)}) collective-permute-start(bf16[256,2048]{1,0:T(8,128)(2,1)} %w_keep.3), channel_id=1, source_target_pairs={{0,1},{1,0},{2,3},{3,2},{4,5},{5,4},{6,7},{7,6},{8,9},{9,8},{10,11... | collective-permute-start | bytes 3145736 | tf_op jit(solution)/shard_map/ppermute | solution.py:363
  1.1 6.9 %collective-permute-start.22 = (bf16[256,256]{1,0:T(8,128)(2,1)}, bf16[256,256]{1,0:T(8,128)(2,1)S(1)}, u32[]{:S(2)}, u32[]{:S(2)}) collective-permute-start(bf16[256,256]{1,0:T(8,128)(2,1)} %refs_0_.1), channel_id=1, source_target_pairs={{0,2},{1,3},{2,0},{3,1},{4,6},{5,7},{6,4},{7,5},{8,10},{9,11},{10,... | collective-permute-start | bytes 393224 | tf_op jit(solution)/shard_map/ppermute | solution.py:363
  3.7 8.6 %collective-permute-start.24 = (bf16[256,256]{1,0:T(8,128)(2,1)}, bf16[256,256]{1,0:T(8,128)(2,1)S(1)}, u32[]{:S(2)}, u32[]{:S(2)}) collective-permute-start(bf16[256,256]{1,0:T(8,128)(2,1)} %refs_0_.1), channel_id=1, source_target_pairs={{0,4},{1,5},{2,6},{3,7},{4,0},{5,1},{6,2},{7,3},{8,12},{9,13},{10,... | collective-permute-start | bytes 393224 | tf_op jit(solution)/shard_map/ppermute | solution.py:363
  5.2 7.1 %collective-permute-start.26 = (bf16[256,256]{1,0:T(8,128)(2,1)}, bf16[256,256]{1,0:T(8,128)(2,1)S(1)}, u32[]{:S(2)}, u32[]{:S(2)}) collective-permute-start(bf16[256,256]{1,0:T(8,128)(2,1)} %refs_0_.1), channel_id=1, source_target_pairs={{0,6},{1,7},{2,4},{3,5},{4,2},{5,3},{6,0},{7,1},{8,14},{9,15},{10,... | collective-permute-start | bytes 393224 | tf_op jit(solution)/shard_map/ppermute | solution.py:363
  5.3 8.3 %collective-permute-start.21 = (bf16[256,256]{1,0:T(8,128)(2,1)}, bf16[256,256]{1,0:T(8,128)(2,1)S(1)}, u32[]{:S(2)}, u32[]{:S(2)}) collective-permute-start(bf16[256,256]{1,0:T(8,128)(2,1)} %refs_0_.1), channel_id=1, source_target_pairs={{0,1},{1,0},{2,3},{3,2},{4,5},{5,4},{6,7},{7,6},{8,9},{9,8},{10,11... | collective-permute-start | bytes 393224 | tf_op jit(solution)/shard_map/ppermute | solution.py:363
  8.1 5.5 %collective-permute-start.23 = (bf16[256,256]{1,0:T(8,128)(2,1)S(1)}, bf16[256,256]{1,0:T(8,128)(2,1)S(1)}, u32[]{:S(2)}, u32[]{:S(2)}) collective-permute-start(bf16[256,256]{1,0:T(8,128)(2,1)S(1)} %collective-permute-done.22.refs_2_), channel_id=1, source_target_pairs={{0,1},{1,0},{2,3},{3,2},{4,5},{5,4},{6,7},{7,6},{8,9},{9,8},{10,11... | collective-permute-start | bytes 393224 | tf_op jit(solution)/shard_map/ppermute | solution.py:363
  12.3 1.3 collective-permute-start.25
  12.3 1.5 collective-permute-start.27
  18.4 99.0 %copy-start.15 = (bf16[256,256]{1,0:T(8,128)(2,1)S(1)}, bf16[256,256]{1,0:T(8,128)(2,1)}, u32[]{:S(2)}) copy-start(bf16[256,256]{1,0:T(8,128)(2,1)} %refs_0_.1) | copy-start | bytes 393220
  20.1 7.9 %collective-permute-start.28 = (bf16[256,256]{1,0:T(8,128)(2,1)S(1)}, bf16[256,256]{1,0:T(8,128)(2,1)S(1)}, u32[]{:S(2)}, u32[]{:S(2)}) collective-permute-start(bf16[256,256]{1,0:T(8,128)(2,1)S(1)} %get-tuple-element.50.query), channel_id=1, source_target_pairs={{0,8},{8,0},{16,24},{24,16},{1,9},{9,1},{17,25},{25,17},{2,10},{10... | collective-permute-start | bytes 393224 | tf_op jit(solution)/shard_map/ppermute | solution.py:366
  21.7 12.9 %collective-permute-start.29 = (bf16[256,256]{1,0:T(8,128)(2,1)S(1)}, bf16[256,256]{1,0:T(8,128)(2,1)S(1)}, u32[]{:S(2)}, u32[]{:S(2)}) collective-permute-start(bf16[256,256]{1,0:T(8,128)(2,1)S(1)} %get-tuple-element.50.query), channel_id=1, source_target_pairs={{0,16},{8,24},{16,0},{24,8},{1,17},{9,25},{17,1},{25,9},{2,18},{10... | collective-permute-start | bytes 393224 | tf_op jit(solution)/shard_map/ppermute | solution.py:366
  24.3 10.3 %collective-permute-start.30 = (bf16[256,256]{1,0:T(8,128)(2,1)S(1)}, bf16[256,256]{1,0:T(8,128)(2,1)S(1)}, u32[]{:S(2)}, u32[]{:S(2)}) collective-permute-start(bf16[256,256]{1,0:T(8,128)(2,1)S(1)} %get-tuple-element.50.query), channel_id=1, source_target_pairs={{0,24},{8,16},{16,8},{24,0},{1,25},{9,17},{17,9},{25,1},{2,26},{10... | collective-permute-start | bytes 393224 | tf_op jit(solution)/shard_map/ppermute | solution.py:366
  40.5 17.7 %collective-permute-start.31 = (bf16[272,256]{1,0:T(8,128)(2,1)S(1)}, bf16[272,256]{1,0:T(8,128)(2,1)S(1)}, u32[]{:S(2)}, u32[]{:S(2)}) collective-permute-start(bf16[272,256]{1,0:T(8,128)(2,1)S(1)} %get-tuple-element.55), channel_id=1, source_target_pairs={{0,8},{8,0},{16,24},{24,16},{1,9},{9,1},{17,25},{25,17},{2,10},{10... | collective-permute-start | bytes 417800 | tf_op jit(solution)/shard_map/ppermute | solution.py:366
  42.1 16.1 %collective-permute-start.32 = (bf16[272,256]{1,0:T(8,128)(2,1)S(1)}, bf16[272,256]{1,0:T(8,128)(2,1)S(1)}, u32[]{:S(2)}, u32[]{:S(2)}) collective-permute-start(bf16[272,256]{1,0:T(8,128)(2,1)S(1)} %get-tuple-element.56), channel_id=1, source_target_pairs={{0,16},{8,24},{16,0},{24,8},{1,17},{9,25},{17,1},{25,9},{2,18},{10... | collective-permute-start | bytes 417800 | tf_op jit(solution)/shard_map/ppermute | solution.py:366
  42.1 16.1 %collective-permute-start.33 = (bf16[272,256]{1,0:T(8,128)(2,1)S(1)}, bf16[272,256]{1,0:T(8,128)(2,1)S(1)}, u32[]{:S(2)}, u32[]{:S(2)}) collective-permute-start(bf16[272,256]{1,0:T(8,128)(2,1)S(1)} %get-tuple-element.57), channel_id=1, source_target_pairs={{0,24},{8,16},{16,8},{24,0},{1,25},{9,17},{17,9},{25,1},{2,26},{10... | collective-permute-start | bytes 417800 | tf_op jit(solution)/shard_map/ppermute | solution.py:366
  52.9 54.5 %collective-permute-start = (bf16[256,256]{1,0:T(8,128)(2,1)}, bf16[256,256]{1,0:T(8,128)(2,1)S(1)}, u32[]{:S(2)}, u32[]{:S(2)}) collective-permute-start(bf16[256,256]{1,0:T(8,128)(2,1)} %gather_fusion), channel_id=1, source_target_pairs={{0,24},{8,16},{16,8},{24,0},{1,25},{9,17},{17,9},{25,1},{2,26},{10... | collective-permute-start | bytes 393224 | tf_op jit(solution)/shard_map/ppermute | solution.py:366
  59.2 10.7 %collective-permute-start.34 = (bf16[128,256]{1,0:T(8,128)(2,1)S(1)}, bf16[128,256]{1,0:T(8,128)(2,1)S(1)}, u32[]{:S(2)}, u32[]{:S(2)}) collective-permute-start(bf16[128,256]{1,0:T(8,128)(2,1)S(1)} %get-tuple-element.59), channel_id=1, source_target_pairs={{0,1},{1,0},{2,3},{3,2},{4,5},{5,4},{6,7},{7,6},{8,9},{9,8},{10,11... | collective-permute-start | bytes 196616 | tf_op jit(solution)/shard_map/ppermute | solution.py:363
  67.3 49.5 %collective-permute-start.1 = (bf16[256,256]{1,0:T(8,128)(2,1)}, bf16[256,256]{1,0:T(8,128)(2,1)}, u32[]{:S(2)}, u32[]{:S(2)}) collective-permute-start(bf16[256,256]{1,0:T(8,128)(2,1)} %gather_fusion.1), channel_id=1, source_target_pairs={{0,16},{8,24},{16,0},{24,8},{1,17},{9,25},{17,1},{25,9},{2,18},{10... | collective-permute-start | bytes 393224 | tf_op jit(solution)/shard_map/ppermute | solution.py:366
  71.7 6.4 %collective-permute-start.35 = (bf16[32,2048]{1,0:T(8,128)(2,1)S(1)}, bf16[32,2048]{1,0:T(8,128)(2,1)S(1)}, u32[]{:S(2)}, u32[]{:S(2)}) collective-permute-start(bf16[32,2048]{1,0:T(8,128)(2,1)S(1)} %get-tuple-element.61), channel_id=1, source_target_pairs={{0,2},{1,3},{2,0},{3,1},{4,6},{5,7},{6,4},{7,5},{8,10},{9,11},{10,... | collective-permute-start | bytes 393224 | tf_op jit(solution)/shard_map/ppermute | solution.py:363
  72.5 7.0 %collective-permute-start.36 = (bf16[32,2048]{1,0:T(8,128)(2,1)S(1)}, bf16[32,2048]{1,0:T(8,128)(2,1)S(1)}, u32[]{:S(2)}, u32[]{:S(2)}) collective-permute-start(bf16[32,2048]{1,0:T(8,128)(2,1)S(1)} %get-tuple-element.62), channel_id=1, source_target_pairs={{0,4},{1,5},{2,6},{3,7},{4,0},{5,1},{6,2},{7,3},{8,12},{9,13},{10,... | collective-permute-start | bytes 393224 | tf_op jit(solution)/shard_map/ppermute | solution.py:363
  73.8 7.3 %collective-permute-start.37 = (bf16[32,2048]{1,0:T(8,128)(2,1)S(1)}, bf16[32,2048]{1,0:T(8,128)(2,1)S(1)}, u32[]{:S(2)}, u32[]{:S(2)}) collective-permute-start(bf16[32,2048]{1,0:T(8,128)(2,1)S(1)} %get-tuple-element.63), channel_id=1, source_target_pairs={{0,6},{1,7},{2,4},{3,5},{4,2},{5,3},{6,0},{7,1},{8,14},{9,15},{10,... | collective-permute-start | bytes 393224 | tf_op jit(solution)/shard_map/ppermute | solution.py:363
  83.3 5.9 %collective-permute-start.38 = (bf16[32,2048]{1,0:T(8,128)(2,1)S(1)}, bf16[32,2048]{1,0:T(8,128)(2,1)S(1)}, u32[]{:S(2)}, u32[]{:S(2)}) collective-permute-start(bf16[32,2048]{1,0:T(8,128)(2,1)S(1)} %get-tuple-element.66), channel_id=1, source_target_pairs={{0,8},{8,0},{16,24},{24,16},{1,9},{9,1},{17,25},{25,17},{2,10},{10... | collective-permute-start | bytes 393224 | tf_op jit(solution)/shard_map/ppermute | solution.py:366
  84.8 12.0 %collective-permute-start.39 = (bf16[32,2048]{1,0:T(8,128)(2,1)S(1)}, bf16[32,2048]{1,0:T(8,128)(2,1)S(1)}, u32[]{:S(2)}, u32[]{:S(2)}) collective-permute-start(bf16[32,2048]{1,0:T(8,128)(2,1)S(1)} %get-tuple-element.66), channel_id=1, source_target_pairs={{0,16},{8,24},{16,0},{24,8},{1,17},{9,25},{17,1},{25,9},{2,18},{10... | collective-permute-start | bytes 393224 | tf_op jit(solution)/shard_map/ppermute | solution.py:366
  86.1 10.7 %collective-permute-start.40 = (bf16[32,2048]{1,0:T(8,128)(2,1)S(1)}, bf16[32,2048]{1,0:T(8,128)(2,1)S(1)}, u32[]{:S(2)}, u32[]{:S(2)}) collective-permute-start(bf16[32,2048]{1,0:T(8,128)(2,1)S(1)} %get-tuple-element.66), channel_id=1, source_target_pairs={{0,24},{8,16},{16,8},{24,0},{1,25},{9,17},{17,9},{25,1},{2,26},{10... | collective-permute-start | bytes 393224 | tf_op jit(solution)/shard_map/ppermute | solution.py:366
  96.9 26.1 %collective-permute-start.41 = (bf16[128,2048]{1,0:T(8,128)(2,1)S(1)}, bf16[128,2048]{1,0:T(8,128)(2,1)S(1)}, u32[]{:S(2)}, u32[]{:S(2)}) collective-permute-start(bf16[128,2048]{1,0:T(8,128)(2,1)S(1)} %constant_dynamic-update-slice_fusion.mine), channel_id=1, source_target_pairs={{0,1},{1,0},{2,3},{3,2},{4,5},{5,4},{6,7},{7,6},{8,9},{9,8},{10,11... | collective-permute-start | bytes 1572872 | tf_op jit(solution)/shard_map/ppermute | solution.py:363
  96.9 24.7 %collective-permute-start.42 = (bf16[128,2048]{1,0:T(8,128)(2,1)S(1)}, bf16[128,2048]{1,0:T(8,128)(2,1)S(1)}, u32[]{:S(2)}, u32[]{:S(2)}) collective-permute-start(bf16[128,2048]{1,0:T(8,128)(2,1)S(1)} %constant_dynamic-update-slice_fusion.mine), channel_id=1, source_target_pairs={{0,2},{1,3},{2,0},{3,1},{4,6},{5,7},{6,4},{7,5},{8,10},{9,11},{10,... | collective-permute-start | bytes 1572872 | tf_op jit(solution)/shard_map/ppermute | solution.py:363
  97.5 23.7 %collective-permute-start.44 = (bf16[128,2048]{1,0:T(8,128)(2,1)S(1)}, bf16[128,2048]{1,0:T(8,128)(2,1)S(1)}, u32[]{:S(2)}, u32[]{:S(2)}) collective-permute-start(bf16[128,2048]{1,0:T(8,128)(2,1)S(1)} %constant_dynamic-update-slice_fusion.mine), channel_id=1, source_target_pairs={{0,4},{1,5},{2,6},{3,7},{4,0},{5,1},{6,2},{7,3},{8,12},{9,13},{10,... | collective-permute-start | bytes 1572872 | tf_op jit(solution)/shard_map/ppermute | solution.py:363
  107.4 2.0 copy-start.20
  107.4 9.3 %collective-permute-start.2 = (bf16[256,256]{1,0:T(8,128)(2,1)}, bf16[256,256]{1,0:T(8,128)(2,1)S(1)}, u32[]{:S(2)}, u32[]{:S(2)}) collective-permute-start(bf16[256,256]{1,0:T(8,128)(2,1)} %gather_fusion.2), channel_id=1, source_target_pairs={{0,8},{8,0},{16,24},{24,16},{1,9},{9,1},{17,25},{25,17},{2,10},{10... | collective-permute-start | bytes 393224 | tf_op jit(solution)/shard_map/ppermute | solution.py:366
  118.7 25.3 %collective-permute-start.4 = (bf16[256,256]{1,0:T(8,128)(2,1)S(1)}, bf16[256,256]{1,0:T(8,128)(2,1)S(1)}, u32[]{:S(2)}, u32[]{:S(2)}) collective-permute-start(bf16[256,256]{1,0:T(8,128)(2,1)S(1)} %select_select_fusion.refs_0_), channel_id=1, source_target_pairs={{0,2},{1,3},{2,0},{3,1},{4,6},{5,7},{6,4},{7,5},{8,10},{9,11},{10,... | collective-permute-start | bytes 393224 | tf_op jit(solution)/shard_map/ppermute | solution.py:363
  119.7 24.3 %collective-permute-start.6 = (bf16[256,256]{1,0:T(8,128)(2,1)S(1)}, bf16[256,256]{1,0:T(8,128)(2,1)S(1)}, u32[]{:S(2)}, u32[]{:S(2)}) collective-permute-start(bf16[256,256]{1,0:T(8,128)(2,1)S(1)} %select_select_fusion.refs_0_), channel_id=1, source_target_pairs={{0,4},{1,5},{2,6},{3,7},{4,0},{5,1},{6,2},{7,3},{8,12},{9,13},{10,... | collective-permute-start | bytes 393224 | tf_op jit(solution)/shard_map/ppermute | solution.py:363
  121.2 10.9 %collective-permute-start.46 = (bf16[64,2048]{1,0:T(8,128)(2,1)S(1)}, bf16[64,2048]{1,0:T(8,128)(2,1)S(1)}, u32[]{:S(2)}, u32[]{:S(2)}) collective-permute-start(bf16[64,2048]{1,0:T(8,128)(2,1)S(1)} %slice.24), channel_id=1, source_target_pairs={{0,2},{1,3},{2,0},{3,1},{4,6},{5,7},{6,4},{7,5},{8,10},{9,11},{10,... | collective-permute-start | bytes 786440 | tf_op jit(solution)/shard_map/ppermute | solution.py:363
  121.7 12.5 %collective-permute-start.47 = (bf16[64,2048]{1,0:T(8,128)(2,1)S(1)}, bf16[64,2048]{1,0:T(8,128)(2,1)S(1)}, u32[]{:S(2)}, u32[]{:S(2)}) collective-permute-start(bf16[64,2048]{1,0:T(8,128)(2,1)S(1)} %slice.25), channel_id=1, source_target_pairs={{0,4},{1,5},{2,6},{3,7},{4,0},{5,1},{6,2},{7,3},{8,12},{9,13},{10,... | collective-permute-start | bytes 786440 | tf_op jit(solution)/shard_map/ppermute | solution.py:363
  123.0 11.4 %collective-permute-start.43 = (bf16[128,2048]{1,0:T(8,128)(2,1)S(1)}, bf16[128,2048]{1,0:T(8,128)(2,1)S(1)}, u32[]{:S(2)}, u32[]{:S(2)}) collective-permute-start(bf16[128,2048]{1,0:T(8,128)(2,1)S(1)} %collective-permute-done.42.mine), channel_id=1, source_target_pairs={{0,1},{1,0},{2,3},{3,2},{4,5},{5,4},{6,7},{7,6},{8,9},{9,8},{10,11... | collective-permute-start | bytes 1572872 | tf_op jit(solution)/shard_map/ppermute | solution.py:363
  132.2 12.3 %collective-permute-start.8 = (bf16[256,256]{1,0:T(8,128)(2,1)S(1)}, bf16[256,256]{1,0:T(8,128)(2,1)S(1)}, u32[]{:S(2)}, u32[]{:S(2)}) collective-permute-start(bf16[256,256]{1,0:T(8,128)(2,1)S(1)} %select_select_fusion.refs_0_), channel_id=1, source_target_pairs={{0,6},{1,7},{2,4},{3,5},{4,2},{5,3},{6,0},{7,1},{8,14},{9,15},{10,... | collective-permute-start | bytes 393224 | tf_op jit(solution)/shard_map/ppermute | solution.py:363
  134.2 10.4 %collective-permute-start.45 = (bf16[128,2048]{1,0:T(8,128)(2,1)S(1)}, bf16[128,2048]{1,0:T(8,128)(2,1)S(1)}, u32[]{:S(2)}, u32[]{:S(2)}) collective-permute-start(bf16[128,2048]{1,0:T(8,128)(2,1)S(1)} %collective-permute-done.44.mine), channel_id=1, source_target_pairs={{0,1},{1,0},{2,3},{3,2},{4,5},{5,4},{6,7},{7,6},{8,9},{9,8},{10,11... | collective-permute-start | bytes 1572872 | tf_op jit(solution)/shard_map/ppermute | solution.py:363
  134.3 19.8 %collective-permute-start.48 = (bf16[128,2048]{1,0:T(8,128)(2,1)S(1)}, bf16[128,2048]{1,0:T(8,128)(2,1)S(1)}, u32[]{:S(2)}, u32[]{:S(2)}) collective-permute-start(bf16[128,2048]{1,0:T(8,128)(2,1)S(1)} %constant_dynamic-update-slice_fusion.4.mine), channel_id=1, source_target_pairs={{0,1},{1,0},{2,3},{3,2},{4,5},{5,4},{6,7},{7,6},{8,9},{9,8},{10,11... | collective-permute-start | bytes 1572872 | tf_op jit(solution)/shard_map/ppermute | solution.py:363
  143.9 20.1 %copy-start.7 = (bf16[2048,256]{1,0:T(8,128)(2,1)S(1)}, bf16[2048,256]{1,0:T(8,128)(2,1)}, u32[]{:S(2)}) copy-start(bf16[2048,256]{1,0:T(8,128)(2,1)} %refs_8_.3) | copy-start | bytes 3145732
  143.9 20.1 %copy-start.9 = (bf16[2048,256]{1,0:T(8,128)(2,1)S(1)}, bf16[2048,256]{1,0:T(8,128)(2,1)}, u32[]{:S(2)}) copy-start(bf16[2048,256]{1,0:T(8,128)(2,1)} %refs_9_.3) | copy-start | bytes 3145732
  143.9 20.1 %copy-start.11 = (bf16[2048,256]{1,0:T(8,128)(2,1)S(1)}, bf16[2048,256]{1,0:T(8,128)(2,1)}, u32[]{:S(2)}) copy-start(bf16[2048,256]{1,0:T(8,128)(2,1)} %refs_10_.3) | copy-start | bytes 3145732
  143.9 35.3 %copy-start.2 = (bf16[1024,256]{1,0:T(8,128)(2,1)S(1)}, bf16[1024,256]{1,0:T(8,128)(2,1)}, u32[]{:S(2)}) copy-start(bf16[1024,256]{1,0:T(8,128)(2,1)} %refs_3_.3) | copy-start | bytes 1572868
  143.9 35.3 %copy-start.5 = (bf16[1024,256]{1,0:T(8,128)(2,1)S(1)}, bf16[1024,256]{1,0:T(8,128)(2,1)}, u32[]{:S(2)}) copy-start(bf16[1024,256]{1,0:T(8,128)(2,1)} %refs_4_.3) | copy-start | bytes 1572868
  143.9 20.0 %collective-permute-start.3 = (bf16[256,256]{1,0:T(8,128)(2,1)S(1)}, bf16[256,256]{1,0:T(8,128)(2,1)S(1)}, u32[]{:S(2)}, u32[]{:S(2)}) collective-permute-start(bf16[256,256]{1,0:T(8,128)(2,1)S(1)} %select_select_fusion.refs_0_), channel_id=1, source_target_pairs={{0,1},{1,0},{2,3},{3,2},{4,5},{5,4},{6,7},{7,6},{8,9},{9,8},{10,11... | collective-permute-start | bytes 393224 | tf_op jit(solution)/shard_map/ppermute | solution.py:363
  144.0 19.9 %collective-permute-start.5 = (bf16[256,256]{1,0:T(8,128)(2,1)S(1)}, bf16[256,256]{1,0:T(8,128)(2,1)S(1)}, u32[]{:S(2)}, u32[]{:S(2)}) collective-permute-start(bf16[256,256]{1,0:T(8,128)(2,1)S(1)} %collective-permute-done.4.refs_2_), channel_id=1, source_target_pairs={{0,1},{1,0},{2,3},{3,2},{4,5},{5,4},{6,7},{7,6},{8,9},{9,8},{10,11... | collective-permute-start | bytes 393224 | tf_op jit(solution)/shard_map/ppermute | solution.py:363
  144.5 19.4 %collective-permute-start.7 = (bf16[256,256]{1,0:T(8,128)(2,1)S(1)}, bf16[256,256]{1,0:T(8,128)(2,1)S(1)}, u32[]{:S(2)}, u32[]{:S(2)}) collective-permute-start(bf16[256,256]{1,0:T(8,128)(2,1)S(1)} %collective-permute-done.6.refs_4_), channel_id=1, source_target_pairs={{0,1},{1,0},{2,3},{3,2},{4,5},{5,4},{6,7},{7,6},{8,9},{9,8},{10,11... | collective-permute-start | bytes 393224 | tf_op jit(solution)/shard_map/ppermute | solution.py:363
  144.6 19.3 %collective-permute-start.9 = (bf16[256,256]{1,0:T(8,128)(2,1)S(1)}, bf16[256,256]{1,0:T(8,128)(2,1)S(1)}, u32[]{:S(2)}, u32[]{:S(2)}) collective-permute-start(bf16[256,256]{1,0:T(8,128)(2,1)S(1)} %collective-permute-done.8.refs_6_), channel_id=1, source_target_pairs={{0,1},{1,0},{2,3},{3,2},{4,5},{5,4},{6,7},{7,6},{8,9},{9,8},{10,11... | collective-permute-start | bytes 393224 | tf_op jit(solution)/shard_map/ppermute | solution.py:363
  154.1 46.8 %copy-start.13 = (bf16[256,2048]{1,0:T(8,128)(2,1)S(1)}, bf16[256,2048]{1,0:T(8,128)(2,1)}, u32[]{:S(2)}) copy-start(bf16[256,2048]{1,0:T(8,128)(2,1)} %w_keep.3) | copy-start | bytes 3145732
  154.1 55.9 %copy-start.17 = (f32[2048]{0:T(1024)S(1)}, f32[2048]{0:T(1024)}, u32[]{:S(2)}) copy-start(f32[2048]{0:T(1024)} %param.24) | copy-start | bytes 24580
  154.1 55.9 %copy-start.19 = (f32[2048]{0:T(1024)S(1)}, f32[2048]{0:T(1024)}, u32[]{:S(2)}) copy-start(f32[2048]{0:T(1024)} %param.25) | copy-start | bytes 24580
  163.8 6.2 %collective-permute-start.49 = (f32[8,256]{1,0:T(8,128)S(1)}, f32[8,256]{1,0:T(8,128)S(1)}, u32[]{:S(2)}, u32[]{:S(2)}) collective-permute-start(f32[8,256]{1,0:T(8,128)S(1)} %gather_best.1), channel_id=1, source_target_pairs={{0,1},{1,0},{2,3},{3,2},{4,5},{5,4},{6,7},{7,6},{8,9},{9,8},{10,11... | collective-permute-start | bytes 24584 | tf_op jit(solution)/shard_map/ppermute | solution.py:413
  165.6 7.4 %collective-permute-start.10 = (bf16[256,256]{1,0:T(8,128)(2,1)S(1)}, bf16[256,256]{1,0:T(8,128)(2,1)S(1)}, u32[]{:S(2)}, u32[]{:S(2)}) collective-permute-start(bf16[256,256]{1,0:T(8,128)(2,1)S(1)} %get-tuple-element.35.query), channel_id=1, source_target_pairs={{0,8},{8,0},{16,24},{24,16},{1,9},{9,1},{17,25},{25,17},{2,10},{10... | collective-permute-start | bytes 393224 | tf_op jit(solution)/shard_map/ppermute | solution.py:366
  166.3 12.9 %collective-permute-start.11 = (bf16[256,256]{1,0:T(8,128)(2,1)S(1)}, bf16[256,256]{1,0:T(8,128)(2,1)S(1)}, u32[]{:S(2)}, u32[]{:S(2)}) collective-permute-start(bf16[256,256]{1,0:T(8,128)(2,1)S(1)} %get-tuple-element.35.query), channel_id=1, source_target_pairs={{0,16},{8,24},{16,0},{24,8},{1,17},{9,25},{17,1},{25,9},{2,18},{10... | collective-permute-start | bytes 393224 | tf_op jit(solution)/shard_map/ppermute | solution.py:366
  167.4 11.8 %collective-permute-start.12 = (bf16[256,256]{1,0:T(8,128)(2,1)S(1)}, bf16[256,256]{1,0:T(8,128)(2,1)S(1)}, u32[]{:S(2)}, u32[]{:S(2)}) collective-permute-start(bf16[256,256]{1,0:T(8,128)(2,1)S(1)} %get-tuple-element.35.query), channel_id=1, source_target_pairs={{0,24},{8,16},{16,8},{24,0},{1,25},{9,17},{17,9},{25,1},{2,26},{10... | collective-permute-start | bytes 393224 | tf_op jit(solution)/shard_map/ppermute | solution.py:366
  170.2 17.2 %collective-permute-start.50 = (f32[8,256]{1,0:T(8,128)S(1)}, f32[8,256]{1,0:T(8,128)S(1)}, u32[]{:S(2)}, u32[]{:S(2)}) collective-permute-start(f32[8,256]{1,0:T(8,128)S(1)} %add_select_fusion.4), channel_id=1, source_target_pairs={{0,2},{1,3},{2,0},{3,1},{4,6},{5,7},{6,4},{7,5},{8,10},{9,11},{10,... | collective-permute-start | bytes 24584 | tf_op jit(solution)/shard_map/ppermute | solution.py:413
  183.0 7.1 %collective-permute-start.13 = (bf16[272,256]{1,0:T(8,128)(2,1)S(1)}, bf16[272,256]{1,0:T(8,128)(2,1)S(1)}, u32[]{:S(2)}, u32[]{:S(2)}) collective-permute-start(bf16[272,256]{1,0:T(8,128)(2,1)S(1)} %get-tuple-element.40), channel_id=1, source_target_pairs={{0,8},{8,0},{16,24},{24,16},{1,9},{9,1},{17,25},{25,17},{2,10},{10... | collective-permute-start | bytes 417800 | tf_op jit(solution)/shard_map/ppermute | solution.py:366
  184.7 11.6 %collective-permute-start.14 = (bf16[272,256]{1,0:T(8,128)(2,1)S(1)}, bf16[272,256]{1,0:T(8,128)(2,1)S(1)}, u32[]{:S(2)}, u32[]{:S(2)}) collective-permute-start(bf16[272,256]{1,0:T(8,128)(2,1)S(1)} %get-tuple-element.41), channel_id=1, source_target_pairs={{0,16},{8,24},{16,0},{24,8},{1,17},{9,25},{17,1},{25,9},{2,18},{10... | collective-permute-start | bytes 417800 | tf_op jit(solution)/shard_map/ppermute | solution.py:366
  184.7 11.6 %collective-permute-start.15 = (bf16[272,256]{1,0:T(8,128)(2,1)S(1)}, bf16[272,256]{1,0:T(8,128)(2,1)S(1)}, u32[]{:S(2)}, u32[]{:S(2)}) collective-permute-start(bf16[272,256]{1,0:T(8,128)(2,1)S(1)} %get-tuple-element.42), channel_id=1, source_target_pairs={{0,24},{8,16},{16,8},{24,0},{1,25},{9,17},{17,9},{25,1},{2,26},{10... | collective-permute-start | bytes 417800 | tf_op jit(solution)/shard_map/ppermute | solution.py:366
  187.5 10.0 %collective-permute-start.51 = (f32[8,256]{1,0:T(8,128)S(1)}, f32[8,256]{1,0:T(8,128)S(1)}, u32[]{:S(2)}, u32[]{:S(2)}) collective-permute-start(f32[8,256]{1,0:T(8,128)S(1)} %add_select_fusion.3), channel_id=1, source_target_pairs={{0,4},{1,5},{2,6},{3,7},{4,0},{5,1},{6,2},{7,3},{8,12},{9,13},{10,... | collective-permute-start | bytes 24584 | tf_op jit(solution)/shard_map/ppermute | solution.py:413
  197.4 3.6 %collective-permute-start.16 = (bf16[128,256]{1,0:T(8,128)(2,1)S(1)}, bf16[128,256]{1,0:T(8,128)(2,1)S(1)}, u32[]{:S(2)}, u32[]{:S(2)}) collective-permute-start(bf16[128,256]{1,0:T(8,128)(2,1)S(1)} %get-tuple-element.44), channel_id=1, source_target_pairs={{0,1},{1,0},{2,3},{3,2},{4,5},{5,4},{6,7},{7,6},{8,9},{9,8},{10,11... | collective-permute-start | bytes 196616 | tf_op jit(solution)/shard_map/ppermute | solution.py:363
  197.5 7.4 %collective-permute-start.52 = (f32[8,256]{1,0:T(8,128)S(1)}, f32[8,256]{1,0:T(8,128)S(1)}, u32[]{:S(2)}, u32[]{:S(2)}) collective-permute-start(f32[8,256]{1,0:T(8,128)S(1)} %add_select_fusion.2), channel_id=1, source_target_pairs={{0,8},{8,0},{16,24},{24,16},{1,9},{9,1},{17,25},{25,17},{2,10},{10... | collective-permute-start | bytes 24584 | tf_op jit(solution)/shard_map/ppermute | solution.py:413
  201.4 6.4 %collective-permute-start.18 = (bf16[32,2048]{1,0:T(8,128)(2,1)S(1)}, bf16[32,2048]{1,0:T(8,128)(2,1)S(1)}, u32[]{:S(2)}, u32[]{:S(2)}) collective-permute-start(bf16[32,2048]{1,0:T(8,128)(2,1)S(1)} %get-tuple-element.46), channel_id=1, source_target_pairs={{0,2},{1,3},{2,0},{3,1},{4,6},{5,7},{6,4},{7,5},{8,10},{9,11},{10,... | collective-permute-start | bytes 393224 | tf_op jit(solution)/shard_map/ppermute | solution.py:363
  201.8 8.1 %collective-permute-start.19 = (bf16[32,2048]{1,0:T(8,128)(2,1)S(1)}, bf16[32,2048]{1,0:T(8,128)(2,1)S(1)}, u32[]{:S(2)}, u32[]{:S(2)}) collective-permute-start(bf16[32,2048]{1,0:T(8,128)(2,1)S(1)} %get-tuple-element.47), channel_id=1, source_target_pairs={{0,4},{1,5},{2,6},{3,7},{4,0},{5,1},{6,2},{7,3},{8,12},{9,13},{10,... | collective-permute-start | bytes 393224 | tf_op jit(solution)/shard_map/ppermute | solution.py:363
  203.1 6.9 %collective-permute-start.20 = (bf16[32,2048]{1,0:T(8,128)(2,1)S(1)}, bf16[32,2048]{1,0:T(8,128)(2,1)S(1)}, u32[]{:S(2)}, u32[]{:S(2)}) collective-permute-start(bf16[32,2048]{1,0:T(8,128)(2,1)S(1)} %get-tuple-element.48), channel_id=1, source_target_pairs={{0,6},{1,7},{2,4},{3,5},{4,2},{5,3},{6,0},{7,1},{8,14},{9,15},{10,... | collective-permute-start | bytes 393224 | tf_op jit(solution)/shard_map/ppermute | solution.py:363
  205.1 5.8 %collective-permute-start.53 = (f32[8,256]{1,0:T(8,128)S(1)}, f32[8,256]{1,0:T(8,128)S(1)}, u32[]{:S(2)}, u32[]{:S(2)}) collective-permute-start(f32[8,256]{1,0:T(8,128)S(1)} %add_select_fusion.1), channel_id=1, source_target_pairs={{0,16},{8,24},{16,0},{24,8},{1,17},{9,25},{17,1},{25,9},{2,18},{10... | collective-permute-start | bytes 24584 | tf_op jit(solution)/shard_map/ppermute | solution.py:413
  (12 other events, 12.0 us)

commit v2 on v1

--- a/solution.py
+++ b/solution.py
@@ -16,9 +16,10 @@
 
 SMEM = pl.BlockSpec(memory_space=pltpu.SMEM)
 VMEM = pl.BlockSpec(memory_space=pltpu.VMEM)
-
-
-def params(mib=48):
+HBM = pl.BlockSpec(memory_space=pltpu.HBM)
+
+
+def params(mib=24):
     return pltpu.CompilerParams(vmem_limit_bytes=mib * 2**20)
 
 
@@ -26,30 +27,52 @@
     return pl.CostEstimate(flops=flops, bytes_accessed=moved, transcendentals=0)
 
 
+def call(kernel, operands, after=(), in_specs=None, **rest):
+    count = len(operands)
+
+    def body(*refs):
+        kernel(*refs[:count], *refs[count + len(after) :])
+
+    specs = list(in_specs) + [pl.BlockSpec(memory_space=pl.ANY)] * len(after)
+    return pl.pallas_call(body, in_specs=specs, **rest)(*operands, *after)
+
+
 def xor_pairs(size, mask):
     return [(i, i ^ mask) for i in range(size)]
+
+
+def fetch(sources, targets, sems):
+    copies = [pltpu.make_async_copy(a, b, sems.at[i]) for i, (a, b) in enumerate(zip(sources, targets, strict=True))]
+    for copy in copies:
+        copy.start()
+    return copies
 
 
 def project_kernel(place, *refs):
     *pieces, wq, wk, wv, q_out, k_out, v_out, res_out, x = refs
     head = place[1]
-    width = pieces[0].shape[1]
-    for mask, piece in enumerate(pieces):
-        at = pl.multiple_of(jnp.bitwise_xor(head, mask) * width, width)
-        x[:, pl.ds(at, width)] = piece[...]
+    rows, width = q_out.shape
+    for odd in range(2):
+        mask = odd
+        for piece in pieces[odd * len(pieces) // 2 : (odd + 1) * len(pieces) // 2]:
+            for start in range(0, piece.shape[0], rows):
+                at = pl.multiple_of(jnp.bitwise_xor(head, mask) * width, width)
+                x[:, pl.ds(at, width)] = piece[start : start + rows, :]
+                mask += 2
     for w, out in ((wq, q_out), (wk, k_out), (wv, v_out)):
         out[...] = jnp.dot(x[...], w[...], preferred_element_type=F32).astype(BF16)
     share = res_out.shape[0]
     res_out[...] = x[pl.ds(pl.multiple_of(head * share, share), share), :]
 
 
-def project(place, pieces, wq, wk, wv):
-    rows, width = pieces[0].shape
-    full = wq.shape[0]
-    share = rows // len(pieces)
+def project(rows, place, pieces, wq, wk, wv, after=()):
+    full, width = wq.shape
+    share = rows // (full // width)
     tile = jax.ShapeDtypeStruct((rows, width), BF16)
-    return pl.pallas_call(
+    return call(
         project_kernel,
+        (place, *pieces, wq, wk, wv),
+        after,
         out_shape=(tile, tile, tile, jax.ShapeDtypeStruct((share, full), BF16)),
         in_specs=[SMEM] + [VMEM] * (len(pieces) + 3),
         out_specs=(VMEM,) * 4,
@@ -57,16 +80,16 @@
         compiler_params=params(),
         cost_estimate=cost(6 * rows * full * width, 8 * full * width),
         name="project",
-    )(place, *pieces, wq, wk, wv)
-
-
-def key_range(place, request, chunk_rows, tok_count):
+    )
+
+
+def key_range(place, request, chunk, chunk_rows, tok_count):
     begin = jnp.int32(0)
     length = jnp.int32(0)
     for i in range(tok_count):
         begin += jnp.where(i < request, place[2 + i], 0)
         length += jnp.where(i == request, place[2 + i], 0)
-    begin -= place[0] * chunk_rows
+    begin -= chunk * chunk_rows
     low = jnp.clip(begin, 0, chunk_rows)
     high = jnp.clip(begin + length, 0, chunk_rows)
     return low, high
@@ -90,7 +113,7 @@
     chunk_rows = keys.shape[0]
     heads = width // HEAD_DIM
     span = min(512, chunk_rows)
-    low, high = key_range(place, request, chunk_rows, tok_count)
+    low, high = key_range(place, request, place[0], chunk_rows, tok_count)
     first = low // span
     last = jnp.where(high > low, (high + span - 1) // span, first)
 
@@ -129,61 +152,113 @@
         log_out[:, cols] = log_sum
 
 
-def own_part(tok_count, place, query, new_keys, new_values, keys, values):
+def own_part(tok_count, place, query, new_keys, new_values, keys, values, after=()):
     rows, width = query.shape
     shape = jax.ShapeDtypeStruct((rows, width), F32)
-    return pl.pallas_call(
+    return call(
         functools.partial(own_kernel, tok_count),
+        (place, query, new_keys, new_values, keys, values),
+        after,
         out_shape=(shape, shape),
         in_specs=[SMEM] + [VMEM] * 5,
         out_specs=(VMEM, VMEM),
         compiler_params=params(),
         cost_estimate=cost(4 * rows * width * keys.shape[0], 4 * keys.shape[0] * width),
         name="own_part",
-    )(place, query, new_keys, new_values, keys, values)
-
-
-def away_kernel(tok_count, masks, place, *refs):
-    queries, (keys, values), outs = refs[: len(masks)], refs[len(masks) : len(masks) + 2], refs[len(masks) + 2 :]
-    for mask, query, out in zip(masks, queries, outs, strict=True):
-        rows, width = query.shape
-        heads = width // HEAD_DIM
-        request = jnp.bitwise_xor(place[0], mask)
-        states = cached_states(place, request, query, keys, values, tok_count)
-        pieces = []
-        for j, state in enumerate(states):
-            mixed, log_sum = settle(state)
-            out[:rows, j * HEAD_DIM : (j + 1) * HEAD_DIM] = mixed.astype(BF16)
-            rest = jnp.transpose(log_sum)[:1, :]
-            for _ in range(3):
-                piece = rest.astype(BF16).astype(F32)
-                pieces.append(piece)
-                rest = rest - piece
-        at = lax.broadcasted_iota(jnp.int32, (16, rows), 0)
-        tail = jnp.zeros((16, rows), F32)
-        for i, piece in enumerate(pieces):
-            tail = jnp.where(at == i, piece, tail)
-        out[rows:, :] = tail.astype(BF16)
-
-
-def away_parts(tok_count, masks, place, queries, keys, values):
+    )
+
+
+def away_part(place, mask, query, keys, values, out, tok_count):
+    rows, width = query.shape
+    states = cached_states(place, jnp.bitwise_xor(place[0], mask), query, keys, values, tok_count)
+    pieces = []
+    for j, state in enumerate(states):
+        mixed, log_sum = settle(state)
+        out[:rows, j * HEAD_DIM : (j + 1) * HEAD_DIM] = mixed.astype(BF16)
+        rest = jnp.transpose(log_sum)[:1, :]
+        for _ in range(3):
+            piece = rest.astype(BF16).astype(F32)
+            pieces.append(piece)
+            rest = rest - piece
+    at = lax.broadcasted_iota(jnp.int32, (16, rows), 0)
+    tail = jnp.zeros((16, rows), F32)
+    for i, piece in enumerate(pieces):
+        tail = jnp.where(at == i, piece, tail)
+    out[rows : rows + 16, :] = tail.astype(BF16)
+
+
+def second_kernel(tok_count, masks, place, *refs):
+    count = len(masks)
+    queries, (keys, values), refs = refs[:count], refs[count : count + 2], refs[count + 2 :]
+    messages, x = refs[-5 - count : -5], refs[-1]
+    project_kernel(place, *refs[: -5 - count], *refs[-5:-1], x)
+    new_query = refs[-5]
+    rows = new_query.shape[0]
+    for mask, query, message in zip(masks, queries, messages, strict=True):
+        away_part(place, mask, query, keys, values, message, tok_count)
+        message[rows + 16 :, :] = new_query[...]
+
+
+def second_stage(tok_count, masks, place, queries, keys, values, pieces, wq, wk, wv, after=()):
     rows, width = queries[0].shape
+    full = wq.shape[0]
+    share = rows // (full // width)
+    tile = jax.ShapeDtypeStruct((rows, width), BF16)
+    message = jax.ShapeDtypeStruct((2 * rows + 16, width), BF16)
+    outs = (message,) * len(masks) + (tile, tile, tile, jax.ShapeDtypeStruct((share, full), BF16))
+    results = call(
+        functools.partial(second_kernel, tok_count, masks),
+        (place, *queries, keys, values, *pieces, wq, wk, wv),
+        after,
+        out_shape=outs,
+        in_specs=[SMEM] + [VMEM] * (len(masks) + len(pieces) + 5),
+        out_specs=(VMEM,) * len(outs),
+        scratch_shapes=[pltpu.VMEM((rows, full), BF16)],
+        compiler_params=params(),
+        cost_estimate=cost(4 * rows * width * keys.shape[0] + 6 * rows * full * width, 8 * full * width),
+        name="second_stage",
+    )
+    return results[: len(masks)], results[len(masks) :]
+
+
+def third_kernel(share, tok_count, masks, place, mixed, logs, *refs):
+    count = len(masks)
+    messages, (keys, values), (keep, send), outs, whole = (
+        refs[:count],
+        refs[count : count + 2],
+        refs[count + 2 : count + 4],
+        refs[count + 4 : -1],
+        refs[-1],
+    )
+    combine_kernel(share, place, mixed, logs, *messages, keep, send, whole)
+    rows = mixed.shape[0]
+    for mask, message, out in zip(masks, messages, outs, strict=True):
+        away_part(place, mask, message.at[pl.ds(rows + 16, rows), :], keys, values, out, tok_count)
+
+
+def third_stage(share, tok_count, masks, place, mixed, logs, messages, keys, values, after=()):
+    rows, width = mixed.shape
+    half = jax.ShapeDtypeStruct((rows // 2, width), BF16)
     message = jax.ShapeDtypeStruct((rows + 16, width), BF16)
-    return pl.pallas_call(
-        functools.partial(away_kernel, tok_count, masks),
-        out_shape=(message,) * len(masks),
-        in_specs=[SMEM] + [VMEM] * (len(masks) + 2),
-        out_specs=(VMEM,) * len(masks),
+    results = call(
+        functools.partial(third_kernel, share, tok_count, masks),
+        (place, mixed, logs, *messages, keys, values),
+        after,
+        out_shape=(half, half) + (message,) * len(masks),
+        in_specs=[SMEM] + [VMEM] * (4 + len(masks)),
+        out_specs=(VMEM,) * (2 + len(masks)),
+        scratch_shapes=[pltpu.VMEM((rows, width), BF16)],
         compiler_params=params(),
         cost_estimate=cost(4 * rows * width * keys.shape[0], 4 * keys.shape[0] * width),
-        name="away_parts",
-    )(place, *queries, keys, values)
+        name="third_stage",
+    )
+    return results[:2], results[2:]
 
 
 def combine_kernel(share, place, mixed, logs, *refs):
     *messages, keep_out, send_out, whole = refs
     rows, width = mixed.shape
-    tails = [message[rows:, :].astype(F32) for message in messages]
+    tails = [message[rows : rows + 16, :].astype(F32) for message in messages]
     for j in range(width // HEAD_DIM):
         cols = slice(j * HEAD_DIM, (j + 1) * HEAD_DIM)
         parts = [(mixed[:, cols], logs[:, cols])]
@@ -208,11 +283,13 @@
         send_out[slot * share : (slot + 1) * share, :] = whole[pl.ds(other, share), :]
 
 
-def combine(share, place, mixed, logs, messages):
+def combine(share, place, mixed, logs, messages, after=()):
     rows, width = mixed.shape
     half = jax.ShapeDtypeStruct((rows // 2, width), BF16)
-    return pl.pallas_call(
+    return call(
         functools.partial(combine_kernel, share),
+        (place, mixed, logs, *messages),
+        after,
         out_shape=(half, half),
         in_specs=[SMEM] + [VMEM] * (len(messages) + 2),
         out_specs=(VMEM, VMEM),
@@ -220,13 +297,88 @@
         compiler_params=params(),
         cost_estimate=cost(rows * width * 40, rows * width * 16),
         name="combine",
-    )(place, mixed, logs, *messages)
+    )
+
+
+def ids_kernel(vocab_here, place, ids, local_out, owner_out):
+    for slot in range(ids.shape[0]):
+        row = ids[pl.ds(jnp.bitwise_xor(place[0], slot), 1), :]
+        local_out[slot : slot + 1, :] = jnp.clip(row - place[0] * vocab_here, 0, vocab_here - 1)
+        if slot == 0:
+            owner = jnp.zeros(row.shape, jnp.int32)
+            for i in range(1, ids.shape[0]):
+                owner += jnp.where(row >= i * vocab_here, 1, 0)
+            owner_out[...] = owner
+
+
+def sort_ids(vocab_here, place, ids, after=()):
+    return call(
+        functools.partial(ids_kernel, vocab_here),
+        (place, ids),
+        after,
+        out_shape=(
+            jax.ShapeDtypeStruct(ids.shape, jnp.int32),
+            jax.ShapeDtypeStruct((1, ids.shape[1]), jnp.int32),
+        ),
+        in_specs=[SMEM, VMEM],
+        out_specs=(VMEM, VMEM),
+        compiler_params=params(),
+        name="sort_ids",
+    )
+
+
+def choose_kernel(place, accept, owner, states, *refs):
+    *found, out = refs
+    rows = states.shape[0]
+    slot = jnp.where(accept[...] == 1, jnp.bitwise_xor(owner[...], place[0]), len(found)).astype(F32)
+    slot = jnp.transpose(jnp.broadcast_to(slot, (128, rows)))
+    for start in range(0, states.shape[1], 128):
+        cols = slice(start, start + 128)
+        value = states[:, cols].astype(F32)
+        for i, rows_found in enumerate(found):
+            value = jnp.where(slot == i, rows_found[:, cols].astype(F32), value)
+        out[:, cols] = value.astype(BF16)
+
+
+def choose(place, accept, owner, states, found, after=()):
+    return call(
+        choose_kernel,
+        (place, accept, owner, states, *found),
+        after,
+        out_shape=jax.ShapeDtypeStruct(states.shape, BF16),
+        in_specs=[SMEM] + [VMEM] * (3 + len(found)),
+        out_specs=VMEM,
+        compiler_params=params(),
+        name="choose",
+    )
+
+
+def stack_kernel(*refs):
+    *pieces, out = refs
+    at = 0
+    for piece in pieces:
+        out[at : at + piece.shape[0], :] = piece[...]
+        at += piece.shape[0]
+
+
+def stack(pieces, after=()):
+    rows = sum(piece.shape[0] for piece in pieces)
+    return call(
+        stack_kernel,
+        tuple(pieces),
+        after,
+        out_shape=jax.ShapeDtypeStruct((rows, pieces[0].shape[1]), BF16),
+        in_specs=[VMEM] * len(pieces),
+        out_specs=VMEM,
+        compiler_params=params(),
+        name="stack",
+    )
 
 
 def out_kernel(keep, other, w_keep, w_other, *outs):
     share = outs[0].shape[0]
-    total = jnp.dot(keep[...], w_keep[...], preferred_element_type=F32)
-    total += jnp.dot(other[...], w_other[...], preferred_element_type=F32)
+    total = jnp.dot(other[...], w_other[...], preferred_element_type=F32)
+    total += jnp.dot(keep[...], w_keep[...], preferred_element_type=F32)
     for slot, out in enumerate(outs):
         out[...] = total[slot * share : (slot + 1) * share].astype(out.dtype)
 
@@ -246,11 +398,15 @@
 
 
 def finish_kernel(last, own, *refs):
-    *others, residual, attn_gain, final_gain, first_out = refs[: len(refs) - (0 if last else 2)]
+    *refs, attn_gain, final_gain, sems = refs
+    *others, residual, attn_far, final_far, first_out = refs[: len(refs) - (0 if last else 2)]
+    copies = fetch((attn_far, final_far), (attn_gain, final_gain), sems)
     total = own[...]
     for other in others:
         total += other[...].astype(F32)
     scale = lax.rsqrt(jnp.mean(total * total, axis=1, keepdims=True) + EPSILON)
+    for copy in copies:
+        copy.wait()
     first = (residual[...].astype(F32) + total * scale * attn_gain[...]).astype(BF16)
     first_out[...] = first
     if not last:
@@ -262,18 +418,21 @@
         square_out[...] = jnp.broadcast_to(jnp.sum(squares, axis=0, keepdims=True), square_out.shape)
 
 
-def finish(last, own, others, residual, attn_gain, final_gain):
+def finish(last, own, others, residual, attn_gain, final_gain, after=()):
     state = jax.ShapeDtypeStruct(residual.shape, BF16)
     outs = (state,) if last else (state, state, jax.ShapeDtypeStruct((1, 128), F32))
-    return pl.pallas_call(
+    return call(
         functools.partial(finish_kernel, last),
+        (own, *others, residual, attn_gain, final_gain),
+        after,
         out_shape=outs,
-        in_specs=[VMEM] * (len(others) + 4),
+        in_specs=[VMEM] * (len(others) + 2) + [HBM] * 2,
         out_specs=(VMEM,) * len(outs),
+        scratch_shapes=[pltpu.VMEM(attn_gain.shape, F32)] * 2 + [pltpu.SemaphoreType.DMA((2,))],
         compiler_params=params(),
         cost_estimate=cost(residual.size * 20, residual.size * 12),
         name="finish",
-    )(own, *others, residual, attn_gain, final_gain)
+    )
 
 
 def logits_kernel(share, tok_count, place, mine, other, lm_block, best_out, x):
@@ -292,12 +451,14 @@
     best_out[...] = jnp.maximum(best_out[...], best)
 
 
-def largest_logits(share, tok_count, place, mine, other, lm_head):
+def largest_logits(share, tok_count, place, mine, other, lm_head, after=()):
     half, full = mine.shape
     vocab = lm_head.shape[0]
-    span = vocab // 7
-    return pl.pallas_call(
+    span = vocab // 4 if vocab % 64 == 0 else vocab // 7
+    return call(
         functools.partial(logits_kernel, share, tok_count),
+        (place, mine, other, lm_head),
+        after,
         out_shape=jax.ShapeDtypeStruct((8, 2 * half), F32),
         grid=(vocab // span,),
         in_specs=[SMEM, VMEM, VMEM, pl.BlockSpec((span, full), lambda i: (i, 0))],
@@ -306,7 +467,7 @@
         compiler_params=params(),
         cost_estimate=cost(4 * half * full * vocab, 2 * full * vocab),
         name="largest_logits",
-    )(place, mine, other, lm_head)
+    )
 
 
 def gather_best_kernel(place, square, *refs):
@@ -365,46 +526,73 @@
     def by_tok(value, mask):
         return lax.ppermute(value, "tok", xor_pairs(tok_count, mask))
 
-    def run_layer(features, last):
-        chip_pieces = [features] + [by_head(features, 2 * s) for s in range(1, chips)]
-        core_pieces = [by_head(piece, 1) for piece in chip_pieces]
-        pieces = [piece for pair in zip(chip_pieces, core_pieces, strict=True) for piece in pair]
-        query, key, value, residual = project(place, pieces, w_query, w_key, w_value)
-        queries = [by_tok(query, mask) for mask in tok_masks]
-        mixed, logs = own_part(tok_count, place, query, key, value, cache_keys, cache_values)
-        messages = away_parts(tok_count, tok_masks, place, queries, cache_keys, cache_values)
-        messages = [by_tok(message, mask) for mask, message in zip(tok_masks, messages, strict=True)]
-        keep, send = combine(share, place, mixed, logs, messages)
-        own, *sums = out_project(share, keep, by_head(send, 1), w_out, w_out_other)
-        sums = [by_head(total, 2 * s) for s, total in enumerate(sums, 1)]
-        return finish(last, own, sums, residual, *gains)
+    def spread(features):
+        pieces = [features] + [by_head(features, 2 * s) for s in range(1, chips)]
+        return pieces, [by_head(piece, 1) for piece in pieces]
+
+    def exchange(arrays):
+        return [by_tok(array, mask) for mask, array in zip(tok_masks, arrays, strict=True)]
+
+    def own_of(query, key, value, after=()):
+        return own_part(tok_count, place, query, key, value, cache_keys, cache_values, after)
+
+    def join(own, messages, after=()):
+        return combine(share, place, *own, messages, after)
+
+    def out_layer(keep, send):
+        return out_project(share, keep, by_head(send, 1), w_out, w_out_other)
+
+    def finish_layer(last, sums, residual, after=()):
+        own, *others = sums
+        others = [by_head(total, 2 * s) for s, total in enumerate(others, 1)]
+        return finish(last, own, others, residual, *gains, after)
+
 
     w_out_other = by_head(w_out, 1)
 
-    _, normed, square = run_layer(block_states, False)
-
     vocab_here = embed.shape[0]
-    local_ids = jnp.clip(token_ids - tok_index * vocab_here, 0, vocab_here - 1).reshape(tok_count, block_rows)
-    owners = lax.dynamic_slice_in_dim(token_ids, tok_index * block_rows, block_rows, 0) // vocab_here
-    chosen = block_states
-    for mask in range(tok_count):
-        other = jnp.bitwise_xor(tok_index, mask)
-        ids = lax.dynamic_slice_in_dim(local_ids, other, 1, 0)[0]
-        found = jnp.take(embed, ids, axis=0, mode="clip")
-        if mask:
-            found = by_tok(found, mask)
-        chosen = jnp.where(((accept == 1) & (owners == other))[:, None], found, chosen)
-    (hiddens,) = run_layer(chosen, True)
-
-    column = jnp.concatenate([normed] + [by_tok(normed, mask) for mask in tok_masks], axis=0)
+    ids, owners = sort_ids(vocab_here, place, token_ids.reshape(tok_count, block_rows))
+    found = embed.at[ids.reshape(-1)].get(mode="promise_in_bounds").reshape(tok_count, block_rows, -1)
+    found = [found[mask] for mask in range(tok_count)]
+    embedded = [found[0], *exchange(found[1:])]
+
+    pieces, others = spread(block_states)
+    query, key, value, residual = project(
+        block_rows, place, pieces + others, w_query, w_key, w_value, [w_out_other, found[1]]
+    )
+    queries = exchange([query] * len(tok_masks))
+    own = own_of(query, key, value)
+    chosen = choose(place, accept.reshape(1, -1), owners, block_states, embedded, queries[:1])
+    pieces, others = spread(chosen)
+    messages, (query, key, value, residual_two) = second_stage(
+        tok_count, tok_masks, place, queries, cache_keys, cache_values, pieces + others, w_query, w_key, w_value, [own[0]]
+    )
+    messages = exchange(messages)
+    own_two = own_of(query, key, value)
+    keep, messages = third_stage(
+        share, tok_count, tok_masks, place, *own, messages, cache_keys, cache_values, [own_two[0]]
+    )
+    messages = exchange(messages)
+    _, normed, square = finish_layer(False, out_layer(*keep), residual)
+
+    column = stack([normed] + exchange([normed] * len(tok_masks)), messages)
+
+    def best_of(piece, after=()):
+        return largest_logits(share, tok_count, place, piece, by_head(piece, 1), lm_head, after)
+
     if chips == 4:
         along_x, along_y = by_head(column, 2), by_head(column, 4)
         half = column.shape[0] // 2
-        across = jnp.concatenate([by_head(along_y[:half], 2), by_head(along_x[half:], 4)], axis=0)
+        across = stack([by_head(along_y[:half], 2), by_head(along_x[half:], 4)])
         columns = [column, along_x, along_y, across]
     else:
         columns = [column] + [by_head(column, 2 * s) for s in range(1, chips)]
-    bests = [largest_logits(share, tok_count, place, piece, by_head(piece, 1), lm_head) for piece in columns]
+    bests = []
+    for piece in columns:
+        bests.append(best_of(piece, bests[-1:]))
+    sums = out_layer(*join(own_two, messages))
+    (hiddens,) = finish_layer(True, sums, residual_two)
+
     best = gather_best(place, square, bests)
     is_max = lax.broadcasted_iota(jnp.int32, best.shape, 0) < chips
     for axis, size in (("head", head_count), ("tok", tok_count)):

time: 213 us -> 186 us (0.87)
  local copies, waits for them, and re-layouts: 44 us -> 26.3 us
  Pallas kernels: 56.6 us -> 40.5 us
  waiting for transfers between devices: 50.2 us -> 59.5 us
  other arithmetic: 5.46 us -> 2.22 us
    gather x4 -> x1, local copies, waits for them, and re-layouts: 31 us -> 11.2 us  [shards(): embed.at[ids.reshape(-1)].get(mode='promise_in_bounds')]
    pallas_call x14 -> x16, Pallas kernels: 55.1 us -> 39 us  [call(): return pl.pallas_call(body, in_specs=specs, **rest)(*operands, *after)]
    ppermute x31, waiting for transfers between devices: 16.8 us -> 25 us  [by_head(): return lax.ppermute(value, 'head', xor_pairs(head_count, mask))]
    ppermute x5, waiting for transfers between devices: 0.01 us -> 4.03 us  [shards(): other = lax.ppermute(best, axis, xor_pairs(size, mask))]
    ppermute x18 -> x15, waiting for transfers between devices: 33.5 us -> 30.5 us  [by_tok(): return lax.ppermute(value, 'tok', xor_pairs(tok_count, mask))]
    ppermute x5, starting transfers between devices: 4.49 us -> 6.85 us  [shards(): other = lax.ppermute(best, axis, xor_pairs(size, mask))]
    ppermute x18 -> x15, starting transfers between devices: 27.9 us -> 27.5 us  [by_tok(): return lax.ppermute(value, 'tok', xor_pairs(tok_count, mask))]
    unnamed x48 -> x41, local copies, waits for them, and re-layouts: 12.1 us -> 12.3 us
  transfers between devices with their start and end apart: 54 -> 51, of which waited for: 16 -> 17; matrix products, arithmetic and copies ran while one was open for 17% -> 8% of each run, Pallas kernels for 27% -> 14%
where the time goes in v2:
time: 186 us
  waiting for transfers between devices  59.5 us (32%)
  starting transfers between devices  56 us (30%)
  Pallas kernels  40.5 us (22%)
  local copies, waits for them, and re-layouts  26.3 us (14%)
  other arithmetic  2.22 us (1%)
    pallas_call x16, Pallas kernels, call(): return pl.pallas_call(body, in_specs=specs, **rest)(*operands, *after)  39 us
    ppermute x15, waiting for transfers between devices, by_tok(): return lax.ppermute(value, 'tok', xor_pairs(tok_count, mask))  30.5 us
    ppermute x15, starting transfers between devices, by_tok(): return lax.ppermute(value, 'tok', xor_pairs(tok_count, mask))  27.5 us
    ppermute x31, waiting for transfers between devices, by_head(): return lax.ppermute(value, 'head', xor_pairs(head_count, mask))  25 us
    ppermute x31, starting transfers between devices, by_head(): return lax.ppermute(value, 'head', xor_pairs(head_count, mask))  21.7 us
    unnamed x41, local copies, waits for them, and re-layouts  12.3 us
    gather x1, local copies, waits for them, and re-layouts, shards(): embed.at[ids.reshape(-1)].get(mode='promise_in_bounds')  11.2 us
    ppermute x5, starting transfers between devices, shards(): other = lax.ppermute(best, axis, xor_pairs(size, mask))  6.85 us
  transfers between devices with their start and end apart: 51, of which 17 were waited for; matrix products, arithmetic and copies ran while one was open for 8% of the time, Pallas kernels for 14%

profile of v2, /device:TPU:0, one launch (start us, length us, event | category | flops | bytes accessed | tf_op | source)
XLA Modules:
  0.0 185.7 jit_solution(9877106817783676790)
XLA Ops:
  1.2 2.6 %collective-permute-start = (bf16[256,256]{1,0:T(8,128)(2,1)}, bf16[256,256]{1,0:T(8,128)(2,1)S(1)}, u32[]{:S(2)}, u32[]{:S(2)}) collective-permute-start(bf16[256,256]{1,0:T(8,128)(2,1)} %refs_3_.5), channel_id=1, source_target_pairs={{0,2},{1,3},{2,0},{3,1},{4,6},{5,7},{6,4},{7,5},{8,10},{9,11},{10,... | collective-permute-start | bytes 393224 | tf_op jit(solution)/shard_map/ppermute | solution.py:524
  3.7 1.5 collective-permute-start.1
  7.9 11.2 %gather_fusion = bf16[1024,256]{1,0:T(8,128)(2,1)} fusion(bf16[25088,256]{1,0:T(8,128)(2,1)} %param.26, s32[1024]{0:T(1024)} %broadcast_clamp_fusion), kind=kCustom, calls=%fused_computation | custom fusion | bytes 1052672 | tf_op jit(solution)/shard_map/gather | solution.py:555
  20.1 1.4 fusion.2
  21.5 2.1 %collective-permute-start.11 = (bf16[256,256]{1,0:T(8,128)(2,1)S(1)}, bf16[256,256]{1,0:T(8,128)(2,1)S(1)}, u32[]{:S(2)}, u32[]{:S(2)}) collective-permute-start(bf16[256,256]{1,0:T(8,128)(2,1)S(1)} %get-tuple-element.74.refs_13_), channel_id=1, source_target_pairs={{0,8},{8,0},{16,24},{24,16},{1,9},{9,1},{17,25},{25,17},{2,10},{10... | collective-permute-start | bytes 393224 | tf_op jit(solution)/shard_map/ppermute | solution.py:527
  23.6 2.6 %collective-permute-start.12 = (bf16[256,256]{1,0:T(8,128)(2,1)S(1)}, bf16[256,256]{1,0:T(8,128)(2,1)S(1)}, u32[]{:S(2)}, u32[]{:S(2)}) collective-permute-start(bf16[256,256]{1,0:T(8,128)(2,1)S(1)} %get-tuple-element.72), channel_id=1, source_target_pairs={{0,16},{8,24},{16,0},{24,8},{1,17},{9,25},{17,1},{25,9},{2,18},{10... | collective-permute-start | bytes 393224 | tf_op jit(solution)/shard_map/ppermute | solution.py:527
  26.3 1.4 copy-done.5
  27.6 1.4 copy-done.7
  29.0 1.2 copy-done.9
  30.2 0.9 copy-done.11
  31.1 2.1 %project.1 = (bf16[256,256]{1,0:T(8,128)(2,1)S(1)}, bf16[256,256]{1,0:T(8,128)(2,1)S(1)}, bf16[256,256]{1,0:T(8,128)(2,1)S(1)}, bf16[32,2048]{1,0:T(8,128)(2,1)S(1)}) custom-call(s32[6]{0:T(128)S(1)} %pad_add_fusion.refs_0_.place, bf16[256,256]{1,0:T(8,128)(2,1)S(1)} %copy-done.11, bf16[256,256]{1,0:T(8,128)(2,1)S(1)} %collective-permute-done.refs_2_, ...), custom_call_target="tpu_custom_call" | custom-call | flops 805306368 | bytes 4194304 | tf_op jit(solution)/shard_map/project/pallas_call | solution.py:37
  33.2 0.9 collective-permute-start.8
  34.1 3.3 %collective-permute-start.9 = (bf16[256,256]{1,0:T(8,128)(2,1)S(1)}, bf16[256,256]{1,0:T(8,128)(2,1)S(1)}, u32[]{:S(2)}, u32[]{:S(2)}) collective-permute-start(bf16[256,256]{1,0:T(8,128)(2,1)S(1)} %get-tuple-element.38.refs_1_), channel_id=1, source_target_pairs={{0,16},{8,24},{16,0},{24,8},{1,17},{9,25},{17,1},{25,9},{2,18},{10... | collective-permute-start | bytes 393224 | tf_op jit(solution)/shard_map/ppermute | solution.py:527
  37.3 2.3 %collective-permute-done.8.refs_8_.refs_1_ = bf16[256,256]{1,0:T(8,128)(2,1)S(1)} collective-permute-done((bf16[256,256]{1,0:T(8,128)(2,1)S(1)}, bf16[256,256]{1,0:T(8,128)(2,1)S(1)}, u32[]{:S(2)}, u32[]{:S(2)}) %collective-permute-start.8) | collective-permute-done | bytes 131104 | tf_op jit(solution)/shard_map/ppermute | solution.py:527
  39.7 0.9 copy-done.12
  42.0 1.6 collective-permute-start.14
  43.5 1.5 collective-permute-start.15
  45.5 2.6 %collective-permute-start.10 = (bf16[256,256]{1,0:T(8,128)(2,1)S(1)}, bf16[256,256]{1,0:T(8,128)(2,1)S(1)}, u32[]{:S(2)}, u32[]{:S(2)}) collective-permute-start(bf16[256,256]{1,0:T(8,128)(2,1)S(1)} %get-tuple-element.38.refs_1_), channel_id=1, source_target_pairs={{0,24},{8,16},{16,8},{24,0},{1,25},{9,17},{17,9},{25,1},{2,26},{10... | collective-permute-start | bytes 393224 | tf_op jit(solution)/shard_map/ppermute | solution.py:527
  48.6 2.6 %collective-permute-done.15.refs_8_ = bf16[256,256]{1,0:T(8,128)(2,1)S(1)} collective-permute-done((bf16[256,256]{1,0:T(8,128)(2,1)S(1)}, bf16[256,256]{1,0:T(8,128)(2,1)S(1)}, u32[]{:S(2)}, u32[]{:S(2)}) %collective-permute-start.15) | collective-permute-done | bytes 131104 | tf_op jit(solution)/shard_map/ppermute | solution.py:524
  51.7 1.0 copy-done
  52.7 1.0 copy-done.2
  53.8 2.0 %own_part.2 = (f32[256,256]{1,0:T(8,128)S(1)}, f32[256,256]{1,0:T(8,128)S(1)}) custom-call(s32[6]{0:T(128)S(1)} %pad_add_fusion.refs_0_.place, bf16[256,256]{1,0:T(8,128)(2,1)S(1)} %get-tuple-element.38.refs_1_, bf16[256,256]{1,0:T(8,128)(2,1)S(1)} %get-tuple-element.40.refs_2_, bf16[256,256]{1,0:T(8,128)(2,1)S(1)} %get-tuple-element.41.refs_3_, ...), custom_call_target="tpu_custom_call" | custom-call | flops 268435456 | bytes 1048576 | tf_op jit(solution)/shard_map/own_part/pallas_call | solution.py:37
  55.9 1.2 copy-done.6
  57.1 1.2 copy-done.8
  58.3 1.2 copy-done.10
  59.6 4.9 %second_stage.1 = (bf16[528,256]{1,0:T(8,128)(2,1)S(1)}, bf16[528,256]{1,0:T(8,128)(2,1)S(1)}, bf16[528,256]{1,0:T(8,128)(2,1)S(1)}, bf16[256,256]{1,0:T(8,128)(...) custom-call(s32[6]{0:T(128)S(1)} %pad_add_fusion.refs_0_.place, ...), custom_call_target="tpu_custom_call" | custom-call | flops 1073741824 | bytes 4194304 | tf_op jit(solution)/shard_map/second_stage/pallas_call | solution.py:37
  64.5 2.3 %collective-permute-start.22 = (bf16[528,256]{1,0:T(8,128)(2,1)S(1)}, bf16[528,256]{1,0:T(8,128)(2,1)S(1)}, u32[]{:S(2)}, u32[]{:S(2)}) collective-permute-start(bf16[528,256]{1,0:T(8,128)(2,1)S(1)} %get-tuple-element.50), channel_id=1, source_target_pairs={{0,16},{8,24},{16,0},{24,8},{1,17},{9,25},{17,1},{25,9},{2,18},{10... | collective-permute-start | bytes 811016 | tf_op jit(solution)/shard_map/ppermute | solution.py:527
  66.8 2.1 %collective-permute-start.23 = (bf16[528,256]{1,0:T(8,128)(2,1)S(1)}, bf16[528,256]{1,0:T(8,128)(2,1)S(1)}, u32[]{:S(2)}, u32[]{:S(2)}) collective-permute-start(bf16[528,256]{1,0:T(8,128)(2,1)S(1)} %get-tuple-element.51), channel_id=1, source_target_pairs={{0,24},{8,16},{16,8},{24,0},{1,25},{9,17},{17,9},{25,1},{2,26},{10... | collective-permute-start | bytes 811016 | tf_op jit(solution)/shard_map/ppermute | solution.py:527
  68.9 2.0 %own_part.3 = (f32[256,256]{1,0:T(8,128)S(1)}, f32[256,256]{1,0:T(8,128)S(1)}) custom-call(s32[6]{0:T(128)S(1)} %pad_add_fusion.refs_0_.place, bf16[256,256]{1,0:T(8,128)(2,1)S(1)} %get-tuple-element.43.refs_1_, bf16[256,256]{1,0:T(8,128)(2,1)S(1)} %get-tuple-element.44.refs_2_, bf16[256,256]{1,0:T(8,128)(2,1)S(1)} %get-tuple-element.45.refs_3_, ...), custom_call_target="tpu_custom_call" | custom-call | flops 268435456 | bytes 1048576 | tf_op jit(solution)/shard_map/own_part/pallas_call | solution.py:37
  70.9 7.5 %collective-permute-done.21.refs_3_ = bf16[528,256]{1,0:T(8,128)(2,1)S(1)} collective-permute-done((bf16[528,256]{1,0:T(8,128)(2,1)S(1)}, bf16[528,256]{1,0:T(8,128)(2,1)S(1)}, u32[]{:S(2)}, u32[]{:S(2)}) %collective-permute-start.21) | collective-permute-done | bytes 270368 | tf_op jit(solution)/shard_map/ppermute | solution.py:527
  78.4 8.0 %collective-permute-done.22.refs_4_ = bf16[528,256]{1,0:T(8,128)(2,1)S(1)} collective-permute-done((bf16[528,256]{1,0:T(8,128)(2,1)S(1)}, bf16[528,256]{1,0:T(8,128)(2,1)S(1)}, u32[]{:S(2)}, u32[]{:S(2)}) %collective-permute-start.22) | collective-permute-done | bytes 270368 | tf_op jit(solution)/shard_map/ppermute | solution.py:527
  86.5 4.4 %third_stage.1 = (bf16[128,256]{1,0:T(8,128)(2,1)S(1)}, bf16[128,256]{1,0:T(8,128)(2,1)S(1)}, bf16[272,256]{1,0:T(8,128)(2,1)S(1)}, bf16[272,256]{1,0:T(8,128)(2,1)S(1)}, bf16[272,256]{1,0:T(8,128)(2,1)S(1)}) custom-call(s32[6]{0:T(128)S(1)} %pad_add_fusion.refs_0_.place, f32[256,256]{1,0:T(8,128)S(1)} %get-tuple-element.42.refs_17_.refs_1_, ...), custom_call_target="tpu_custom_call" | custom-call | flops 268435456 | bytes 1048576 | tf_op jit(solution)/shard_map/third_stage/pallas_call | solution.py:37
  90.9 1.2 collective-permute-done.31.other
  92.8 4.8 %collective-permute-start.24 = (bf16[272,256]{1,0:T(8,128)(2,1)S(1)}, bf16[272,256]{1,0:T(8,128)(2,1)S(1)}, u32[]{:S(2)}, u32[]{:S(2)}) collective-permute-start(bf16[272,256]{1,0:T(8,128)(2,1)S(1)} %get-tuple-element.52), channel_id=1, source_target_pairs={{0,8},{8,0},{16,24},{24,16},{1,9},{9,1},{17,25},{25,17},{2,10},{10... | collective-permute-start | bytes 417800 | tf_op jit(solution)/shard_map/ppermute | solution.py:527
  97.6 0.9 collective-permute-start.33
  98.5 2.2 %collective-permute-start.34 = (bf16[32,2048]{1,0:T(8,128)(2,1)S(1)}, bf16[32,2048]{1,0:T(8,128)(2,1)S(1)}, u32[]{:S(2)}, u32[]{:S(2)}) collective-permute-start(bf16[32,2048]{1,0:T(8,128)(2,1)S(1)} %get-tuple-element.67), channel_id=1, source_target_pairs={{0,6},{1,7},{2,4},{3,5},{4,2},{5,3},{6,0},{7,1},{8,14},{9,15},{10,... | collective-permute-start | bytes 393224 | tf_op jit(solution)/shard_map/ppermute | solution.py:524
  100.7 2.4 %collective-permute-start.26 = (bf16[272,256]{1,0:T(8,128)(2,1)S(1)}, bf16[272,256]{1,0:T(8,128)(2,1)S(1)}, u32[]{:S(2)}, u32[]{:S(2)}) collective-permute-start(bf16[272,256]{1,0:T(8,128)(2,1)S(1)} %get-tuple-element.54), channel_id=1, source_target_pairs={{0,24},{8,16},{16,8},{24,0},{1,25},{9,17},{17,9},{25,1},{2,26},{10... | collective-permute-start | bytes 417800 | tf_op jit(solution)/shard_map/ppermute | solution.py:527
  103.1 2.4 %collective-permute-done.33.refs_2_ = bf16[32,2048]{1,0:T(8,128)(2,1)S(1)} collective-permute-done((bf16[32,2048]{1,0:T(8,128)(2,1)S(1)}, bf16[32,2048]{1,0:T(8,128)(2,1)S(1)}, u32[]{:S(2)}, u32[]{:S(2)}) %collective-permute-start.33) | collective-permute-done | bytes 131104 | tf_op jit(solution)/shard_map/ppermute | solution.py:524
  105.5 0.9 finish.3
  107.0 1.5 collective-permute-start.36
  108.5 2.3 %collective-permute-start.37 = (bf16[32,2048]{1,0:T(8,128)(2,1)S(1)}, bf16[32,2048]{1,0:T(8,128)(2,1)S(1)}, u32[]{:S(2)}, u32[]{:S(2)}) collective-permute-start(bf16[32,2048]{1,0:T(8,128)(2,1)S(1)} %get-tuple-element.70.refs_0_), channel_id=1, source_target_pairs={{0,24},{8,16},{16,8},{24,0},{1,25},{9,17},{17,9},{25,1},{2,26},{10... | collective-permute-start | bytes 393224 | tf_op jit(solution)/shard_map/ppermute | solution.py:527
  110.8 6.8 %collective-permute-done.25.refs_4_.refs_5_ = bf16[272,256]{1,0:T(8,128)(2,1)S(1)} collective-permute-done((bf16[272,256]{1,0:T(8,128)(2,1)S(1)}, bf16[272,256]{1,0:T(8,128)(2,1)S(1)}, u32[]{:S(2)}, u32[]{:S(2)}) %collective-permute-start.25) | collective-permute-done | bytes 139296 | tf_op jit(solution)/shard_map/ppermute | solution.py:527
  117.7 5.8 %collective-permute-done.36.refs_2_ = bf16[32,2048]{1,0:T(8,128)(2,1)S(1)} collective-permute-done((bf16[32,2048]{1,0:T(8,128)(2,1)S(1)}, bf16[32,2048]{1,0:T(8,128)(2,1)S(1)}, u32[]{:S(2)}, u32[]{:S(2)}) %collective-permute-start.36) | collective-permute-done | bytes 131104 | tf_op jit(solution)/shard_map/ppermute | solution.py:527
  123.5 1.2 collective-permute-start.39
  125.2 12.1 %collective-permute-done.39.refs_1_ = bf16[128,2048]{1,0:T(8,128)(2,1)S(1)} collective-permute-done((bf16[128,2048]{1,0:T(8,128)(2,1)S(1)}, bf16[128,2048]{1,0:T(8,128)(2,1)S(1)}, u32[]{:S(2)}, u32[]{:S(2)}) %collective-permute-start.39) | collective-permute-done | bytes 524320 | tf_op jit(solution)/shard_map/ppermute | solution.py:524
  137.4 1.7 collective-permute-start.43
  139.2 1.1 collective-permute-start.44
  140.3 4.9 %largest_logits.4.refs_4_.refs_0_ = f32[8,256]{1,0:T(8,128)S(1)} custom-call(s32[6]{0:T(128)S(1)} %pad_add_fusion.refs_0_.place, bf16[128,2048]{1,0:T(8,128)(2,1)S(1)} %stack.10.refs_1_, bf16[128,2048]{1,0:T(8,128)(2,1)S(1)} %collective-permute-done.38.refs_2_, bf16[3136,2048]{1,0:T(8,128)(2,1)S(1)} %bitcast.16), custom_call_target="tpu_custom_call" | custom-call | flops 3288334336 | bytes 12845056 | tf_op jit(solution)/shard_map/largest_logits/pallas_call | solution.py:37
  145.2 0.9 collective-permute-done.43.refs_0_
  146.3 4.9 %largest_logits.5.refs_4_.refs_1_ = f32[8,256]{1,0:T(8,128)S(1)} custom-call(s32[6]{0:T(128)S(1)} %pad_add_fusion.refs_0_.place, bf16[128,2048]{1,0:T(8,128)(2,1)S(1)} %collective-permute-done.39.refs_1_, bf16[128,2048]{1,0:T(8,128)(2,1)S(1)} %collective-permute-done.40.refs_2_, bf16[3136,2048]{1,0:T(8,128)(2,1)S(1)} %bitcast.16, ...), custom_call_target="tpu_custom_call" | custom-call | flops 3288334336 | bytes 12845056 | tf_op jit(solution)/shard_map/largest_logits/pallas_call | solution.py:37
  151.2 4.9 %largest_logits.6.refs_4_.refs_2_ = f32[8,256]{1,0:T(8,128)S(1)} custom-call(s32[6]{0:T(128)S(1)} %pad_add_fusion.refs_0_.place, bf16[128,2048]{1,0:T(8,128)(2,1)S(1)} %collective-permute-done.41.refs_1_, bf16[128,2048]{1,0:T(8,128)(2,1)S(1)} %collective-permute-done.42.refs_2_, bf16[3136,2048]{1,0:T(8,128)(2,1)S(1)} %bitcast.16, ...), custom_call_target="tpu_custom_call" | custom-call | flops 3288334336 | bytes 12845056 | tf_op jit(solution)/shard_map/largest_logits/pallas_call | solution.py:37
  156.1 4.9 %largest_logits.7.refs_3_ = f32[8,256]{1,0:T(8,128)S(1)} custom-call(s32[6]{0:T(128)S(1)} %pad_add_fusion.refs_0_.place, bf16[128,2048]{1,0:T(8,128)(2,1)S(1)} %stack.11.refs_1_, bf16[128,2048]{1,0:T(8,128)(2,1)S(1)} %collective-permute-done.45.refs_2_, bf16[3136,2048]{1,0:T(8,128)(2,1)S(1)} %bitcast.16, f32[8,256]{1,0:T(8,128)S(1)} %largest_logits.6.refs_4_.refs_2_), custom_call_target="tpu_custom_call" | custom-call | flops 3288334336 | bytes 12845056 | tf_op jit(solution)/shard_map/largest_logits/pallas_call | solution.py:37
  162.1 0.8 collective-permute-done.46
  163.0 1.7 collective-permute-start.47
  164.7 1.9 %collective-permute-done.47 = f32[8,256]{1,0:T(8,128)S(1)} collective-permute-done((f32[8,256]{1,0:T(8,128)S(1)}, f32[8,256]{1,0:T(8,128)S(1)}, u32[]{:S(2)}, u32[]{:S(2)}) %collective-permute-start.47) | collective-permute-done | bytes 8224 | tf_op jit(solution)/shard_map/ppermute | solution.py:601
  166.7 1.3 collective-permute-start.48
  168.0 1.0 combine.1
  169.1 1.3 collective-permute-done.48
  170.4 3.4 %collective-permute-start.49 = (f32[8,256]{1,0:T(8,128)S(1)}, f32[8,256]{1,0:T(8,128)S(1)}, u32[]{:S(2)}, u32[]{:S(2)}) collective-permute-start(f32[8,256]{1,0:T(8,128)S(1)} %add_select_fusion.2), channel_id=1, source_target_pairs={{0,8},{8,0},{16,24},{24,16},{1,9},{9,1},{17,25},{25,17},{2,10},{10... | collective-permute-start | bytes 24584 | tf_op jit(solution)/shard_map/ppermute | solution.py:601
  174.3 1.8 collective-permute-start.28
  176.1 1.0 collective-permute-start.29
  177.9 2.5 %collective-permute-done.28.refs_1_ = bf16[32,2048]{1,0:T(8,128)(2,1)S(1)} collective-permute-done((bf16[32,2048]{1,0:T(8,128)(2,1)S(1)}, bf16[32,2048]{1,0:T(8,128)(2,1)S(1)}, u32[]{:S(2)}, u32[]{:S(2)}) %collective-permute-start.28) | collective-permute-done | bytes 131104 | tf_op jit(solution)/shard_map/ppermute | solution.py:524
  180.4 3.0 %collective-permute-done.29.refs_2_ = bf16[32,2048]{1,0:T(8,128)(2,1)S(1)} collective-permute-done((bf16[32,2048]{1,0:T(8,128)(2,1)S(1)}, bf16[32,2048]{1,0:T(8,128)(2,1)S(1)}, u32[]{:S(2)}, u32[]{:S(2)}) %collective-permute-start.29) | collective-permute-done | bytes 131104 | tf_op jit(solution)/shard_map/ppermute | solution.py:524
  183.4 0.9 finish.2
  (118 shorter events, 13.4 us)
Async XLA Ops:
  0.6 91.5 %copy-start.4 = (bf16[256,2048]{1,0:T(8,128)(2,1)S(1)}, bf16[256,2048]{1,0:T(8,128)(2,1)}, u32[]{:S(2)}) copy-start(bf16[256,2048]{1,0:T(8,128)(2,1)} %w_keep.3) | copy-start | bytes 3145732
  0.6 55.2 %copy-start.1 = (bf16[1024,256]{1,0:T(8,128)(2,1)S(1)}, bf16[1024,256]{1,0:T(8,128)(2,1)}, u32[]{:S(2)}) copy-start(bf16[1024,256]{1,0:T(8,128)(2,1)} %refs_6_.1) | copy-start | bytes 1572868
  0.7 55.2 %copy-start.3 = (bf16[1024,256]{1,0:T(8,128)(2,1)S(1)}, bf16[1024,256]{1,0:T(8,128)(2,1)}, u32[]{:S(2)}) copy-start(bf16[1024,256]{1,0:T(8,128)(2,1)} %refs_7_.1) | copy-start | bytes 1572868
  0.7 25.6 %collective-permute-start.7 = (bf16[256,2048]{1,0:T(8,128)(2,1)}, bf16[256,2048]{1,0:T(8,128)(2,1)S(1)}, u32[]{:S(2)}, u32[]{:S(2)}) collective-permute-start(bf16[256,2048]{1,0:T(8,128)(2,1)} %w_keep.3), channel_id=1, source_target_pairs={{0,1},{1,0},{2,3},{3,2},{4,5},{5,4},{6,7},{7,6},{8,9},{9,8},{10,11... | collective-permute-start | bytes 3145736 | tf_op jit(solution)/shard_map/ppermute | solution.py:524
  1.2 17.9 %collective-permute-start = (bf16[256,256]{1,0:T(8,128)(2,1)}, bf16[256,256]{1,0:T(8,128)(2,1)S(1)}, u32[]{:S(2)}, u32[]{:S(2)}) collective-permute-start(bf16[256,256]{1,0:T(8,128)(2,1)} %refs_3_.5), channel_id=1, source_target_pairs={{0,2},{1,3},{2,0},{3,1},{4,6},{5,7},{6,4},{7,5},{8,10},{9,11},{10,... | collective-permute-start | bytes 393224 | tf_op jit(solution)/shard_map/ppermute | solution.py:524
  3.7 15.9 %collective-permute-start.1 = (bf16[256,256]{1,0:T(8,128)(2,1)}, bf16[256,256]{1,0:T(8,128)(2,1)S(1)}, u32[]{:S(2)}, u32[]{:S(2)}) collective-permute-start(bf16[256,256]{1,0:T(8,128)(2,1)} %refs_3_.5), channel_id=1, source_target_pairs={{0,4},{1,5},{2,6},{3,7},{4,0},{5,1},{6,2},{7,3},{8,12},{9,13},{10,... | collective-permute-start | bytes 393224 | tf_op jit(solution)/shard_map/ppermute | solution.py:524
  5.3 14.5 %collective-permute-start.2 = (bf16[256,256]{1,0:T(8,128)(2,1)}, bf16[256,256]{1,0:T(8,128)(2,1)S(1)}, u32[]{:S(2)}, u32[]{:S(2)}) collective-permute-start(bf16[256,256]{1,0:T(8,128)(2,1)} %refs_3_.5), channel_id=1, source_target_pairs={{0,6},{1,7},{2,4},{3,5},{4,2},{5,3},{6,0},{7,1},{8,14},{9,15},{10,... | collective-permute-start | bytes 393224 | tf_op jit(solution)/shard_map/ppermute | solution.py:524
  5.3 16.2 %collective-permute-start.3 = (bf16[256,256]{1,0:T(8,128)(2,1)}, bf16[256,256]{1,0:T(8,128)(2,1)}, u32[]{:S(2)}, u32[]{:S(2)}) collective-permute-start(bf16[256,256]{1,0:T(8,128)(2,1)} %refs_3_.5), channel_id=1, source_target_pairs={{0,1},{1,0},{2,3},{3,2},{4,5},{5,4},{6,7},{7,6},{8,9},{9,8},{10,11... | collective-permute-start | bytes 393224 | tf_op jit(solution)/shard_map/ppermute | solution.py:524
  7.9 97.5 %copy-start.13 = (f32[2048]{0:T(1024)S(1)}, f32[2048]{0:T(1024)}, u32[]{:S(2)}) copy-start(f32[2048]{0:T(1024)} %param.24) | copy-start | bytes 24580
  19.1 121.1 %slice-start = ((s8[12845056]{0:T(1024)(128)(4,1)}), s8[4194304]{0:T(1024)(128)(4,1)S(1)}, s32[]{:S(2)}) async-start(s8[12845056]{0:T(1024)(128)(4,1)} %bitcast.15), calls=%async_computation | async-start | bytes 8388608
  19.1 4.5 %collective-permute-start.4 = (bf16[256,256]{1,0:T(8,128)(2,1)S(1)}, bf16[256,256]{1,0:T(8,128)(2,1)S(1)}, u32[]{:S(2)}, u32[]{:S(2)}) collective-permute-start(bf16[256,256]{1,0:T(8,128)(2,1)S(1)} %collective-permute-done.refs_2_), channel_id=1, source_target_pairs={{0,1},{1,0},{2,3},{3,2},{4,5},{5,4},{6,7},{7,6},{8,9},{9,8},{10,11... | collective-permute-start | bytes 393224 | tf_op jit(solution)/shard_map/ppermute | solution.py:524
  19.6 6.6 %collective-permute-start.5 = (bf16[256,256]{1,0:T(8,128)(2,1)S(1)}, bf16[256,256]{1,0:T(8,128)(2,1)S(1)}, u32[]{:S(2)}, u32[]{:S(2)}) collective-permute-start(bf16[256,256]{1,0:T(8,128)(2,1)S(1)} %collective-permute-done.1.refs_3_), channel_id=1, source_target_pairs={{0,1},{1,0},{2,3},{3,2},{4,5},{5,4},{6,7},{7,6},{8,9},{9,8},{10,11... | collective-permute-start | bytes 393224 | tf_op jit(solution)/shard_map/ppermute | solution.py:524
  19.7 6.5 %collective-permute-start.6 = (bf16[256,256]{1,0:T(8,128)(2,1)S(1)}, bf16[256,256]{1,0:T(8,128)(2,1)S(1)}, u32[]{:S(2)}, u32[]{:S(2)}) collective-permute-start(bf16[256,256]{1,0:T(8,128)(2,1)S(1)} %collective-permute-done.2.refs_4_), channel_id=1, source_target_pairs={{0,1},{1,0},{2,3},{3,2},{4,5},{5,4},{6,7},{7,6},{8,9},{9,8},{10,11... | collective-permute-start | bytes 393224 | tf_op jit(solution)/shard_map/ppermute | solution.py:524
  21.5 15.8 %collective-permute-start.11 = (bf16[256,256]{1,0:T(8,128)(2,1)S(1)}, bf16[256,256]{1,0:T(8,128)(2,1)S(1)}, u32[]{:S(2)}, u32[]{:S(2)}) collective-permute-start(bf16[256,256]{1,0:T(8,128)(2,1)S(1)} %get-tuple-element.74.refs_13_), channel_id=1, source_target_pairs={{0,8},{8,0},{16,24},{24,16},{1,9},{9,1},{17,25},{25,17},{2,10},{10... | collective-permute-start | bytes 393224 | tf_op jit(solution)/shard_map/ppermute | solution.py:527
  23.6 13.7 %collective-permute-start.12 = (bf16[256,256]{1,0:T(8,128)(2,1)S(1)}, bf16[256,256]{1,0:T(8,128)(2,1)S(1)}, u32[]{:S(2)}, u32[]{:S(2)}) collective-permute-start(bf16[256,256]{1,0:T(8,128)(2,1)S(1)} %get-tuple-element.72), channel_id=1, source_target_pairs={{0,16},{8,24},{16,0},{24,8},{1,17},{9,25},{17,1},{25,9},{2,18},{10... | collective-permute-start | bytes 393224 | tf_op jit(solution)/shard_map/ppermute | solution.py:527
  26.2 114.0 %slice-start.1 = ((s8[12845056]{0:T(1024)(128)(4,1)}), s8[4194304]{0:T(1024)(128)(4,1)S(1)}, s32[]{:S(2)}) async-start(s8[12845056]{0:T(1024)(128)(4,1)} %bitcast.15), calls=%async_computation.1 | async-start | bytes 8388608
  26.2 11.1 %collective-permute-start.13 = (bf16[256,256]{1,0:T(8,128)(2,1)S(1)}, bf16[256,256]{1,0:T(8,128)(2,1)S(1)}, u32[]{:S(2)}, u32[]{:S(2)}) collective-permute-start(bf16[256,256]{1,0:T(8,128)(2,1)S(1)} %get-tuple-element.71), channel_id=1, source_target_pairs={{0,24},{8,16},{16,8},{24,0},{1,25},{9,17},{17,9},{25,1},{2,26},{10... | collective-permute-start | bytes 393224 | tf_op jit(solution)/shard_map/ppermute | solution.py:527
  26.2 1.4 copy-start.5
  27.6 1.4 copy-start.7
  29.0 1.2 copy-start.9
  33.2 6.4 %collective-permute-start.8 = (bf16[256,256]{1,0:T(8,128)(2,1)S(1)}, bf16[256,256]{1,0:T(8,128)(2,1)S(1)}, u32[]{:S(2)}, u32[]{:S(2)}) collective-permute-start(bf16[256,256]{1,0:T(8,128)(2,1)S(1)} %get-tuple-element.38.refs_1_), channel_id=1, source_target_pairs={{0,8},{8,0},{16,24},{24,16},{1,9},{9,1},{17,25},{25,17},{2,10},{10... | collective-permute-start | bytes 393224 | tf_op jit(solution)/shard_map/ppermute | solution.py:527
  34.1 14.1 %collective-permute-start.9 = (bf16[256,256]{1,0:T(8,128)(2,1)S(1)}, bf16[256,256]{1,0:T(8,128)(2,1)S(1)}, u32[]{:S(2)}, u32[]{:S(2)}) collective-permute-start(bf16[256,256]{1,0:T(8,128)(2,1)S(1)} %get-tuple-element.38.refs_1_), channel_id=1, source_target_pairs={{0,16},{8,24},{16,0},{24,8},{1,17},{9,25},{17,1},{25,9},{2,18},{10... | collective-permute-start | bytes 393224 | tf_op jit(solution)/shard_map/ppermute | solution.py:527
  42.0 6.2 %collective-permute-start.14 = (bf16[256,256]{1,0:T(8,128)(2,1)S(1)}, bf16[256,256]{1,0:T(8,128)(2,1)S(1)}, u32[]{:S(2)}, u32[]{:S(2)}) collective-permute-start(bf16[256,256]{1,0:T(8,128)(2,1)S(1)} %choose.1.refs_6_), channel_id=1, source_target_pairs={{0,2},{1,3},{2,0},{3,1},{4,6},{5,7},{6,4},{7,5},{8,10},{9,11},{10,... | collective-permute-start | bytes 393224 | tf_op jit(solution)/shard_map/ppermute | solution.py:524
  43.5 7.7 %collective-permute-start.15 = (bf16[256,256]{1,0:T(8,128)(2,1)S(1)}, bf16[256,256]{1,0:T(8,128)(2,1)S(1)}, u32[]{:S(2)}, u32[]{:S(2)}) collective-permute-start(bf16[256,256]{1,0:T(8,128)(2,1)S(1)} %choose.1.refs_6_), channel_id=1, source_target_pairs={{0,4},{1,5},{2,6},{3,7},{4,0},{5,1},{6,2},{7,3},{8,12},{9,13},{10,... | collective-permute-start | bytes 393224 | tf_op jit(solution)/shard_map/ppermute | solution.py:524
  45.0 6.2 %collective-permute-start.16 = (bf16[256,256]{1,0:T(8,128)(2,1)S(1)}, bf16[256,256]{1,0:T(8,128)(2,1)S(1)}, u32[]{:S(2)}, u32[]{:S(2)}) collective-permute-start(bf16[256,256]{1,0:T(8,128)(2,1)S(1)} %choose.1.refs_6_), channel_id=1, source_target_pairs={{0,6},{1,7},{2,4},{3,5},{4,2},{5,3},{6,0},{7,1},{8,14},{9,15},{10,... | collective-permute-start | bytes 393224 | tf_op jit(solution)/shard_map/ppermute | solution.py:524
  45.5 10.3 %collective-permute-start.10 = (bf16[256,256]{1,0:T(8,128)(2,1)S(1)}, bf16[256,256]{1,0:T(8,128)(2,1)S(1)}, u32[]{:S(2)}, u32[]{:S(2)}) collective-permute-start(bf16[256,256]{1,0:T(8,128)(2,1)S(1)} %get-tuple-element.38.refs_1_), channel_id=1, source_target_pairs={{0,24},{8,16},{16,8},{24,0},{1,25},{9,17},{17,9},{25,1},{2,26},{10... | collective-permute-start | bytes 393224 | tf_op jit(solution)/shard_map/ppermute | solution.py:527
  48.1 7.7 %collective-permute-start.17 = (bf16[256,256]{1,0:T(8,128)(2,1)S(1)}, bf16[256,256]{1,0:T(8,128)(2,1)S(1)}, u32[]{:S(2)}, u32[]{:S(2)}) collective-permute-start(bf16[256,256]{1,0:T(8,128)(2,1)S(1)} %choose.1.refs_6_), channel_id=1, source_target_pairs={{0,1},{1,0},{2,3},{3,2},{4,5},{5,4},{6,7},{7,6},{8,9},{9,8},{10,11... | collective-permute-start | bytes 393224 | tf_op jit(solution)/shard_map/ppermute | solution.py:524
  48.1 7.7 %collective-permute-start.18 = (bf16[256,256]{1,0:T(8,128)(2,1)S(1)}, bf16[256,256]{1,0:T(8,128)(2,1)S(1)}, u32[]{:S(2)}, u32[]{:S(2)}) collective-permute-start(bf16[256,256]{1,0:T(8,128)(2,1)S(1)} %collective-permute-done.14.refs_7_), channel_id=1, source_target_pairs={{0,1},{1,0},{2,3},{3,2},{4,5},{5,4},{6,7},{7,6},{8,9},{9,8},{10,11... | collective-permute-start | bytes 393224 | tf_op jit(solution)/shard_map/ppermute | solution.py:524
  51.2 4.7 %collective-permute-start.19 = (bf16[256,256]{1,0:T(8,128)(2,1)S(1)}, bf16[256,256]{1,0:T(8,128)(2,1)S(1)}, u32[]{:S(2)}, u32[]{:S(2)}) collective-permute-start(bf16[256,256]{1,0:T(8,128)(2,1)S(1)} %collective-permute-done.15.refs_8_), channel_id=1, source_target_pairs={{0,1},{1,0},{2,3},{3,2},{4,5},{5,4},{6,7},{7,6},{8,9},{9,8},{10,11... | collective-permute-start | bytes 393224 | tf_op jit(solution)/shard_map/ppermute | solution.py:524
  51.2 4.7 %collective-permute-start.20 = (bf16[256,256]{1,0:T(8,128)(2,1)S(1)}, bf16[256,256]{1,0:T(8,128)(2,1)S(1)}, u32[]{:S(2)}, u32[]{:S(2)}) collective-permute-start(bf16[256,256]{1,0:T(8,128)(2,1)S(1)} %collective-permute-done.16.refs_9_), channel_id=1, source_target_pairs={{0,1},{1,0},{2,3},{3,2},{4,5},{5,4},{6,7},{7,6},{8,9},{9,8},{10,11... | collective-permute-start | bytes 393224 | tf_op jit(solution)/shard_map/ppermute | solution.py:524
  53.8 51.7 %copy-start.14 = (f32[2048]{0:T(1024)S(1)}, f32[2048]{0:T(1024)}, u32[]{:S(2)}) copy-start(f32[2048]{0:T(1024)} %param.25) | copy-start | bytes 24580
  55.9 1.2 copy-start.6
  59.6 80.7 %slice-start.2 = ((s8[12845056]{0:T(1024)(128)(4,1)}), s8[4194304]{0:T(1024)(128)(4,1)S(1)}, s32[]{:S(2)}) async-start(s8[12845056]{0:T(1024)(128)(4,1)} %bitcast.15), calls=%async_computation.2 | async-start | bytes 8388608
  64.5 14.0 %collective-permute-start.21 = (bf16[528,256]{1,0:T(8,128)(2,1)S(1)}, bf16[528,256]{1,0:T(8,128)(2,1)S(1)}, u32[]{:S(2)}, u32[]{:S(2)}) collective-permute-start(bf16[528,256]{1,0:T(8,128)(2,1)S(1)} %get-tuple-element.49), channel_id=1, source_target_pairs={{0,8},{8,0},{16,24},{24,16},{1,9},{9,1},{17,25},{25,17},{2,10},{10... | collective-permute-start | bytes 811016 | tf_op jit(solution)/shard_map/ppermute | solution.py:527
  64.5 21.9 %collective-permute-start.22 = (bf16[528,256]{1,0:T(8,128)(2,1)S(1)}, bf16[528,256]{1,0:T(8,128)(2,1)S(1)}, u32[]{:S(2)}, u32[]{:S(2)}) collective-permute-start(bf16[528,256]{1,0:T(8,128)(2,1)S(1)} %get-tuple-element.50), channel_id=1, source_target_pairs={{0,16},{8,24},{16,0},{24,8},{1,17},{9,25},{17,1},{25,9},{2,18},{10... | collective-permute-start | bytes 811016 | tf_op jit(solution)/shard_map/ppermute | solution.py:527
  66.8 19.7 %collective-permute-start.23 = (bf16[528,256]{1,0:T(8,128)(2,1)S(1)}, bf16[528,256]{1,0:T(8,128)(2,1)S(1)}, u32[]{:S(2)}, u32[]{:S(2)}) collective-permute-start(bf16[528,256]{1,0:T(8,128)(2,1)S(1)} %get-tuple-element.51), channel_id=1, source_target_pairs={{0,24},{8,16},{16,8},{24,0},{1,25},{9,17},{17,9},{25,1},{2,26},{10... | collective-permute-start | bytes 811016 | tf_op jit(solution)/shard_map/ppermute | solution.py:527
  86.5 53.8 %slice-start.3 = ((s8[12845056]{0:T(1024)(128)(4,1)}), s8[262144]{0:T(1024)(128)(4,1)S(1)}, s32[]{:S(2)}) async-start(s8[12845056]{0:T(1024)(128)(4,1)} %bitcast.15), calls=%async_computation.3 | async-start | bytes 524288
  90.9 1.3 collective-permute-start.31
  92.6 8.1 %collective-permute-start.32 = (bf16[32,2048]{1,0:T(8,128)(2,1)S(1)}, bf16[32,2048]{1,0:T(8,128)(2,1)S(1)}, u32[]{:S(2)}, u32[]{:S(2)}) collective-permute-start(bf16[32,2048]{1,0:T(8,128)(2,1)S(1)} %get-tuple-element.65), channel_id=1, source_target_pairs={{0,2},{1,3},{2,0},{3,1},{4,6},{5,7},{6,4},{7,5},{8,10},{9,11},{10,... | collective-permute-start | bytes 393224 | tf_op jit(solution)/shard_map/ppermute | solution.py:524
  92.8 15.7 %collective-permute-start.24 = (bf16[272,256]{1,0:T(8,128)(2,1)S(1)}, bf16[272,256]{1,0:T(8,128)(2,1)S(1)}, u32[]{:S(2)}, u32[]{:S(2)}) collective-permute-start(bf16[272,256]{1,0:T(8,128)(2,1)S(1)} %get-tuple-element.52), channel_id=1, source_target_pairs={{0,8},{8,0},{16,24},{24,16},{1,9},{9,1},{17,25},{25,17},{2,10},{10... | collective-permute-start | bytes 417800 | tf_op jit(solution)/shard_map/ppermute | solution.py:527
  97.6 7.8 %collective-permute-start.33 = (bf16[32,2048]{1,0:T(8,128)(2,1)S(1)}, bf16[32,2048]{1,0:T(8,128)(2,1)S(1)}, u32[]{:S(2)}, u32[]{:S(2)}) collective-permute-start(bf16[32,2048]{1,0:T(8,128)(2,1)S(1)} %get-tuple-element.66), channel_id=1, source_target_pairs={{0,4},{1,5},{2,6},{3,7},{4,0},{5,1},{6,2},{7,3},{8,12},{9,13},{10,... | collective-permute-start | bytes 393224 | tf_op jit(solution)/shard_map/ppermute | solution.py:524
  98.5 6.9 %collective-permute-start.34 = (bf16[32,2048]{1,0:T(8,128)(2,1)S(1)}, bf16[32,2048]{1,0:T(8,128)(2,1)S(1)}, u32[]{:S(2)}, u32[]{:S(2)}) collective-permute-start(bf16[32,2048]{1,0:T(8,128)(2,1)S(1)} %get-tuple-element.67), channel_id=1, source_target_pairs={{0,6},{1,7},{2,4},{3,5},{4,2},{5,3},{6,0},{7,1},{8,14},{9,15},{10,... | collective-permute-start | bytes 393224 | tf_op jit(solution)/shard_map/ppermute | solution.py:524
  100.7 17.0 %collective-permute-start.25 = (bf16[272,256]{1,0:T(8,128)(2,1)S(1)}, bf16[272,256]{1,0:T(8,128)(2,1)S(1)}, u32[]{:S(2)}, u32[]{:S(2)}) collective-permute-start(bf16[272,256]{1,0:T(8,128)(2,1)S(1)} %get-tuple-element.53), channel_id=1, source_target_pairs={{0,16},{8,24},{16,0},{24,8},{1,17},{9,25},{17,1},{25,9},{2,18},{10... | collective-permute-start | bytes 417800 | tf_op jit(solution)/shard_map/ppermute | solution.py:527
  100.7 16.9 %collective-permute-start.26 = (bf16[272,256]{1,0:T(8,128)(2,1)S(1)}, bf16[272,256]{1,0:T(8,128)(2,1)S(1)}, u32[]{:S(2)}, u32[]{:S(2)}) collective-permute-start(bf16[272,256]{1,0:T(8,128)(2,1)S(1)} %get-tuple-element.54), channel_id=1, source_target_pairs={{0,24},{8,16},{16,8},{24,0},{1,25},{9,17},{17,9},{25,1},{2,26},{10... | collective-permute-start | bytes 417800 | tf_op jit(solution)/shard_map/ppermute | solution.py:527
  106.4 11.3 %collective-permute-start.35 = (bf16[32,2048]{1,0:T(8,128)(2,1)S(1)}, bf16[32,2048]{1,0:T(8,128)(2,1)S(1)}, u32[]{:S(2)}, u32[]{:S(2)}) collective-permute-start(bf16[32,2048]{1,0:T(8,128)(2,1)S(1)} %get-tuple-element.70.refs_0_), channel_id=1, source_target_pairs={{0,8},{8,0},{16,24},{24,16},{1,9},{9,1},{17,25},{25,17},{2,10},{10... | collective-permute-start | bytes 393224 | tf_op jit(solution)/shard_map/ppermute | solution.py:527
  107.0 16.4 %collective-permute-start.36 = (bf16[32,2048]{1,0:T(8,128)(2,1)S(1)}, bf16[32,2048]{1,0:T(8,128)(2,1)S(1)}, u32[]{:S(2)}, u32[]{:S(2)}) collective-permute-start(bf16[32,2048]{1,0:T(8,128)(2,1)S(1)} %get-tuple-element.70.refs_0_), channel_id=1, source_target_pairs={{0,16},{8,24},{16,0},{24,8},{1,17},{9,25},{17,1},{25,9},{2,18},{10... | collective-permute-start | bytes 393224 | tf_op jit(solution)/shard_map/ppermute | solution.py:527
  108.5 15.0 %collective-permute-start.37 = (bf16[32,2048]{1,0:T(8,128)(2,1)S(1)}, bf16[32,2048]{1,0:T(8,128)(2,1)S(1)}, u32[]{:S(2)}, u32[]{:S(2)}) collective-permute-start(bf16[32,2048]{1,0:T(8,128)(2,1)S(1)} %get-tuple-element.70.refs_0_), channel_id=1, source_target_pairs={{0,24},{8,16},{16,8},{24,0},{1,25},{9,17},{17,9},{25,1},{2,26},{10... | collective-permute-start | bytes 393224 | tf_op jit(solution)/shard_map/ppermute | solution.py:527
  123.5 13.8 %collective-permute-start.39 = (bf16[128,2048]{1,0:T(8,128)(2,1)S(1)}, bf16[128,2048]{1,0:T(8,128)(2,1)S(1)}, u32[]{:S(2)}, u32[]{:S(2)}) collective-permute-start(bf16[128,2048]{1,0:T(8,128)(2,1)S(1)} %stack.10.refs_1_), channel_id=1, source_target_pairs={{0,2},{1,3},{2,0},{3,1},{4,6},{5,7},{6,4},{7,5},{8,10},{9,11},{10,... | collective-permute-start | bytes 1572872 | tf_op jit(solution)/shard_map/ppermute | solution.py:524
  124.7 12.7 %collective-permute-start.41 = (bf16[128,2048]{1,0:T(8,128)(2,1)S(1)}, bf16[128,2048]{1,0:T(8,128)(2,1)S(1)}, u32[]{:S(2)}, u32[]{:S(2)}) collective-permute-start(bf16[128,2048]{1,0:T(8,128)(2,1)S(1)} %stack.10.refs_1_), channel_id=1, source_target_pairs={{0,4},{1,5},{2,6},{3,7},{4,0},{5,1},{6,2},{7,3},{8,12},{9,13},{10,... | collective-permute-start | bytes 1572872 | tf_op jit(solution)/shard_map/ppermute | solution.py:524
  125.2 15.1 %collective-permute-start.38 = (bf16[128,2048]{1,0:T(8,128)(2,1)S(1)}, bf16[128,2048]{1,0:T(8,128)(2,1)S(1)}, u32[]{:S(2)}, u32[]{:S(2)}) collective-permute-start(bf16[128,2048]{1,0:T(8,128)(2,1)S(1)} %stack.10.refs_1_), channel_id=1, source_target_pairs={{0,1},{1,0},{2,3},{3,2},{4,5},{5,4},{6,7},{7,6},{8,9},{9,8},{10,11... | collective-permute-start | bytes 1572872 | tf_op jit(solution)/shard_map/ppermute | solution.py:524
  137.3 9.0 %collective-permute-start.40 = (bf16[128,2048]{1,0:T(8,128)(2,1)S(1)}, bf16[128,2048]{1,0:T(8,128)(2,1)S(1)}, u32[]{:S(2)}, u32[]{:S(2)}) collective-permute-start(bf16[128,2048]{1,0:T(8,128)(2,1)S(1)} %collective-permute-done.39.refs_1_), channel_id=1, source_target_pairs={{0,1},{1,0},{2,3},{3,2},{4,5},{5,4},{6,7},{7,6},{8,9},{9,8},{10,11... | collective-permute-start | bytes 1572872 | tf_op jit(solution)/shard_map/ppermute | solution.py:524
  137.4 8.7 %collective-permute-start.43 = (bf16[64,2048]{1,0:T(8,128)(2,1)S(1)}, bf16[64,2048]{1,0:T(8,128)(2,1)S(1)}, u32[]{:S(2)}, u32[]{:S(2)}) collective-permute-start(bf16[64,2048]{1,0:T(8,128)(2,1)S(1)} %slice.42), channel_id=1, source_target_pairs={{0,2},{1,3},{2,0},{3,1},{4,6},{5,7},{6,4},{7,5},{8,10},{9,11},{10,... | collective-permute-start | bytes 786440 | tf_op jit(solution)/shard_map/ppermute | solution.py:524
  139.2 7.1 %collective-permute-start.44 = (bf16[64,2048]{1,0:T(8,128)(2,1)S(1)}, bf16[64,2048]{1,0:T(8,128)(2,1)S(1)}, u32[]{:S(2)}, u32[]{:S(2)}) collective-permute-start(bf16[64,2048]{1,0:T(8,128)(2,1)S(1)} %slice.43), channel_id=1, source_target_pairs={{0,4},{1,5},{2,6},{3,7},{4,0},{5,1},{6,2},{7,3},{8,12},{9,13},{10,... | collective-permute-start | bytes 786440 | tf_op jit(solution)/shard_map/ppermute | solution.py:524
  140.2 11.0 %collective-permute-start.42 = (bf16[128,2048]{1,0:T(8,128)(2,1)S(1)}, bf16[128,2048]{1,0:T(8,128)(2,1)S(1)}, u32[]{:S(2)}, u32[]{:S(2)}) collective-permute-start(bf16[128,2048]{1,0:T(8,128)(2,1)S(1)} %collective-permute-done.41.refs_1_), channel_id=1, source_target_pairs={{0,1},{1,0},{2,3},{3,2},{4,5},{5,4},{6,7},{7,6},{8,9},{9,8},{10,11... | collective-permute-start | bytes 1572872 | tf_op jit(solution)/shard_map/ppermute | solution.py:524
  146.3 9.9 %collective-permute-start.45 = (bf16[128,2048]{1,0:T(8,128)(2,1)S(1)}, bf16[128,2048]{1,0:T(8,128)(2,1)S(1)}, u32[]{:S(2)}, u32[]{:S(2)}) collective-permute-start(bf16[128,2048]{1,0:T(8,128)(2,1)S(1)} %stack.11.refs_1_), channel_id=1, source_target_pairs={{0,1},{1,0},{2,3},{3,2},{4,5},{5,4},{6,7},{7,6},{8,9},{9,8},{10,11... | collective-permute-start | bytes 1572872 | tf_op jit(solution)/shard_map/ppermute | solution.py:524
  161.6 1.3 collective-permute-start.46
  163.0 3.7 %collective-permute-start.47 = (f32[8,256]{1,0:T(8,128)S(1)}, f32[8,256]{1,0:T(8,128)S(1)}, u32[]{:S(2)}, u32[]{:S(2)}) collective-permute-start(f32[8,256]{1,0:T(8,128)S(1)} %add_select_fusion.4), channel_id=1, source_target_pairs={{0,2},{1,3},{2,0},{3,1},{4,6},{5,7},{6,4},{7,5},{8,10},{9,11},{10,... | collective-permute-start | bytes 24584 | tf_op jit(solution)/shard_map/ppermute | solution.py:601
  166.7 3.7 %collective-permute-start.48 = (f32[8,256]{1,0:T(8,128)S(1)}, f32[8,256]{1,0:T(8,128)S(1)}, u32[]{:S(2)}, u32[]{:S(2)}) collective-permute-start(f32[8,256]{1,0:T(8,128)S(1)} %add_select_fusion.3), channel_id=1, source_target_pairs={{0,4},{1,5},{2,6},{3,7},{4,0},{5,1},{6,2},{7,3},{8,12},{9,13},{10,... | collective-permute-start | bytes 24584 | tf_op jit(solution)/shard_map/ppermute | solution.py:601
  169.0 4.8 %collective-permute-start.27 = (bf16[128,256]{1,0:T(8,128)(2,1)S(1)}, bf16[128,256]{1,0:T(8,128)(2,1)S(1)}, u32[]{:S(2)}, u32[]{:S(2)}) collective-permute-start(bf16[128,256]{1,0:T(8,128)(2,1)S(1)} %get-tuple-element.56), channel_id=1, source_target_pairs={{0,1},{1,0},{2,3},{3,2},{4,5},{5,4},{6,7},{7,6},{8,9},{9,8},{10,11... | collective-permute-start | bytes 196616 | tf_op jit(solution)/shard_map/ppermute | solution.py:524
  170.4 7.4 %collective-permute-start.49 = (f32[8,256]{1,0:T(8,128)S(1)}, f32[8,256]{1,0:T(8,128)S(1)}, u32[]{:S(2)}, u32[]{:S(2)}) collective-permute-start(f32[8,256]{1,0:T(8,128)S(1)} %add_select_fusion.2), channel_id=1, source_target_pairs={{0,8},{8,0},{16,24},{24,16},{1,9},{9,1},{17,25},{25,17},{2,10},{10... | collective-permute-start | bytes 24584 | tf_op jit(solution)/shard_map/ppermute | solution.py:601
  174.3 6.2 %collective-permute-start.28 = (bf16[32,2048]{1,0:T(8,128)(2,1)S(1)}, bf16[32,2048]{1,0:T(8,128)(2,1)S(1)}, u32[]{:S(2)}, u32[]{:S(2)}) collective-permute-start(bf16[32,2048]{1,0:T(8,128)(2,1)S(1)} %get-tuple-element.58), channel_id=1, source_target_pairs={{0,2},{1,3},{2,0},{3,1},{4,6},{5,7},{6,4},{7,5},{8,10},{9,11},{10,... | collective-permute-start | bytes 393224 | tf_op jit(solution)/shard_map/ppermute | solution.py:524
  176.1 7.3 %collective-permute-start.29 = (bf16[32,2048]{1,0:T(8,128)(2,1)S(1)}, bf16[32,2048]{1,0:T(8,128)(2,1)S(1)}, u32[]{:S(2)}, u32[]{:S(2)}) collective-permute-start(bf16[32,2048]{1,0:T(8,128)(2,1)S(1)} %get-tuple-element.59), channel_id=1, source_target_pairs={{0,4},{1,5},{2,6},{3,7},{4,0},{5,1},{6,2},{7,3},{8,12},{9,13},{10,... | collective-permute-start | bytes 393224 | tf_op jit(solution)/shard_map/ppermute | solution.py:524
  177.1 6.3 %collective-permute-start.30 = (bf16[32,2048]{1,0:T(8,128)(2,1)S(1)}, bf16[32,2048]{1,0:T(8,128)(2,1)S(1)}, u32[]{:S(2)}, u32[]{:S(2)}) collective-permute-start(bf16[32,2048]{1,0:T(8,128)(2,1)S(1)} %get-tuple-element.60), channel_id=1, source_target_pairs={{0,6},{1,7},{2,4},{3,5},{4,2},{5,3},{6,0},{7,1},{8,14},{9,15},{10,... | collective-permute-start | bytes 393224 | tf_op jit(solution)/shard_map/ppermute | solution.py:524
  177.9 6.4 %collective-permute-start.50 = (f32[8,256]{1,0:T(8,128)S(1)}, f32[8,256]{1,0:T(8,128)S(1)}, u32[]{:S(2)}, u32[]{:S(2)}) collective-permute-start(f32[8,256]{1,0:T(8,128)S(1)} %add_select_fusion.1), channel_id=1, source_target_pairs={{0,16},{8,24},{16,0},{24,8},{1,17},{9,25},{17,1},{25,9},{2,18},{10... | collective-permute-start | bytes 24584 | tf_op jit(solution)/shard_map/ppermute | solution.py:601
  (7 other events, 7.0 us)

commit v3 on v2

--- a/solution.py
+++ b/solution.py
@@ -46,6 +46,29 @@
     for copy in copies:
         copy.start()
     return copies
+
+
+def carry_kernel(*refs):
+    count = len(refs) // 2
+    for source, out in zip(refs[:count], refs[count:], strict=True):
+        out[...] = source[...]
+
+
+def carry(*arrays):
+    return pl.pallas_call(
+        carry_kernel,
+        out_shape=tuple(jax.ShapeDtypeStruct(a.shape, a.dtype) for a in arrays),
+        in_specs=[VMEM] * len(arrays),
+        out_specs=(VMEM,) * len(arrays),
+        compiler_params=params(),
+        name="carry",
+    )(*arrays)
+
+
+def first_kernel(place, *refs):
+    project_kernel(place, *refs[:-5], refs[-1])
+    for source, out in zip((refs[0], *refs[-12:-9]), refs[-5:-1], strict=True):
+        out[...] = source[...]
 
 
 def project_kernel(place, *refs):
@@ -70,12 +93,12 @@
     share = rows // (full // width)
     tile = jax.ShapeDtypeStruct((rows, width), BF16)
     return call(
-        project_kernel,
+        first_kernel,
         (place, *pieces, wq, wk, wv),
         after,
-        out_shape=(tile, tile, tile, jax.ShapeDtypeStruct((share, full), BF16)),
+        out_shape=(tile, tile, tile, jax.ShapeDtypeStruct((share, full), BF16), tile) + (jax.ShapeDtypeStruct(wq.shape, BF16),) * 3,
         in_specs=[SMEM] + [VMEM] * (len(pieces) + 3),
-        out_specs=(VMEM,) * 4,
+        out_specs=(VMEM,) * 8,
         scratch_shapes=[pltpu.VMEM((rows, full), BF16)],
         compiler_params=params(),
         cost_estimate=cost(6 * rows * full * width, 8 * full * width),
@@ -192,11 +215,8 @@
     queries, (keys, values), refs = refs[:count], refs[count : count + 2], refs[count + 2 :]
     messages, x = refs[-5 - count : -5], refs[-1]
     project_kernel(place, *refs[: -5 - count], *refs[-5:-1], x)
-    new_query = refs[-5]
-    rows = new_query.shape[0]
     for mask, query, message in zip(masks, queries, messages, strict=True):
         away_part(place, mask, query, keys, values, message, tok_count)
-        message[rows + 16 :, :] = new_query[...]
 
 
 def second_stage(tok_count, masks, place, queries, keys, values, pieces, wq, wk, wv, after=()):
@@ -204,7 +224,7 @@
     full = wq.shape[0]
     share = rows // (full // width)
     tile = jax.ShapeDtypeStruct((rows, width), BF16)
-    message = jax.ShapeDtypeStruct((2 * rows + 16, width), BF16)
+    message = jax.ShapeDtypeStruct((rows + 16, width), BF16)
     outs = (message,) * len(masks) + (tile, tile, tile, jax.ShapeDtypeStruct((share, full), BF16))
     results = call(
         functools.partial(second_kernel, tok_count, masks),
@@ -221,38 +241,27 @@
     return results[: len(masks)], results[len(masks) :]
 
 
-def third_kernel(share, tok_count, masks, place, mixed, logs, *refs):
+def away_kernel(tok_count, masks, place, *refs):
     count = len(masks)
-    messages, (keys, values), (keep, send), outs, whole = (
-        refs[:count],
-        refs[count : count + 2],
-        refs[count + 2 : count + 4],
-        refs[count + 4 : -1],
-        refs[-1],
-    )
-    combine_kernel(share, place, mixed, logs, *messages, keep, send, whole)
-    rows = mixed.shape[0]
-    for mask, message, out in zip(masks, messages, outs, strict=True):
-        away_part(place, mask, message.at[pl.ds(rows + 16, rows), :], keys, values, out, tok_count)
-
-
-def third_stage(share, tok_count, masks, place, mixed, logs, messages, keys, values, after=()):
-    rows, width = mixed.shape
-    half = jax.ShapeDtypeStruct((rows // 2, width), BF16)
-    message = jax.ShapeDtypeStruct((rows + 16, width), BF16)
-    results = call(
-        functools.partial(third_kernel, share, tok_count, masks),
-        (place, mixed, logs, *messages, keys, values),
-        after,
-        out_shape=(half, half) + (message,) * len(masks),
-        in_specs=[SMEM] + [VMEM] * (4 + len(masks)),
-        out_specs=(VMEM,) * (2 + len(masks)),
-        scratch_shapes=[pltpu.VMEM((rows, width), BF16)],
+    queries, (keys, values), outs = refs[:count], refs[count : count + 2], refs[count + 2 :]
+    for mask, query, out in zip(masks, queries, outs, strict=True):
+        away_part(place, mask, query, keys, values, out, tok_count)
+
+
+def away_parts(tok_count, masks, place, queries, keys, values, after=()):
+    rows, width = queries[0].shape
+    out = jax.ShapeDtypeStruct((rows + 16, width), BF16)
+    return call(
+        functools.partial(away_kernel, tok_count, masks),
+        (place, *queries, keys, values),
+        after,
+        out_shape=(out,) * len(masks),
+        in_specs=[SMEM] + [VMEM] * (len(masks) + 2),
+        out_specs=(VMEM,) * len(masks),
         compiler_params=params(),
         cost_estimate=cost(4 * rows * width * keys.shape[0], 4 * keys.shape[0] * width),
-        name="third_stage",
-    )
-    return results[:2], results[2:]
+        name="away_parts",
+    )
 
 
 def combine_kernel(share, place, mixed, logs, *refs):
@@ -300,31 +309,34 @@
     )
 
 
-def ids_kernel(vocab_here, place, ids, local_out, owner_out):
-    for slot in range(ids.shape[0]):
-        row = ids[pl.ds(jnp.bitwise_xor(place[0], slot), 1), :]
-        local_out[slot : slot + 1, :] = jnp.clip(row - place[0] * vocab_here, 0, vocab_here - 1)
-        if slot == 0:
-            owner = jnp.zeros(row.shape, jnp.int32)
-            for i in range(1, ids.shape[0]):
-                owner += jnp.where(row >= i * vocab_here, 1, 0)
-            owner_out[...] = owner
-
-
-def sort_ids(vocab_here, place, ids, after=()):
-    return call(
-        functools.partial(ids_kernel, vocab_here),
-        (place, ids),
-        after,
+def ids_kernel(tok_count, vocab_here, place, ids, local_out, owner_out):
+    tiles = ids.shape[0] // tok_count
+    for slot in range(tok_count):
+        for tile in range(tiles):
+            row = ids[pl.ds(jnp.bitwise_xor(place[0], slot) * tiles + tile, 1), :]
+            at = slot * tiles + tile
+            local_out[at : at + 1, :] = jnp.clip(row - place[0] * vocab_here, 0, vocab_here - 1)
+            if slot == 0:
+                owner = jnp.zeros(row.shape, jnp.int32)
+                for i in range(1, tok_count):
+                    owner += jnp.where(row >= i * vocab_here, 1, 0)
+                owner_out[:, tile * 128 : (tile + 1) * 128] = owner
+
+
+def sort_ids(tok_count, vocab_here, place, ids):
+    ids = ids.reshape(-1, 128)
+    local, owner = pl.pallas_call(
+        functools.partial(ids_kernel, tok_count, vocab_here),
         out_shape=(
             jax.ShapeDtypeStruct(ids.shape, jnp.int32),
-            jax.ShapeDtypeStruct((1, ids.shape[1]), jnp.int32),
+            jax.ShapeDtypeStruct((1, ids.size // tok_count), jnp.int32),
         ),
         in_specs=[SMEM, VMEM],
         out_specs=(VMEM, VMEM),
         compiler_params=params(),
         name="sort_ids",
-    )
+    )(place, ids)
+    return local.reshape(-1), owner
 
 
 def choose_kernel(place, accept, owner, states, *refs):
@@ -432,6 +444,29 @@
         compiler_params=params(),
         cost_estimate=cost(residual.size * 20, residual.size * 12),
         name="finish",
+    )
+
+
+def hand_on_kernel(first, second, *outs):
+    half = first.shape[0] // 2
+    outs[0][...] = first[...]
+    outs[1][...] = second[...]
+    outs[2][...] = second[:half, :]
+    outs[3][...] = first[half:, :]
+
+
+def hand_on(first, second, after=()):
+    whole = jax.ShapeDtypeStruct(first.shape, BF16)
+    half = jax.ShapeDtypeStruct((first.shape[0] // 2, first.shape[1]), BF16)
+    return call(
+        hand_on_kernel,
+        (first, second),
+        after,
+        out_shape=(whole, whole, half, half),
+        in_specs=[VMEM] * 2,
+        out_specs=(VMEM,) * 4,
+        compiler_params=params(),
+        name="hand_on",
     )
 
 
@@ -533,9 +568,6 @@
     def exchange(arrays):
         return [by_tok(array, mask) for mask, array in zip(tok_masks, arrays, strict=True)]
 
-    def own_of(query, key, value, after=()):
-        return own_part(tok_count, place, query, key, value, cache_keys, cache_values, after)
-
     def join(own, messages, after=()):
         return combine(share, place, *own, messages, after)
 
@@ -551,46 +583,49 @@
     w_out_other = by_head(w_out, 1)
 
     vocab_here = embed.shape[0]
-    ids, owners = sort_ids(vocab_here, place, token_ids.reshape(tok_count, block_rows))
-    found = embed.at[ids.reshape(-1)].get(mode="promise_in_bounds").reshape(tok_count, block_rows, -1)
+    ids, owners = sort_ids(tok_count, vocab_here, place, token_ids)
+    found = embed.at[ids].get(mode="promise_in_bounds").reshape(tok_count, block_rows, -1)
     found = [found[mask] for mask in range(tok_count)]
     embedded = [found[0], *exchange(found[1:])]
 
     pieces, others = spread(block_states)
-    query, key, value, residual = project(
+    query, key, value, residual, states, *weights = project(
         block_rows, place, pieces + others, w_query, w_key, w_value, [w_out_other, found[1]]
     )
     queries = exchange([query] * len(tok_masks))
-    own = own_of(query, key, value)
-    chosen = choose(place, accept.reshape(1, -1), owners, block_states, embedded, queries[:1])
+    cache_keys, cache_values = carry(cache_keys, cache_values)
+    own = own_part(tok_count, place, query, key, value, cache_keys, cache_values)
+    chosen = choose(place, accept.reshape(1, -1), owners, states, embedded, queries[:1])
     pieces, others = spread(chosen)
     messages, (query, key, value, residual_two) = second_stage(
-        tok_count, tok_masks, place, queries, cache_keys, cache_values, pieces + others, w_query, w_key, w_value, [own[0]]
+        tok_count, tok_masks, place, queries, cache_keys, cache_values, pieces + others, *weights
     )
     messages = exchange(messages)
-    own_two = own_of(query, key, value)
-    keep, messages = third_stage(
-        share, tok_count, tok_masks, place, *own, messages, cache_keys, cache_values, [own_two[0]]
-    )
-    messages = exchange(messages)
-    _, normed, square = finish_layer(False, out_layer(*keep), residual)
-
-    column = stack([normed] + exchange([normed] * len(tok_masks)), messages)
+    queries = exchange([query] * len(tok_masks))
+    own_two = own_part(tok_count, place, query, key, value, cache_keys, cache_values)
+    keep = join(own, messages, [own_two[0]])
+    parts = away_parts(tok_count, tok_masks, place, queries, cache_keys, cache_values, [keep[0]])
+    _, normed, square = finish_layer(False, out_layer(*keep), residual, parts[:1])
+
+    column = stack([normed] + exchange([normed] * len(tok_masks)))
+    parts = exchange(parts)
 
     def best_of(piece, after=()):
         return largest_logits(share, tok_count, place, piece, by_head(piece, 1), lm_head, after)
 
+    bests = [best_of(column)]
     if chips == 4:
-        along_x, along_y = by_head(column, 2), by_head(column, 4)
-        half = column.shape[0] // 2
-        across = stack([by_head(along_y[:half], 2), by_head(along_x[half:], 4)])
-        columns = [column, along_x, along_y, across]
+        along_x, along_y, along_y_half, along_x_half = hand_on(
+            by_head(column, 2), by_head(column, 4), [bests[0], *parts]
+        )
+        bests.append(best_of(along_x))
+        bests.append(best_of(along_y, bests[1:]))
+        across = stack([by_head(along_y_half, 2), by_head(along_x_half, 4)], bests[2:])
+        bests.append(best_of(across))
     else:
-        columns = [column] + [by_head(column, 2 * s) for s in range(1, chips)]
-    bests = []
-    for piece in columns:
-        bests.append(best_of(piece, bests[-1:]))
-    sums = out_layer(*join(own_two, messages))
+        for s in range(1, chips):
+            bests.append(best_of(by_head(column, 2 * s), bests[-1:]))
+    sums = out_layer(*join(own_two, parts))
     (hiddens,) = finish_layer(True, sums, residual_two)
 
     best = gather_best(place, square, bests)

time: 186 us -> 162 us (0.87)
  waiting for transfers between devices: 59.5 us -> 40.8 us
  local copies, waits for them, and re-layouts: 26.3 us -> 18.9 us
  starting transfers between devices: 56 us -> 58.4 us
    ppermute x31, waiting for transfers between devices: 25 us -> 7.28 us  [by_head(): return lax.ppermute(value, 'head', xor_pairs(head_count, mask))]
    ppermute x15 -> x18, starting transfers between devices: 27.5 us -> 32 us  [by_tok(): return lax.ppermute(value, 'tok', xor_pairs(tok_count, mask))]
    unnamed x41 -> x30, local copies, waits for them, and re-layouts: 12.3 us -> 8.26 us
    ppermute x15 -> x18, waiting for transfers between devices: 30.5 us -> 27.2 us  [by_tok(): return lax.ppermute(value, 'tok', xor_pairs(tok_count, mask))]
    ppermute x5, starting transfers between devices: 6.85 us -> 3.88 us  [shards(): other = lax.ppermute(best, axis, xor_pairs(size, mask))]
    ppermute x5, waiting for transfers between devices: 4.03 us -> 6.31 us  [shards(): other = lax.ppermute(best, axis, xor_pairs(size, mask))]
    pallas_call x16 -> x17, Pallas kernels: 39 us -> 38.7 us  [call(): return pl.pallas_call(body, in_specs=specs, **rest)(*operands, *after)]
  transfers between devices with their start and end apart: 51 -> 54, of which waited for: 17 -> 14; matrix products, arithmetic and copies ran while one was open for 8% -> 7% of each run, Pallas kernels for 14% -> 18%
where the time goes in v3:
time: 162 us
  starting transfers between devices  58.4 us (36%)
  Pallas kernels  40.9 us (25%)
  waiting for transfers between devices  40.8 us (25%)
  local copies, waits for them, and re-layouts  18.9 us (12%)
  other arithmetic  1.63 us (1%)
    pallas_call x17, Pallas kernels, call(): return pl.pallas_call(body, in_specs=specs, **rest)(*operands, *after)  38.7 us
    ppermute x18, starting transfers between devices, by_tok(): return lax.ppermute(value, 'tok', xor_pairs(tok_count, mask))  32 us
    ppermute x18, waiting for transfers between devices, by_tok(): return lax.ppermute(value, 'tok', xor_pairs(tok_count, mask))  27.2 us
    ppermute x31, starting transfers between devices, by_head(): return lax.ppermute(value, 'head', xor_pairs(head_count, mask))  22.5 us
    gather x1, local copies, waits for them, and re-layouts, shards(): embed.at[ids].get(mode='promise_in_bounds')  9.81 us
    unnamed x30, local copies, waits for them, and re-layouts  8.26 us
    ppermute x31, waiting for transfers between devices, by_head(): return lax.ppermute(value, 'head', xor_pairs(head_count, mask))  7.28 us
    ppermute x5, waiting for transfers between devices, shards(): other = lax.ppermute(best, axis, xor_pairs(size, mask))  6.31 us
  transfers between devices with their start and end apart: 54, of which 14 were waited for; matrix products, arithmetic and copies ran while one was open for 7% of the time, Pallas kernels for 18%

profile of v3, /device:TPU:0, one launch (start us, length us, event | category | flops | bytes accessed | tf_op | source)
XLA Modules:
  0.0 161.7 jit_solution(12567062723313479259)
XLA Ops:
  1.2 2.6 %collective-permute-start = (bf16[256,256]{1,0:T(8,128)(2,1)}, bf16[256,256]{1,0:T(8,128)(2,1)S(1)}, u32[]{:S(2)}, u32[]{:S(2)}) collective-permute-start(bf16[256,256]{1,0:T(8,128)(2,1)} %refs_1_.2), channel_id=1, source_target_pairs={{0,2},{1,3},{2,0},{3,1},{4,6},{5,7},{6,4},{7,5},{8,10},{9,11},{10,... | collective-permute-start | bytes 393224 | tf_op jit(solution)/shard_map/ppermute | solution.py:559
  3.7 1.5 collective-permute-start.1
  5.3 0.7 pad_add_fusion.place.refs_0_
  6.0 0.7 copy-done.9
  7.3 9.8 %gather_fusion = bf16[1024,256]{1,0:T(8,128)(2,1)S(1)} fusion(bf16[25088,256]{1,0:T(8,128)(2,1)} %param.26, s32[1024]{0:T(1024)S(1)} %broadcast_clamp_fusion), kind=kCustom, calls=%fused_computation | custom fusion | bytes 1052672 | tf_op jit(solution)/shard_map/gather | solution.py:587
  18.3 2.1 %collective-permute-start.11 = (bf16[256,256]{1,0:T(8,128)(2,1)S(1)}, bf16[256,256]{1,0:T(8,128)(2,1)S(1)}, u32[]{:S(2)}, u32[]{:S(2)}) collective-permute-start(bf16[256,256]{1,0:T(8,128)(2,1)S(1)} %get-tuple-element.94.refs_13_), channel_id=1, source_target_pairs={{0,8},{8,0},{16,24},{24,16},{1,9},{9,1},{17,25},{25,17},{2,10},{10... | collective-permute-start | bytes 393224 | tf_op jit(solution)/shard_map/ppermute | solution.py:562
  20.4 2.6 %collective-permute-start.12 = (bf16[256,256]{1,0:T(8,128)(2,1)S(1)}, bf16[256,256]{1,0:T(8,128)(2,1)S(1)}, u32[]{:S(2)}, u32[]{:S(2)}) collective-permute-start(bf16[256,256]{1,0:T(8,128)(2,1)S(1)} %get-tuple-element.92), channel_id=1, source_target_pairs={{0,16},{8,24},{16,0},{24,8},{1,17},{9,25},{17,1},{25,9},{2,18},{10... | collective-permute-start | bytes 393224 | tf_op jit(solution)/shard_map/ppermute | solution.py:562
  23.1 1.4 copy-done.1
  24.5 1.3 copy-done.2
  25.8 1.2 copy-done.3
  27.0 0.9 copy-done.6
  27.9 1.8 %project.1 = (bf16[256,256]{1,0:T(8,128)(2,1)S(1)}, bf16[256,256]{1,0:T(8,128)(2,1)S(1)}, bf16[256,256]{1,0:T(8,128)(2,1)S(1)}, bf16[32,2048]{1,0:T(8,128)(2,1)S...) custom-call(s32[6]{0:T(128)S(1)} %pad_add_fusion.place.refs_0_, ...), custom_call_target="tpu_custom_call" | custom-call | flops 805306368 | bytes 4194304 | tf_op jit(solution)/shard_map/project/pallas_call | solution.py:37
  29.7 0.9 collective-permute-start.8
  30.6 2.8 %collective-permute-start.10 = (bf16[256,256]{1,0:T(8,128)(2,1)S(1)}, bf16[256,256]{1,0:T(8,128)(2,1)S(1)}, u32[]{:S(2)}, u32[]{:S(2)}) collective-permute-start(bf16[256,256]{1,0:T(8,128)(2,1)S(1)} %get-tuple-element.48.refs_1_), channel_id=1, source_target_pairs={{0,24},{8,16},{16,8},{24,0},{1,25},{9,17},{17,9},{25,1},{2,26},{10... | collective-permute-start | bytes 393224 | tf_op jit(solution)/shard_map/ppermute | solution.py:562
  33.3 3.2 %collective-permute-done.8.refs_8_.refs_1_ = bf16[256,256]{1,0:T(8,128)(2,1)S(1)} collective-permute-done((bf16[256,256]{1,0:T(8,128)(2,1)S(1)}, bf16[256,256]{1,0:T(8,128)(2,1)S(1)}, u32[]{:S(2)}, u32[]{:S(2)}) %collective-permute-start.8) | collective-permute-done | bytes 131104 | tf_op jit(solution)/shard_map/ppermute | solution.py:562
  36.5 0.7 copy-done.10
  37.2 0.7 choose.1.refs_6_
  37.9 1.6 collective-permute-start.14
  39.5 1.5 collective-permute-start.15
  41.5 3.8 %collective-permute-start.9 = (bf16[256,256]{1,0:T(8,128)(2,1)S(1)}, bf16[256,256]{1,0:T(8,128)(2,1)S(1)}, u32[]{:S(2)}, u32[]{:S(2)}) collective-permute-start(bf16[256,256]{1,0:T(8,128)(2,1)S(1)} %get-tuple-element.48.refs_1_), channel_id=1, source_target_pairs={{0,16},{8,24},{16,0},{24,8},{1,17},{9,25},{17,1},{25,9},{2,18},{10... | collective-permute-start | bytes 393224 | tf_op jit(solution)/shard_map/ppermute | solution.py:562
  45.9 1.3 collective-permute-done.15.refs_8_
  47.7 1.0 copy-done.4
  48.7 1.0 copy-done.5
  49.9 4.9 %second_stage.1 = (bf16[272,256]{1,0:T(8,128)(2,1)S(1)}, bf16[272,256]{1,0:T(8,128)(2,1)S(1)}, bf16[272,256]{1,0:T(8,128)(2,1)S(1)}, bf16[256,256]{1,0:T(8,128)(...) custom-call(s32[6]{0:T(128)S(1)} %pad_add_fusion.place.refs_0_, ...), custom_call_target="tpu_custom_call" | custom-call | flops 1073741824 | bytes 4194304 | tf_op jit(solution)/shard_map/second_stage/pallas_call | solution.py:37
  55.1 2.3 %collective-permute-start.25 = (bf16[272,256]{1,0:T(8,128)(2,1)S(1)}, bf16[272,256]{1,0:T(8,128)(2,1)S(1)}, u32[]{:S(2)}, u32[]{:S(2)}) collective-permute-start(bf16[272,256]{1,0:T(8,128)(2,1)S(1)} %get-tuple-element.66), channel_id=1, source_target_pairs={{0,16},{8,24},{16,0},{24,8},{1,17},{9,25},{17,1},{25,9},{2,18},{10... | collective-permute-start | bytes 417800 | tf_op jit(solution)/shard_map/ppermute | solution.py:562
  57.4 1.8 %collective-permute-start.26 = (bf16[272,256]{1,0:T(8,128)(2,1)S(1)}, bf16[272,256]{1,0:T(8,128)(2,1)S(1)}, u32[]{:S(2)}, u32[]{:S(2)}) collective-permute-start(bf16[272,256]{1,0:T(8,128)(2,1)S(1)} %get-tuple-element.67), channel_id=1, source_target_pairs={{0,24},{8,16},{16,8},{24,0},{1,25},{9,17},{17,9},{25,1},{2,26},{10... | collective-permute-start | bytes 417800 | tf_op jit(solution)/shard_map/ppermute | solution.py:562
  59.2 2.0 %own_part.3 = (f32[256,256]{1,0:T(8,128)S(1)}, f32[256,256]{1,0:T(8,128)S(1)}) custom-call(s32[6]{0:T(128)S(1)} %pad_add_fusion.place.refs_0_, bf16[256,256]{1,0:T(8,128)(2,1)S(1)} %get-tuple-element.48.refs_1_, bf16[256,256]{1,0:T(8,128)(2,1)S(1)} %get-tuple-element.61.refs_2_, bf16[256,256]{1,0:T(8,128)(2,1)S(1)} %get-tuple-element.62.refs_3_, ...), custom_call_target="tpu_custom_call" | custom-call | flops 268435456 | bytes 1048576 | tf_op jit(solution)/shard_map/own_part/pallas_call | solution.py:37
  61.2 2.2 %own_part.2 = (f32[256,256]{1,0:T(8,128)S(1)}, f32[256,256]{1,0:T(8,128)S(1)}) custom-call(s32[6]{0:T(128)S(1)} %pad_add_fusion.place.refs_0_, bf16[256,256]{1,0:T(8,128)(2,1)S(1)} %get-tuple-element.56.refs_1_, bf16[256,256]{1,0:T(8,128)(2,1)S(1)} %get-tuple-element.57.refs_2_, bf16[256,256]{1,0:T(8,128)(2,1)S(1)} %get-tuple-element.58.refs_3_, ...), custom_call_target="tpu_custom_call" | custom-call | flops 268435456 | bytes 1048576 | tf_op jit(solution)/shard_map/own_part/pallas_call | solution.py:37
  63.7 4.8 %collective-permute-done.25.refs_4_ = bf16[272,256]{1,0:T(8,128)(2,1)S(1)} collective-permute-done((bf16[272,256]{1,0:T(8,128)(2,1)S(1)}, bf16[272,256]{1,0:T(8,128)(2,1)S(1)}, u32[]{:S(2)}, u32[]{:S(2)}) %collective-permute-start.25) | collective-permute-done | bytes 139296 | tf_op jit(solution)/shard_map/ppermute | solution.py:562
  68.5 1.0 combine.2
  69.7 3.6 %collective-permute-start.22 = (bf16[256,256]{1,0:T(8,128)(2,1)S(1)}, bf16[256,256]{1,0:T(8,128)(2,1)S(1)}, u32[]{:S(2)}, u32[]{:S(2)}) collective-permute-start(bf16[256,256]{1,0:T(8,128)(2,1)S(1)} %get-tuple-element.56.refs_1_), channel_id=1, source_target_pairs={{0,16},{8,24},{16,0},{24,8},{1,17},{9,25},{17,1},{25,9},{2,18},{10... | collective-permute-start | bytes 393224 | tf_op jit(solution)/shard_map/ppermute | solution.py:562
  73.2 1.7 %collective-permute-start.23 = (bf16[256,256]{1,0:T(8,128)(2,1)S(1)}, bf16[256,256]{1,0:T(8,128)(2,1)S(1)}, u32[]{:S(2)}, u32[]{:S(2)}) collective-permute-start(bf16[256,256]{1,0:T(8,128)(2,1)S(1)} %get-tuple-element.56.refs_1_), channel_id=1, source_target_pairs={{0,24},{8,16},{16,8},{24,0},{1,25},{9,17},{17,9},{25,1},{2,26},{10... | collective-permute-start | bytes 393224 | tf_op jit(solution)/shard_map/ppermute | solution.py:562
  76.0 0.8 collective-permute-start.36
  76.8 2.2 %collective-permute-start.37 = (bf16[32,2048]{1,0:T(8,128)(2,1)S(1)}, bf16[32,2048]{1,0:T(8,128)(2,1)S(1)}, u32[]{:S(2)}, u32[]{:S(2)}) collective-permute-start(bf16[32,2048]{1,0:T(8,128)(2,1)S(1)} %get-tuple-element.83), channel_id=1, source_target_pairs={{0,6},{1,7},{2,4},{3,5},{4,2},{5,3},{6,0},{7,1},{8,14},{9,15},{10,... | collective-permute-start | bytes 393224 | tf_op jit(solution)/shard_map/ppermute | solution.py:559
  78.9 4.2 %collective-permute-done.22.refs_2_ = bf16[256,256]{1,0:T(8,128)(2,1)S(1)} collective-permute-done((bf16[256,256]{1,0:T(8,128)(2,1)S(1)}, bf16[256,256]{1,0:T(8,128)(2,1)S(1)}, u32[]{:S(2)}, u32[]{:S(2)}) %collective-permute-start.22) | collective-permute-done | bytes 131104 | tf_op jit(solution)/shard_map/ppermute | solution.py:562
  83.2 3.8 %away_parts.1 = (bf16[272,256]{1,0:T(8,128)(2,1)S(1)}, bf16[272,256]{1,0:T(8,128)(2,1)S(1)}, bf16[272,256]{1,0:T(8,128)(2,1)S(1)}) custom-call(s32[6]{0:T(128)S(1)} %pad_add_fusion.place.refs_0_, bf16[256,256]{1,0:T(8,128)(2,1)S(1)} %collective-permute-done.21.refs_1_, bf16[256,256]{1,0:T(8,128)(2,1)S(1)} %collective-permute-done.22.refs_2_, ...), custom_call_target="tpu_custom_call" | custom-call | flops 268435456 | bytes 1048576 | tf_op jit(solution)/shard_map/away_parts/pallas_call | solution.py:37
  87.0 0.9 finish.3
  87.9 2.3 %collective-permute-start.38 = (bf16[32,2048]{1,0:T(8,128)(2,1)S(1)}, bf16[32,2048]{1,0:T(8,128)(2,1)S(1)}, u32[]{:S(2)}, u32[]{:S(2)}) collective-permute-start(bf16[32,2048]{1,0:T(8,128)(2,1)S(1)} %get-tuple-element.86.refs_0_), channel_id=1, source_target_pairs={{0,8},{8,0},{16,24},{24,16},{1,9},{9,1},{17,25},{25,17},{2,10},{10... | collective-permute-start | bytes 393224 | tf_op jit(solution)/shard_map/ppermute | solution.py:562
  90.2 2.4 %collective-permute-start.40 = (bf16[32,2048]{1,0:T(8,128)(2,1)S(1)}, bf16[32,2048]{1,0:T(8,128)(2,1)S(1)}, u32[]{:S(2)}, u32[]{:S(2)}) collective-permute-start(bf16[32,2048]{1,0:T(8,128)(2,1)S(1)} %get-tuple-element.86.refs_0_), channel_id=1, source_target_pairs={{0,24},{8,16},{16,8},{24,0},{1,25},{9,17},{17,9},{25,1},{2,26},{10... | collective-permute-start | bytes 393224 | tf_op jit(solution)/shard_map/ppermute | solution.py:562
  92.6 1.5 collective-permute-done.38.refs_1_
  94.1 7.8 %collective-permute-done.39.refs_2_ = bf16[32,2048]{1,0:T(8,128)(2,1)S(1)} collective-permute-done((bf16[32,2048]{1,0:T(8,128)(2,1)S(1)}, bf16[32,2048]{1,0:T(8,128)(2,1)S(1)}, u32[]{:S(2)}, u32[]{:S(2)}) %collective-permute-start.39) | collective-permute-done | bytes 131104 | tf_op jit(solution)/shard_map/ppermute | solution.py:562
  102.5 0.8 collective-permute-start.43
  103.4 2.9 %collective-permute-start.27 = (bf16[272,256]{1,0:T(8,128)(2,1)S(1)}, bf16[272,256]{1,0:T(8,128)(2,1)S(1)}, u32[]{:S(2)}, u32[]{:S(2)}) collective-permute-start(bf16[272,256]{1,0:T(8,128)(2,1)S(1)} %get-tuple-element.69.refs_7_), channel_id=1, source_target_pairs={{0,8},{8,0},{16,24},{24,16},{1,9},{9,1},{17,25},{25,17},{2,10},{10... | collective-permute-start | bytes 417800 | tf_op jit(solution)/shard_map/ppermute | solution.py:562
  106.2 2.4 %collective-permute-start.29 = (bf16[272,256]{1,0:T(8,128)(2,1)S(1)}, bf16[272,256]{1,0:T(8,128)(2,1)S(1)}, u32[]{:S(2)}, u32[]{:S(2)}) collective-permute-start(bf16[272,256]{1,0:T(8,128)(2,1)S(1)} %get-tuple-element.71), channel_id=1, source_target_pairs={{0,24},{8,16},{16,8},{24,0},{1,25},{9,17},{17,9},{25,1},{2,26},{10... | collective-permute-start | bytes 417800 | tf_op jit(solution)/shard_map/ppermute | solution.py:562
  108.6 4.8 %largest_logits.4.refs_2_.refs_0_ = f32[8,256]{1,0:T(8,128)S(1)} custom-call(s32[6]{0:T(128)S(1)} %pad_add_fusion.place.refs_0_, bf16[128,2048]{1,0:T(8,128)(2,1)S(1)} %stack.10.refs_1_, bf16[128,2048]{1,0:T(8,128)(2,1)S(1)} %collective-permute-done.41.refs_2_, bf16[3136,2048]{1,0:T(8,128)(2,1)S(1)} %bitcast.14), custom_call_target="tpu_custom_call" | custom-call | flops 3288334336 | bytes 12845056 | tf_op jit(solution)/shard_map/largest_logits/pallas_call | solution.py:37
  113.5 5.4 %collective-permute-done.28.refs_4_ = bf16[272,256]{1,0:T(8,128)(2,1)S(1)} collective-permute-done((bf16[272,256]{1,0:T(8,128)(2,1)S(1)}, bf16[272,256]{1,0:T(8,128)(2,1)S(1)}, u32[]{:S(2)}, u32[]{:S(2)}) %collective-permute-start.28) | collective-permute-done | bytes 139296 | tf_op jit(solution)/shard_map/ppermute | solution.py:562
  119.6 1.4 collective-permute-start.46
  121.0 1.6 collective-permute-start.47
  122.6 4.8 %largest_logits.5.refs_4_.refs_1_ = f32[8,256]{1,0:T(8,128)S(1)} custom-call(s32[6]{0:T(128)S(1)} %pad_add_fusion.place.refs_0_, bf16[128,2048]{1,0:T(8,128)(2,1)S(1)} %get-tuple-element.87.refs_1_, bf16[128,2048]{1,0:T(8,128)(2,1)S(1)} %collective-permute-done.44.refs_2_, bf16[3136,2048]{1,0:T(8,128)(2,1)S(1)} %bitcast.14), custom_call_target="tpu_custom_call" | custom-call | flops 3288334336 | bytes 12845056 | tf_op jit(solution)/shard_map/largest_logits/pallas_call | solution.py:37
  127.4 4.8 %largest_logits.6.refs_2_ = f32[8,256]{1,0:T(8,128)S(1)} custom-call(s32[6]{0:T(128)S(1)} %pad_add_fusion.place.refs_0_, bf16[128,2048]{1,0:T(8,128)(2,1)S(1)} %get-tuple-element.88.refs_1_, bf16[128,2048]{1,0:T(8,128)(2,1)S(1)} %collective-permute-done.45.refs_2_, bf16[3136,2048]{1,0:T(8,128)(2,1)S(1)} %bitcast.14, f32[8,256]{1,0:T(8,128)S(1)} %largest_logits.5.refs_4_.refs_1_), custom_call_target="tpu_custom_call" | custom-call | flops 3288334336 | bytes 12845056 | tf_op jit(solution)/shard_map/largest_logits/pallas_call | solution.py:37
  132.4 1.9 %collective-permute-done.48.refs_2_ = bf16[128,2048]{1,0:T(8,128)(2,1)S(1)} collective-permute-done((bf16[128,2048]{1,0:T(8,128)(2,1)S(1)}, bf16[128,2048]{1,0:T(8,128)(2,1)S(1)}, u32[]{:S(2)}, u32[]{:S(2)}) %collective-permute-start.48) | collective-permute-done | bytes 524320 | tf_op jit(solution)/shard_map/ppermute | solution.py:559
  134.3 4.8 %largest_logits.7.refs_3_ = f32[8,256]{1,0:T(8,128)S(1)} custom-call(s32[6]{0:T(128)S(1)} %pad_add_fusion.place.refs_0_, bf16[128,2048]{1,0:T(8,128)(2,1)S(1)} %stack.11.refs_1_, bf16[128,2048]{1,0:T(8,128)(2,1)S(1)} %collective-permute-done.48.refs_2_, bf16[3136,2048]{1,0:T(8,128)(2,1)S(1)} %bitcast.14), custom_call_target="tpu_custom_call" | custom-call | flops 3288334336 | bytes 12845056 | tf_op jit(solution)/shard_map/largest_logits/pallas_call | solution.py:37
  139.1 0.6 gather_best.1
  139.9 1.0 collective-permute-done.49
  141.5 3.2 %collective-permute-done.50 = f32[8,256]{1,0:T(8,128)S(1)} collective-permute-done((f32[8,256]{1,0:T(8,128)S(1)}, f32[8,256]{1,0:T(8,128)S(1)}, u32[]{:S(2)}, u32[]{:S(2)}) %collective-permute-start.50) | collective-permute-done | bytes 8224 | tf_op jit(solution)/shard_map/ppermute | solution.py:636
  145.2 1.0 combine.3
  146.3 2.1 %collective-permute-done.51 = f32[8,256]{1,0:T(8,128)S(1)} collective-permute-done((f32[8,256]{1,0:T(8,128)S(1)}, f32[8,256]{1,0:T(8,128)S(1)}, u32[]{:S(2)}, u32[]{:S(2)}) %collective-permute-start.51) | collective-permute-done | bytes 8224 | tf_op jit(solution)/shard_map/ppermute | solution.py:636
  148.5 2.8 %collective-permute-start.52 = (f32[8,256]{1,0:T(8,128)S(1)}, f32[8,256]{1,0:T(8,128)S(1)}, u32[]{:S(2)}, u32[]{:S(2)}) collective-permute-start(f32[8,256]{1,0:T(8,128)S(1)} %add_select_fusion.2), channel_id=1, source_target_pairs={{0,8},{8,0},{16,24},{24,16},{1,9},{9,1},{17,25},{25,17},{2,10},{10... | collective-permute-start | bytes 24584 | tf_op jit(solution)/shard_map/ppermute | solution.py:636
  152.2 1.0 collective-permute-start.32
  153.2 2.1 %collective-permute-start.33 = (bf16[32,2048]{1,0:T(8,128)(2,1)S(1)}, bf16[32,2048]{1,0:T(8,128)(2,1)S(1)}, u32[]{:S(2)}, u32[]{:S(2)}) collective-permute-start(bf16[32,2048]{1,0:T(8,128)(2,1)S(1)} %get-tuple-element.77), channel_id=1, source_target_pairs={{0,6},{1,7},{2,4},{3,5},{4,2},{5,3},{6,0},{7,1},{8,14},{9,15},{10,... | collective-permute-start | bytes 393224 | tf_op jit(solution)/shard_map/ppermute | solution.py:559
  155.4 1.8 %collective-permute-done.31.refs_1_ = bf16[32,2048]{1,0:T(8,128)(2,1)S(1)} collective-permute-done((bf16[32,2048]{1,0:T(8,128)(2,1)S(1)}, bf16[32,2048]{1,0:T(8,128)(2,1)S(1)}, u32[]{:S(2)}, u32[]{:S(2)}) %collective-permute-start.31) | collective-permute-done | bytes 131104 | tf_op jit(solution)/shard_map/ppermute | solution.py:559
  157.2 2.2 %collective-permute-done.32.refs_2_ = bf16[32,2048]{1,0:T(8,128)(2,1)S(1)} collective-permute-done((bf16[32,2048]{1,0:T(8,128)(2,1)S(1)}, bf16[32,2048]{1,0:T(8,128)(2,1)S(1)}, u32[]{:S(2)}, u32[]{:S(2)}) %collective-permute-start.32) | collective-permute-done | bytes 131104 | tf_op jit(solution)/shard_map/ppermute | solution.py:559
  159.4 0.9 finish.2
  161.0 0.7 reshape.73
  (113 shorter events, 10.2 us)
Async XLA Ops:
  0.6 74.3 %copy-start = (bf16[256,2048]{1,0:T(8,128)(2,1)S(1)}, bf16[256,2048]{1,0:T(8,128)(2,1)}, u32[]{:S(2)}) copy-start(bf16[256,2048]{1,0:T(8,128)(2,1)} %w_keep.3) | copy-start | bytes 3145732
  0.6 22.5 %collective-permute-start.7 = (bf16[256,2048]{1,0:T(8,128)(2,1)}, bf16[256,2048]{1,0:T(8,128)(2,1)S(1)}, u32[]{:S(2)}, u32[]{:S(2)}) collective-permute-start(bf16[256,2048]{1,0:T(8,128)(2,1)} %w_keep.3), channel_id=1, source_target_pairs={{0,1},{1,0},{2,3},{3,2},{4,5},{5,4},{6,7},{7,6},{8,9},{9,8},{10,11... | collective-permute-start | bytes 3145736 | tf_op jit(solution)/shard_map/ppermute | solution.py:559
  1.2 16.0 %collective-permute-start = (bf16[256,256]{1,0:T(8,128)(2,1)}, bf16[256,256]{1,0:T(8,128)(2,1)S(1)}, u32[]{:S(2)}, u32[]{:S(2)}) collective-permute-start(bf16[256,256]{1,0:T(8,128)(2,1)} %refs_1_.2), channel_id=1, source_target_pairs={{0,2},{1,3},{2,0},{3,1},{4,6},{5,7},{6,4},{7,5},{8,10},{9,11},{10,... | collective-permute-start | bytes 393224 | tf_op jit(solution)/shard_map/ppermute | solution.py:559
  3.7 14.0 %collective-permute-start.1 = (bf16[256,256]{1,0:T(8,128)(2,1)}, bf16[256,256]{1,0:T(8,128)(2,1)S(1)}, u32[]{:S(2)}, u32[]{:S(2)}) collective-permute-start(bf16[256,256]{1,0:T(8,128)(2,1)} %refs_1_.2), channel_id=1, source_target_pairs={{0,4},{1,5},{2,6},{3,7},{4,0},{5,1},{6,2},{7,3},{8,12},{9,13},{10,... | collective-permute-start | bytes 393224 | tf_op jit(solution)/shard_map/ppermute | solution.py:559
  5.2 12.6 %collective-permute-start.2 = (bf16[256,256]{1,0:T(8,128)(2,1)}, bf16[256,256]{1,0:T(8,128)(2,1)S(1)}, u32[]{:S(2)}, u32[]{:S(2)}) collective-permute-start(bf16[256,256]{1,0:T(8,128)(2,1)} %refs_1_.2), channel_id=1, source_target_pairs={{0,6},{1,7},{2,4},{3,5},{4,2},{5,3},{6,0},{7,1},{8,14},{9,15},{10,... | collective-permute-start | bytes 393224 | tf_op jit(solution)/shard_map/ppermute | solution.py:559
  5.3 13.0 %collective-permute-start.3 = (bf16[256,256]{1,0:T(8,128)(2,1)}, bf16[256,256]{1,0:T(8,128)(2,1)S(1)}, u32[]{:S(2)}, u32[]{:S(2)}) collective-permute-start(bf16[256,256]{1,0:T(8,128)(2,1)} %refs_1_.2), channel_id=1, source_target_pairs={{0,1},{1,0},{2,3},{3,2},{4,5},{5,4},{6,7},{7,6},{8,9},{9,8},{10,11... | collective-permute-start | bytes 393224 | tf_op jit(solution)/shard_map/ppermute | solution.py:559
  7.3 79.7 %copy-start.7 = (f32[2048]{0:T(1024)S(1)}, f32[2048]{0:T(1024)}, u32[]{:S(2)}) copy-start(f32[2048]{0:T(1024)} %param.24) | copy-start | bytes 24580
  7.3 79.7 %copy-start.8 = (f32[2048]{0:T(1024)S(1)}, f32[2048]{0:T(1024)}, u32[]{:S(2)}) copy-start(f32[2048]{0:T(1024)} %param.25) | copy-start | bytes 24580
  7.3 101.3 %slice-start = ((s8[12845056]{0:T(1024)(128)(4,1)}), s8[262144]{0:T(1024)(128)(4,1)S(1)}, s32[]{:S(2)}) async-start(s8[12845056]{0:T(1024)(128)(4,1)} %bitcast.13), calls=%async_computation | async-start | bytes 524288
  17.1 3.2 %collective-permute-start.4 = (bf16[256,256]{1,0:T(8,128)(2,1)S(1)}, bf16[256,256]{1,0:T(8,128)(2,1)S(1)}, u32[]{:S(2)}, u32[]{:S(2)}) collective-permute-start(bf16[256,256]{1,0:T(8,128)(2,1)S(1)} %collective-permute-done.refs_2_), channel_id=1, source_target_pairs={{0,1},{1,0},{2,3},{3,2},{4,5},{5,4},{6,7},{7,6},{8,9},{9,8},{10,11... | collective-permute-start | bytes 393224 | tf_op jit(solution)/shard_map/ppermute | solution.py:559
  17.7 5.3 %collective-permute-start.5 = (bf16[256,256]{1,0:T(8,128)(2,1)S(1)}, bf16[256,256]{1,0:T(8,128)(2,1)S(1)}, u32[]{:S(2)}, u32[]{:S(2)}) collective-permute-start(bf16[256,256]{1,0:T(8,128)(2,1)S(1)} %collective-permute-done.1.refs_3_), channel_id=1, source_target_pairs={{0,1},{1,0},{2,3},{3,2},{4,5},{5,4},{6,7},{7,6},{8,9},{9,8},{10,11... | collective-permute-start | bytes 393224 | tf_op jit(solution)/shard_map/ppermute | solution.py:559
  17.8 5.3 %collective-permute-start.6 = (bf16[256,256]{1,0:T(8,128)(2,1)S(1)}, bf16[256,256]{1,0:T(8,128)(2,1)S(1)}, u32[]{:S(2)}, u32[]{:S(2)}) collective-permute-start(bf16[256,256]{1,0:T(8,128)(2,1)S(1)} %collective-permute-done.2.refs_4_), channel_id=1, source_target_pairs={{0,1},{1,0},{2,3},{3,2},{4,5},{5,4},{6,7},{7,6},{8,9},{9,8},{10,11... | collective-permute-start | bytes 393224 | tf_op jit(solution)/shard_map/ppermute | solution.py:559
  18.3 15.1 %collective-permute-start.11 = (bf16[256,256]{1,0:T(8,128)(2,1)S(1)}, bf16[256,256]{1,0:T(8,128)(2,1)S(1)}, u32[]{:S(2)}, u32[]{:S(2)}) collective-permute-start(bf16[256,256]{1,0:T(8,128)(2,1)S(1)} %get-tuple-element.94.refs_13_), channel_id=1, source_target_pairs={{0,8},{8,0},{16,24},{24,16},{1,9},{9,1},{17,25},{25,17},{2,10},{10... | collective-permute-start | bytes 393224 | tf_op jit(solution)/shard_map/ppermute | solution.py:562
  20.4 13.0 %collective-permute-start.12 = (bf16[256,256]{1,0:T(8,128)(2,1)S(1)}, bf16[256,256]{1,0:T(8,128)(2,1)S(1)}, u32[]{:S(2)}, u32[]{:S(2)}) collective-permute-start(bf16[256,256]{1,0:T(8,128)(2,1)S(1)} %get-tuple-element.92), channel_id=1, source_target_pairs={{0,16},{8,24},{16,0},{24,8},{1,17},{9,25},{17,1},{25,9},{2,18},{10... | collective-permute-start | bytes 393224 | tf_op jit(solution)/shard_map/ppermute | solution.py:562
  23.0 85.6 %slice-start.1 = ((s8[12845056]{0:T(1024)(128)(4,1)}), s8[4194304]{0:T(1024)(128)(4,1)S(1)}, s32[]{:S(2)}) async-start(s8[12845056]{0:T(1024)(128)(4,1)} %bitcast.13), calls=%async_computation.1 | async-start | bytes 8388608
  23.0 10.4 %collective-permute-start.13 = (bf16[256,256]{1,0:T(8,128)(2,1)S(1)}, bf16[256,256]{1,0:T(8,128)(2,1)S(1)}, u32[]{:S(2)}, u32[]{:S(2)}) collective-permute-start(bf16[256,256]{1,0:T(8,128)(2,1)S(1)} %get-tuple-element.91), channel_id=1, source_target_pairs={{0,24},{8,16},{16,8},{24,0},{1,25},{9,17},{17,9},{25,1},{2,26},{10... | collective-permute-start | bytes 393224 | tf_op jit(solution)/shard_map/ppermute | solution.py:562
  23.1 1.4 copy-start.1
  24.5 1.3 copy-start.2
  25.8 1.2 copy-start.3
  29.7 6.8 %collective-permute-start.8 = (bf16[256,256]{1,0:T(8,128)(2,1)S(1)}, bf16[256,256]{1,0:T(8,128)(2,1)S(1)}, u32[]{:S(2)}, u32[]{:S(2)}) collective-permute-start(bf16[256,256]{1,0:T(8,128)(2,1)S(1)} %get-tuple-element.48.refs_1_), channel_id=1, source_target_pairs={{0,8},{8,0},{16,24},{24,16},{1,9},{9,1},{17,25},{25,17},{2,10},{10... | collective-permute-start | bytes 393224 | tf_op jit(solution)/shard_map/ppermute | solution.py:562
  30.6 14.8 %collective-permute-start.10 = (bf16[256,256]{1,0:T(8,128)(2,1)S(1)}, bf16[256,256]{1,0:T(8,128)(2,1)S(1)}, u32[]{:S(2)}, u32[]{:S(2)}) collective-permute-start(bf16[256,256]{1,0:T(8,128)(2,1)S(1)} %get-tuple-element.48.refs_1_), channel_id=1, source_target_pairs={{0,24},{8,16},{16,8},{24,0},{1,25},{9,17},{17,9},{25,1},{2,26},{10... | collective-permute-start | bytes 393224 | tf_op jit(solution)/shard_map/ppermute | solution.py:562
  37.9 7.4 %collective-permute-start.14 = (bf16[256,256]{1,0:T(8,128)(2,1)S(1)}, bf16[256,256]{1,0:T(8,128)(2,1)S(1)}, u32[]{:S(2)}, u32[]{:S(2)}) collective-permute-start(bf16[256,256]{1,0:T(8,128)(2,1)S(1)} %choose.1.refs_6_), channel_id=1, source_target_pairs={{0,2},{1,3},{2,0},{3,1},{4,6},{5,7},{6,4},{7,5},{8,10},{9,11},{10,... | collective-permute-start | bytes 393224 | tf_op jit(solution)/shard_map/ppermute | solution.py:559
  39.5 7.7 %collective-permute-start.15 = (bf16[256,256]{1,0:T(8,128)(2,1)S(1)}, bf16[256,256]{1,0:T(8,128)(2,1)S(1)}, u32[]{:S(2)}, u32[]{:S(2)}) collective-permute-start(bf16[256,256]{1,0:T(8,128)(2,1)S(1)} %choose.1.refs_6_), channel_id=1, source_target_pairs={{0,4},{1,5},{2,6},{3,7},{4,0},{5,1},{6,2},{7,3},{8,12},{9,13},{10,... | collective-permute-start | bytes 393224 | tf_op jit(solution)/shard_map/ppermute | solution.py:559
  41.0 6.1 %collective-permute-start.16 = (bf16[256,256]{1,0:T(8,128)(2,1)S(1)}, bf16[256,256]{1,0:T(8,128)(2,1)S(1)}, u32[]{:S(2)}, u32[]{:S(2)}) collective-permute-start(bf16[256,256]{1,0:T(8,128)(2,1)S(1)} %choose.1.refs_6_), channel_id=1, source_target_pairs={{0,6},{1,7},{2,4},{3,5},{4,2},{5,3},{6,0},{7,1},{8,14},{9,15},{10,... | collective-permute-start | bytes 393224 | tf_op jit(solution)/shard_map/ppermute | solution.py:559
  41.5 8.3 %collective-permute-start.9 = (bf16[256,256]{1,0:T(8,128)(2,1)S(1)}, bf16[256,256]{1,0:T(8,128)(2,1)S(1)}, u32[]{:S(2)}, u32[]{:S(2)}) collective-permute-start(bf16[256,256]{1,0:T(8,128)(2,1)S(1)} %get-tuple-element.48.refs_1_), channel_id=1, source_target_pairs={{0,16},{8,24},{16,0},{24,8},{1,17},{9,25},{17,1},{25,9},{2,18},{10... | collective-permute-start | bytes 393224 | tf_op jit(solution)/shard_map/ppermute | solution.py:562
  45.3 4.5 %collective-permute-start.17 = (bf16[256,256]{1,0:T(8,128)(2,1)S(1)}, bf16[256,256]{1,0:T(8,128)(2,1)S(1)}, u32[]{:S(2)}, u32[]{:S(2)}) collective-permute-start(bf16[256,256]{1,0:T(8,128)(2,1)S(1)} %choose.1.refs_6_), channel_id=1, source_target_pairs={{0,1},{1,0},{2,3},{3,2},{4,5},{5,4},{6,7},{7,6},{8,9},{9,8},{10,11... | collective-permute-start | bytes 393224 | tf_op jit(solution)/shard_map/ppermute | solution.py:559
  45.3 4.5 %collective-permute-start.18 = (bf16[256,256]{1,0:T(8,128)(2,1)S(1)}, bf16[256,256]{1,0:T(8,128)(2,1)S(1)}, u32[]{:S(2)}, u32[]{:S(2)}) collective-permute-start(bf16[256,256]{1,0:T(8,128)(2,1)S(1)} %collective-permute-done.14.refs_7_), channel_id=1, source_target_pairs={{0,1},{1,0},{2,3},{3,2},{4,5},{5,4},{6,7},{7,6},{8,9},{9,8},{10,11... | collective-permute-start | bytes 393224 | tf_op jit(solution)/shard_map/ppermute | solution.py:559
  47.2 2.7 %collective-permute-start.19 = (bf16[256,256]{1,0:T(8,128)(2,1)S(1)}, bf16[256,256]{1,0:T(8,128)(2,1)S(1)}, u32[]{:S(2)}, u32[]{:S(2)}) collective-permute-start(bf16[256,256]{1,0:T(8,128)(2,1)S(1)} %collective-permute-done.15.refs_8_), channel_id=1, source_target_pairs={{0,1},{1,0},{2,3},{3,2},{4,5},{5,4},{6,7},{7,6},{8,9},{9,8},{10,11... | collective-permute-start | bytes 393224 | tf_op jit(solution)/shard_map/ppermute | solution.py:559
  47.2 2.7 %collective-permute-start.20 = (bf16[256,256]{1,0:T(8,128)(2,1)S(1)}, bf16[256,256]{1,0:T(8,128)(2,1)S(1)}, u32[]{:S(2)}, u32[]{:S(2)}) collective-permute-start(bf16[256,256]{1,0:T(8,128)(2,1)S(1)} %collective-permute-done.16.refs_9_), channel_id=1, source_target_pairs={{0,1},{1,0},{2,3},{3,2},{4,5},{5,4},{6,7},{7,6},{8,9},{9,8},{10,11... | collective-permute-start | bytes 393224 | tf_op jit(solution)/shard_map/ppermute | solution.py:559
  49.9 58.7 %slice-start.2 = ((s8[12845056]{0:T(1024)(128)(4,1)}), s8[4194304]{0:T(1024)(128)(4,1)S(1)}, s32[]{:S(2)}) async-start(s8[12845056]{0:T(1024)(128)(4,1)} %bitcast.13), calls=%async_computation.2 | async-start | bytes 8388608
  54.8 8.9 %collective-permute-start.24 = (bf16[272,256]{1,0:T(8,128)(2,1)S(1)}, bf16[272,256]{1,0:T(8,128)(2,1)S(1)}, u32[]{:S(2)}, u32[]{:S(2)}) collective-permute-start(bf16[272,256]{1,0:T(8,128)(2,1)S(1)} %get-tuple-element.65), channel_id=1, source_target_pairs={{0,8},{8,0},{16,24},{24,16},{1,9},{9,1},{17,25},{25,17},{2,10},{10... | collective-permute-start | bytes 417800 | tf_op jit(solution)/shard_map/ppermute | solution.py:562
  55.1 13.5 %collective-permute-start.25 = (bf16[272,256]{1,0:T(8,128)(2,1)S(1)}, bf16[272,256]{1,0:T(8,128)(2,1)S(1)}, u32[]{:S(2)}, u32[]{:S(2)}) collective-permute-start(bf16[272,256]{1,0:T(8,128)(2,1)S(1)} %get-tuple-element.66), channel_id=1, source_target_pairs={{0,16},{8,24},{16,0},{24,8},{1,17},{9,25},{17,1},{25,9},{2,18},{10... | collective-permute-start | bytes 417800 | tf_op jit(solution)/shard_map/ppermute | solution.py:562
  57.4 11.2 %collective-permute-start.26 = (bf16[272,256]{1,0:T(8,128)(2,1)S(1)}, bf16[272,256]{1,0:T(8,128)(2,1)S(1)}, u32[]{:S(2)}, u32[]{:S(2)}) collective-permute-start(bf16[272,256]{1,0:T(8,128)(2,1)S(1)} %get-tuple-element.67), channel_id=1, source_target_pairs={{0,24},{8,16},{16,8},{24,0},{1,25},{9,17},{17,9},{25,1},{2,26},{10... | collective-permute-start | bytes 417800 | tf_op jit(solution)/shard_map/ppermute | solution.py:562
  59.2 17.6 %collective-permute-start.21 = (bf16[256,256]{1,0:T(8,128)(2,1)S(1)}, bf16[256,256]{1,0:T(8,128)(2,1)S(1)}, u32[]{:S(2)}, u32[]{:S(2)}) collective-permute-start(bf16[256,256]{1,0:T(8,128)(2,1)S(1)} %get-tuple-element.56.refs_1_), channel_id=1, source_target_pairs={{0,8},{8,0},{16,24},{24,16},{1,9},{9,1},{17,25},{25,17},{2,10},{10... | collective-permute-start | bytes 393224 | tf_op jit(solution)/shard_map/ppermute | solution.py:562
  61.2 47.4 %slice-start.3 = ((s8[12845056]{0:T(1024)(128)(4,1)}), s8[4194304]{0:T(1024)(128)(4,1)S(1)}, s32[]{:S(2)}) async-start(s8[12845056]{0:T(1024)(128)(4,1)} %bitcast.13), calls=%async_computation.3 | async-start | bytes 8388608
  69.6 5.3 %collective-permute-start.34 = (bf16[128,256]{1,0:T(8,128)(2,1)S(1)}, bf16[128,256]{1,0:T(8,128)(2,1)S(1)}, u32[]{:S(2)}, u32[]{:S(2)}) collective-permute-start(bf16[128,256]{1,0:T(8,128)(2,1)S(1)} %get-tuple-element.79), channel_id=1, source_target_pairs={{0,1},{1,0},{2,3},{3,2},{4,5},{5,4},{6,7},{7,6},{8,9},{9,8},{10,11... | collective-permute-start | bytes 196616 | tf_op jit(solution)/shard_map/ppermute | solution.py:559
  69.7 13.5 %collective-permute-start.22 = (bf16[256,256]{1,0:T(8,128)(2,1)S(1)}, bf16[256,256]{1,0:T(8,128)(2,1)S(1)}, u32[]{:S(2)}, u32[]{:S(2)}) collective-permute-start(bf16[256,256]{1,0:T(8,128)(2,1)S(1)} %get-tuple-element.56.refs_1_), channel_id=1, source_target_pairs={{0,16},{8,24},{16,0},{24,8},{1,17},{9,25},{17,1},{25,9},{2,18},{10... | collective-permute-start | bytes 393224 | tf_op jit(solution)/shard_map/ppermute | solution.py:562
  73.2 10.0 %collective-permute-start.23 = (bf16[256,256]{1,0:T(8,128)(2,1)S(1)}, bf16[256,256]{1,0:T(8,128)(2,1)S(1)}, u32[]{:S(2)}, u32[]{:S(2)}) collective-permute-start(bf16[256,256]{1,0:T(8,128)(2,1)S(1)} %get-tuple-element.56.refs_1_), channel_id=1, source_target_pairs={{0,24},{8,16},{16,8},{24,0},{1,25},{9,17},{17,9},{25,1},{2,26},{10... | collective-permute-start | bytes 393224 | tf_op jit(solution)/shard_map/ppermute | solution.py:562
  75.4 11.6 %collective-permute-start.35 = (bf16[32,2048]{1,0:T(8,128)(2,1)S(1)}, bf16[32,2048]{1,0:T(8,128)(2,1)S(1)}, u32[]{:S(2)}, u32[]{:S(2)}) collective-permute-start(bf16[32,2048]{1,0:T(8,128)(2,1)S(1)} %get-tuple-element.81), channel_id=1, source_target_pairs={{0,2},{1,3},{2,0},{3,1},{4,6},{5,7},{6,4},{7,5},{8,10},{9,11},{10,... | collective-permute-start | bytes 393224 | tf_op jit(solution)/shard_map/ppermute | solution.py:559
  76.0 11.0 %collective-permute-start.36 = (bf16[32,2048]{1,0:T(8,128)(2,1)S(1)}, bf16[32,2048]{1,0:T(8,128)(2,1)S(1)}, u32[]{:S(2)}, u32[]{:S(2)}) collective-permute-start(bf16[32,2048]{1,0:T(8,128)(2,1)S(1)} %get-tuple-element.82), channel_id=1, source_target_pairs={{0,4},{1,5},{2,6},{3,7},{4,0},{5,1},{6,2},{7,3},{8,12},{9,13},{10,... | collective-permute-start | bytes 393224 | tf_op jit(solution)/shard_map/ppermute | solution.py:559
  76.8 10.2 %collective-permute-start.37 = (bf16[32,2048]{1,0:T(8,128)(2,1)S(1)}, bf16[32,2048]{1,0:T(8,128)(2,1)S(1)}, u32[]{:S(2)}, u32[]{:S(2)}) collective-permute-start(bf16[32,2048]{1,0:T(8,128)(2,1)S(1)} %get-tuple-element.83), channel_id=1, source_target_pairs={{0,6},{1,7},{2,4},{3,5},{4,2},{5,3},{6,0},{7,1},{8,14},{9,15},{10,... | collective-permute-start | bytes 393224 | tf_op jit(solution)/shard_map/ppermute | solution.py:559
  87.9 6.2 %collective-permute-start.38 = (bf16[32,2048]{1,0:T(8,128)(2,1)S(1)}, bf16[32,2048]{1,0:T(8,128)(2,1)S(1)}, u32[]{:S(2)}, u32[]{:S(2)}) collective-permute-start(bf16[32,2048]{1,0:T(8,128)(2,1)S(1)} %get-tuple-element.86.refs_0_), channel_id=1, source_target_pairs={{0,8},{8,0},{16,24},{24,16},{1,9},{9,1},{17,25},{25,17},{2,10},{10... | collective-permute-start | bytes 393224 | tf_op jit(solution)/shard_map/ppermute | solution.py:562
  90.2 11.7 %collective-permute-start.39 = (bf16[32,2048]{1,0:T(8,128)(2,1)S(1)}, bf16[32,2048]{1,0:T(8,128)(2,1)S(1)}, u32[]{:S(2)}, u32[]{:S(2)}) collective-permute-start(bf16[32,2048]{1,0:T(8,128)(2,1)S(1)} %get-tuple-element.86.refs_0_), channel_id=1, source_target_pairs={{0,16},{8,24},{16,0},{24,8},{1,17},{9,25},{17,1},{25,9},{2,18},{10... | collective-permute-start | bytes 393224 | tf_op jit(solution)/shard_map/ppermute | solution.py:562
  90.2 11.7 %collective-permute-start.40 = (bf16[32,2048]{1,0:T(8,128)(2,1)S(1)}, bf16[32,2048]{1,0:T(8,128)(2,1)S(1)}, u32[]{:S(2)}, u32[]{:S(2)}) collective-permute-start(bf16[32,2048]{1,0:T(8,128)(2,1)S(1)} %get-tuple-element.86.refs_0_), channel_id=1, source_target_pairs={{0,24},{8,16},{16,8},{24,0},{1,25},{9,17},{17,9},{25,1},{2,26},{10... | collective-permute-start | bytes 393224 | tf_op jit(solution)/shard_map/ppermute | solution.py:562
  102.0 4.3 %collective-permute-start.41 = (bf16[128,2048]{1,0:T(8,128)(2,1)S(1)}, bf16[128,2048]{1,0:T(8,128)(2,1)S(1)}, u32[]{:S(2)}, u32[]{:S(2)}) collective-permute-start(bf16[128,2048]{1,0:T(8,128)(2,1)S(1)} %stack.10.refs_1_), channel_id=1, source_target_pairs={{0,1},{1,0},{2,3},{3,2},{4,5},{5,4},{6,7},{7,6},{8,9},{9,8},{10,11... | collective-permute-start | bytes 1572872 | tf_op jit(solution)/shard_map/ppermute | solution.py:559
  102.0 16.8 %collective-permute-start.42 = (bf16[128,2048]{1,0:T(8,128)(2,1)S(1)}, bf16[128,2048]{1,0:T(8,128)(2,1)S(1)}, u32[]{:S(2)}, u32[]{:S(2)}) collective-permute-start(bf16[128,2048]{1,0:T(8,128)(2,1)S(1)} %stack.10.refs_1_), channel_id=1, source_target_pairs={{0,2},{1,3},{2,0},{3,1},{4,6},{5,7},{6,4},{7,5},{8,10},{9,11},{10,... | collective-permute-start | bytes 1572872 | tf_op jit(solution)/shard_map/ppermute | solution.py:559
  102.5 16.4 %collective-permute-start.43 = (bf16[128,2048]{1,0:T(8,128)(2,1)S(1)}, bf16[128,2048]{1,0:T(8,128)(2,1)S(1)}, u32[]{:S(2)}, u32[]{:S(2)}) collective-permute-start(bf16[128,2048]{1,0:T(8,128)(2,1)S(1)} %stack.10.refs_1_), channel_id=1, source_target_pairs={{0,4},{1,5},{2,6},{3,7},{4,0},{5,1},{6,2},{7,3},{8,12},{9,13},{10,... | collective-permute-start | bytes 1572872 | tf_op jit(solution)/shard_map/ppermute | solution.py:559
  103.4 10.1 %collective-permute-start.27 = (bf16[272,256]{1,0:T(8,128)(2,1)S(1)}, bf16[272,256]{1,0:T(8,128)(2,1)S(1)}, u32[]{:S(2)}, u32[]{:S(2)}) collective-permute-start(bf16[272,256]{1,0:T(8,128)(2,1)S(1)} %get-tuple-element.69.refs_7_), channel_id=1, source_target_pairs={{0,8},{8,0},{16,24},{24,16},{1,9},{9,1},{17,25},{25,17},{2,10},{10... | collective-permute-start | bytes 417800 | tf_op jit(solution)/shard_map/ppermute | solution.py:562
  106.2 12.6 %collective-permute-start.28 = (bf16[272,256]{1,0:T(8,128)(2,1)S(1)}, bf16[272,256]{1,0:T(8,128)(2,1)S(1)}, u32[]{:S(2)}, u32[]{:S(2)}) collective-permute-start(bf16[272,256]{1,0:T(8,128)(2,1)S(1)} %get-tuple-element.70), channel_id=1, source_target_pairs={{0,16},{8,24},{16,0},{24,8},{1,17},{9,25},{17,1},{25,9},{2,18},{10... | collective-permute-start | bytes 417800 | tf_op jit(solution)/shard_map/ppermute | solution.py:562
  106.2 12.6 %collective-permute-start.29 = (bf16[272,256]{1,0:T(8,128)(2,1)S(1)}, bf16[272,256]{1,0:T(8,128)(2,1)S(1)}, u32[]{:S(2)}, u32[]{:S(2)}) collective-permute-start(bf16[272,256]{1,0:T(8,128)(2,1)S(1)} %get-tuple-element.71), channel_id=1, source_target_pairs={{0,24},{8,16},{16,8},{24,0},{1,25},{9,17},{17,9},{25,1},{2,26},{10... | collective-permute-start | bytes 417800 | tf_op jit(solution)/shard_map/ppermute | solution.py:562
  119.0 3.6 %collective-permute-start.44 = (bf16[128,2048]{1,0:T(8,128)(2,1)S(1)}, bf16[128,2048]{1,0:T(8,128)(2,1)S(1)}, u32[]{:S(2)}, u32[]{:S(2)}) collective-permute-start(bf16[128,2048]{1,0:T(8,128)(2,1)S(1)} %get-tuple-element.87.refs_1_), channel_id=1, source_target_pairs={{0,1},{1,0},{2,3},{3,2},{4,5},{5,4},{6,7},{7,6},{8,9},{9,8},{10,11... | collective-permute-start | bytes 1572872 | tf_op jit(solution)/shard_map/ppermute | solution.py:559
  119.1 8.3 %collective-permute-start.45 = (bf16[128,2048]{1,0:T(8,128)(2,1)S(1)}, bf16[128,2048]{1,0:T(8,128)(2,1)S(1)}, u32[]{:S(2)}, u32[]{:S(2)}) collective-permute-start(bf16[128,2048]{1,0:T(8,128)(2,1)S(1)} %get-tuple-element.88.refs_1_), channel_id=1, source_target_pairs={{0,1},{1,0},{2,3},{3,2},{4,5},{5,4},{6,7},{7,6},{8,9},{9,8},{10,11... | collective-permute-start | bytes 1572872 | tf_op jit(solution)/shard_map/ppermute | solution.py:559
  119.6 12.7 %collective-permute-start.46 = (bf16[64,2048]{1,0:T(8,128)(2,1)S(1)}, bf16[64,2048]{1,0:T(8,128)(2,1)S(1)}, u32[]{:S(2)}, u32[]{:S(2)}) collective-permute-start(bf16[64,2048]{1,0:T(8,128)(2,1)S(1)} %get-tuple-element.89), channel_id=1, source_target_pairs={{0,2},{1,3},{2,0},{3,1},{4,6},{5,7},{6,4},{7,5},{8,10},{9,11},{10,... | collective-permute-start | bytes 786440 | tf_op jit(solution)/shard_map/ppermute | solution.py:559
  121.0 11.3 %collective-permute-start.47 = (bf16[64,2048]{1,0:T(8,128)(2,1)S(1)}, bf16[64,2048]{1,0:T(8,128)(2,1)S(1)}, u32[]{:S(2)}, u32[]{:S(2)}) collective-permute-start(bf16[64,2048]{1,0:T(8,128)(2,1)S(1)} %get-tuple-element.90), channel_id=1, source_target_pairs={{0,4},{1,5},{2,6},{3,7},{4,0},{5,1},{6,2},{7,3},{8,12},{9,13},{10,... | collective-permute-start | bytes 786440 | tf_op jit(solution)/shard_map/ppermute | solution.py:559
  132.3 2.0 %collective-permute-start.48 = (bf16[128,2048]{1,0:T(8,128)(2,1)S(1)}, bf16[128,2048]{1,0:T(8,128)(2,1)S(1)}, u32[]{:S(2)}, u32[]{:S(2)}) collective-permute-start(bf16[128,2048]{1,0:T(8,128)(2,1)S(1)} %stack.11.refs_1_), channel_id=1, source_target_pairs={{0,1},{1,0},{2,3},{3,2},{4,5},{5,4},{6,7},{7,6},{8,9},{9,8},{10,11... | collective-permute-start | bytes 1572872 | tf_op jit(solution)/shard_map/ppermute | solution.py:559
  139.8 1.2 collective-permute-start.49
  141.0 3.7 %collective-permute-start.50 = (f32[8,256]{1,0:T(8,128)S(1)}, f32[8,256]{1,0:T(8,128)S(1)}, u32[]{:S(2)}, u32[]{:S(2)}) collective-permute-start(f32[8,256]{1,0:T(8,128)S(1)} %add_select_fusion.4), channel_id=1, source_target_pairs={{0,2},{1,3},{2,0},{3,1},{4,6},{5,7},{6,4},{7,5},{8,10},{9,11},{10,... | collective-permute-start | bytes 24584 | tf_op jit(solution)/shard_map/ppermute | solution.py:636
  144.7 3.7 %collective-permute-start.51 = (f32[8,256]{1,0:T(8,128)S(1)}, f32[8,256]{1,0:T(8,128)S(1)}, u32[]{:S(2)}, u32[]{:S(2)}) collective-permute-start(f32[8,256]{1,0:T(8,128)S(1)} %add_select_fusion.3), channel_id=1, source_target_pairs={{0,4},{1,5},{2,6},{3,7},{4,0},{5,1},{6,2},{7,3},{8,12},{9,13},{10,... | collective-permute-start | bytes 24584 | tf_op jit(solution)/shard_map/ppermute | solution.py:636
  146.2 5.0 %collective-permute-start.30 = (bf16[128,256]{1,0:T(8,128)(2,1)S(1)}, bf16[128,256]{1,0:T(8,128)(2,1)S(1)}, u32[]{:S(2)}, u32[]{:S(2)}) collective-permute-start(bf16[128,256]{1,0:T(8,128)(2,1)S(1)} %get-tuple-element.73), channel_id=1, source_target_pairs={{0,1},{1,0},{2,3},{3,2},{4,5},{5,4},{6,7},{7,6},{8,9},{9,8},{10,11... | collective-permute-start | bytes 196616 | tf_op jit(solution)/shard_map/ppermute | solution.py:559
  148.5 6.8 %collective-permute-start.52 = (f32[8,256]{1,0:T(8,128)S(1)}, f32[8,256]{1,0:T(8,128)S(1)}, u32[]{:S(2)}, u32[]{:S(2)}) collective-permute-start(f32[8,256]{1,0:T(8,128)S(1)} %add_select_fusion.2), channel_id=1, source_target_pairs={{0,8},{8,0},{16,24},{24,16},{1,9},{9,1},{17,25},{25,17},{2,10},{10... | collective-permute-start | bytes 24584 | tf_op jit(solution)/shard_map/ppermute | solution.py:636
  151.7 5.4 %collective-permute-start.31 = (bf16[32,2048]{1,0:T(8,128)(2,1)S(1)}, bf16[32,2048]{1,0:T(8,128)(2,1)S(1)}, u32[]{:S(2)}, u32[]{:S(2)}) collective-permute-start(bf16[32,2048]{1,0:T(8,128)(2,1)S(1)} %get-tuple-element.75), channel_id=1, source_target_pairs={{0,2},{1,3},{2,0},{3,1},{4,6},{5,7},{6,4},{7,5},{8,10},{9,11},{10,... | collective-permute-start | bytes 393224 | tf_op jit(solution)/shard_map/ppermute | solution.py:559
  152.2 7.1 %collective-permute-start.32 = (bf16[32,2048]{1,0:T(8,128)(2,1)S(1)}, bf16[32,2048]{1,0:T(8,128)(2,1)S(1)}, u32[]{:S(2)}, u32[]{:S(2)}) collective-permute-start(bf16[32,2048]{1,0:T(8,128)(2,1)S(1)} %get-tuple-element.76), channel_id=1, source_target_pairs={{0,4},{1,5},{2,6},{3,7},{4,0},{5,1},{6,2},{7,3},{8,12},{9,13},{10,... | collective-permute-start | bytes 393224 | tf_op jit(solution)/shard_map/ppermute | solution.py:559
  153.2 6.2 %collective-permute-start.33 = (bf16[32,2048]{1,0:T(8,128)(2,1)S(1)}, bf16[32,2048]{1,0:T(8,128)(2,1)S(1)}, u32[]{:S(2)}, u32[]{:S(2)}) collective-permute-start(bf16[32,2048]{1,0:T(8,128)(2,1)S(1)} %get-tuple-element.77), channel_id=1, source_target_pairs={{0,6},{1,7},{2,4},{3,5},{4,2},{5,3},{6,0},{7,1},{8,14},{9,15},{10,... | collective-permute-start | bytes 393224 | tf_op jit(solution)/shard_map/ppermute | solution.py:559
  155.4 4.9 %collective-permute-start.53 = (f32[8,256]{1,0:T(8,128)S(1)}, f32[8,256]{1,0:T(8,128)S(1)}, u32[]{:S(2)}, u32[]{:S(2)}) collective-permute-start(f32[8,256]{1,0:T(8,128)S(1)} %add_select_fusion.1), channel_id=1, source_target_pairs={{0,16},{8,24},{16,0},{24,8},{1,17},{9,25},{17,1},{25,9},{2,18},{10... | collective-permute-start | bytes 24584 | tf_op jit(solution)/shard_map/ppermute | solution.py:636
  (5 other events, 4.4 us)

commit v4 on v3

--- a/solution.py
+++ b/solution.py
@@ -489,7 +489,7 @@
 def largest_logits(share, tok_count, place, mine, other, lm_head, after=()):
     half, full = mine.shape
     vocab = lm_head.shape[0]
-    span = vocab // 4 if vocab % 64 == 0 else vocab // 7
+    span = vocab // 2 if vocab % 32 == 0 else vocab // 7
     return call(
         functools.partial(logits_kernel, share, tok_count),
         (place, mine, other, lm_head),
@@ -593,9 +593,9 @@
         block_rows, place, pieces + others, w_query, w_key, w_value, [w_out_other, found[1]]
     )
     queries = exchange([query] * len(tok_masks))
-    cache_keys, cache_values = carry(cache_keys, cache_values)
+    cache_keys, cache_values, accepted = carry(cache_keys, cache_values, accept.reshape(1, -1))
     own = own_part(tok_count, place, query, key, value, cache_keys, cache_values)
-    chosen = choose(place, accept.reshape(1, -1), owners, states, embedded, queries[:1])
+    chosen = choose(place, accepted, owners, states, embedded, queries[:1])
     pieces, others = spread(chosen)
     messages, (query, key, value, residual_two) = second_stage(
         tok_count, tok_masks, place, queries, cache_keys, cache_values, pieces + others, *weights
@@ -605,9 +605,9 @@
     own_two = own_part(tok_count, place, query, key, value, cache_keys, cache_values)
     keep = join(own, messages, [own_two[0]])
     parts = away_parts(tok_count, tok_masks, place, queries, cache_keys, cache_values, [keep[0]])
-    _, normed, square = finish_layer(False, out_layer(*keep), residual, parts[:1])
-
-    column = stack([normed] + exchange([normed] * len(tok_masks)))
+    _, normed, square = finish_layer(False, out_layer(*keep), residual)
+
+    column = stack([normed] + exchange([normed] * len(tok_masks)), parts[:1])
     parts = exchange(parts)
 
     def best_of(piece, after=()):

time: 162 us -> 157 us (0.969)
  starting transfers between devices: 58.4 us -> 54 us
  Pallas kernels: 40.9 us -> 39.2 us
    ppermute x31, waiting for transfers between devices: 7.28 us -> 12.6 us  [by_head(): return lax.ppermute(value, 'head', xor_pairs(head_count, mask))]
    ppermute x18, waiting for transfers between devices: 27.2 us -> 23.2 us  [by_tok(): return lax.ppermute(value, 'tok', xor_pairs(tok_count, mask))]
    ppermute x18, starting transfers between devices: 32 us -> 28 us  [by_tok(): return lax.ppermute(value, 'tok', xor_pairs(tok_count, mask))]
    pallas_call x17, Pallas kernels: 38.7 us -> 37 us  [call(): return pl.pallas_call(body, in_specs=specs, **rest)(*operands, *after)]
  transfers between devices with their start and end apart: 54 -> 54, of which waited for: 14 -> 17; matrix products, arithmetic and copies ran while one was open for 7% -> 7% of each run, Pallas kernels for 18% -> 18%
where the time goes in v4:
time: 157 us; the launch traced here: 156 us
  starting transfers between devices  54 us (34%)
  waiting for transfers between devices  41.6 us (26%)
  Pallas kernels  39.2 us (25%)
  local copies, waits for them, and re-layouts  18.9 us (12%)
  other arithmetic  1.63 us (1%)
    pallas_call x17, Pallas kernels, call(): return pl.pallas_call(body, in_specs=specs, **rest)(*operands, *after)  37 us
    ppermute x18, starting transfers between devices, by_tok(): return lax.ppermute(value, 'tok', xor_pairs(tok_count, mask))  28 us
    ppermute x18, waiting for transfers between devices, by_tok(): return lax.ppermute(value, 'tok', xor_pairs(tok_count, mask))  23.2 us
    ppermute x31, starting transfers between devices, by_head(): return lax.ppermute(value, 'head', xor_pairs(head_count, mask))  21.9 us
    ppermute x31, waiting for transfers between devices, by_head(): return lax.ppermute(value, 'head', xor_pairs(head_count, mask))  12.6 us
    gather x1, local copies, waits for them, and re-layouts, shards(): embed.at[ids].get(mode='promise_in_bounds')  9.81 us
    unnamed x30, local copies, waits for them, and re-layouts  8.26 us
    ppermute x5, waiting for transfers between devices, shards(): other = lax.ppermute(best, axis, xor_pairs(size, mask))  5.82 us
  transfers between devices with their start and end apart: 54, of which 17 were waited for; matrix products, arithmetic and copies ran while one was open for 7% of the time, Pallas kernels for 18%

profile of v4, /device:TPU:0, one launch (start us, length us, event | category | flops | bytes accessed | tf_op | source)
XLA Modules:
  0.0 156.3 jit_solution(971819868460353015)
XLA Ops:
  1.2 2.6 %collective-permute-start = (bf16[256,256]{1,0:T(8,128)(2,1)}, bf16[256,256]{1,0:T(8,128)(2,1)S(1)}, u32[]{:S(2)}, u32[]{:S(2)}) collective-permute-start(bf16[256,256]{1,0:T(8,128)(2,1)} %refs_1_.2), channel_id=1, source_target_pairs={{0,2},{1,3},{2,0},{3,1},{4,6},{5,7},{6,4},{7,5},{8,10},{9,11},{10,... | collective-permute-start | bytes 393224 | tf_op jit(solution)/shard_map/ppermute | solution.py:559
  3.7 1.5 collective-permute-start.1
  5.3 0.7 pad_add_fusion.place.refs_0_
  6.0 0.7 copy-done.9
  7.3 9.8 %gather_fusion = bf16[1024,256]{1,0:T(8,128)(2,1)S(1)} fusion(bf16[25088,256]{1,0:T(8,128)(2,1)} %param.26, s32[1024]{0:T(1024)S(1)} %broadcast_clamp_fusion), kind=kCustom, calls=%fused_computation | custom fusion | bytes 1052672 | tf_op jit(solution)/shard_map/gather | solution.py:587
  18.3 2.1 %collective-permute-start.11 = (bf16[256,256]{1,0:T(8,128)(2,1)S(1)}, bf16[256,256]{1,0:T(8,128)(2,1)S(1)}, u32[]{:S(2)}, u32[]{:S(2)}) collective-permute-start(bf16[256,256]{1,0:T(8,128)(2,1)S(1)} %get-tuple-element.96.refs_13_), channel_id=1, source_target_pairs={{0,8},{8,0},{16,24},{24,16},{1,9},{9,1},{17,25},{25,17},{2,10},{10... | collective-permute-start | bytes 393224 | tf_op jit(solution)/shard_map/ppermute | solution.py:562
  20.4 2.6 %collective-permute-start.12 = (bf16[256,256]{1,0:T(8,128)(2,1)S(1)}, bf16[256,256]{1,0:T(8,128)(2,1)S(1)}, u32[]{:S(2)}, u32[]{:S(2)}) collective-permute-start(bf16[256,256]{1,0:T(8,128)(2,1)S(1)} %get-tuple-element.94), channel_id=1, source_target_pairs={{0,16},{8,24},{16,0},{24,8},{1,17},{9,25},{17,1},{25,9},{2,18},{10... | collective-permute-start | bytes 393224 | tf_op jit(solution)/shard_map/ppermute | solution.py:562
  23.1 1.4 copy-done.1
  24.5 1.3 copy-done.2
  25.8 1.2 copy-done.3
  27.0 0.9 copy-done.6
  27.9 1.8 %project.1 = (bf16[256,256]{1,0:T(8,128)(2,1)S(1)}, bf16[256,256]{1,0:T(8,128)(2,1)S(1)}, bf16[256,256]{1,0:T(8,128)(2,1)S(1)}, bf16[32,2048]{1,0:T(8,128)(2,1)S...) custom-call(s32[6]{0:T(128)S(1)} %pad_add_fusion.place.refs_0_, ...), custom_call_target="tpu_custom_call" | custom-call | flops 805306368 | bytes 4194304 | tf_op jit(solution)/shard_map/project/pallas_call | solution.py:37
  29.7 0.9 collective-permute-start.8
  30.6 1.0 copy-done.4
  31.6 1.0 copy-done.5
  33.4 2.8 %collective-permute-start.10 = (bf16[256,256]{1,0:T(8,128)(2,1)S(1)}, bf16[256,256]{1,0:T(8,128)(2,1)S(1)}, u32[]{:S(2)}, u32[]{:S(2)}) collective-permute-start(bf16[256,256]{1,0:T(8,128)(2,1)S(1)} %get-tuple-element.49.refs_1_), channel_id=1, source_target_pairs={{0,24},{8,16},{16,8},{24,0},{1,25},{9,17},{17,9},{25,1},{2,26},{10... | collective-permute-start | bytes 393224 | tf_op jit(solution)/shard_map/ppermute | solution.py:562
  36.2 0.7 choose.1.refs_6_
  36.9 1.6 collective-permute-start.14
  38.5 1.5 collective-permute-start.15
  40.5 0.8 collective-permute-start.9
  41.2 1.8 %collective-permute-done.14.refs_7_ = bf16[256,256]{1,0:T(8,128)(2,1)S(1)} collective-permute-done((bf16[256,256]{1,0:T(8,128)(2,1)S(1)}, bf16[256,256]{1,0:T(8,128)(2,1)S(1)}, u32[]{:S(2)}, u32[]{:S(2)}) %collective-permute-start.14) | collective-permute-done | bytes 131104 | tf_op jit(solution)/shard_map/ppermute | solution.py:559
  43.1 3.1 %collective-permute-done.15.refs_8_ = bf16[256,256]{1,0:T(8,128)(2,1)S(1)} collective-permute-done((bf16[256,256]{1,0:T(8,128)(2,1)S(1)}, bf16[256,256]{1,0:T(8,128)(2,1)S(1)}, u32[]{:S(2)}, u32[]{:S(2)}) %collective-permute-start.15) | collective-permute-done | bytes 131104 | tf_op jit(solution)/shard_map/ppermute | solution.py:559
  46.7 1.1 collective-permute-done.9.refs_2_
  47.8 4.9 %second_stage.1 = (bf16[272,256]{1,0:T(8,128)(2,1)S(1)}, bf16[272,256]{1,0:T(8,128)(2,1)S(1)}, bf16[272,256]{1,0:T(8,128)(2,1)S(1)}, bf16[256,256]{1,0:T(8,128)(...) custom-call(s32[6]{0:T(128)S(1)} %pad_add_fusion.place.refs_0_, ...), custom_call_target="tpu_custom_call" | custom-call | flops 1073741824 | bytes 4194304 | tf_op jit(solution)/shard_map/second_stage/pallas_call | solution.py:37
  52.7 1.5 collective-permute-start.25
  54.2 2.9 %collective-permute-start.26 = (bf16[272,256]{1,0:T(8,128)(2,1)S(1)}, bf16[272,256]{1,0:T(8,128)(2,1)S(1)}, u32[]{:S(2)}, u32[]{:S(2)}) collective-permute-start(bf16[272,256]{1,0:T(8,128)(2,1)S(1)} %get-tuple-element.69), channel_id=1, source_target_pairs={{0,24},{8,16},{16,8},{24,0},{1,25},{9,17},{17,9},{25,1},{2,26},{10... | collective-permute-start | bytes 417800 | tf_op jit(solution)/shard_map/ppermute | solution.py:562
  57.1 2.0 %own_part.3 = (f32[256,256]{1,0:T(8,128)S(1)}, f32[256,256]{1,0:T(8,128)S(1)}) custom-call(s32[6]{0:T(128)S(1)} %pad_add_fusion.place.refs_0_, bf16[256,256]{1,0:T(8,128)(2,1)S(1)} %get-tuple-element.49.refs_1_, bf16[256,256]{1,0:T(8,128)(2,1)S(1)} %get-tuple-element.63.refs_2_, bf16[256,256]{1,0:T(8,128)(2,1)S(1)} %get-tuple-element.64.refs_3_, ...), custom_call_target="tpu_custom_call" | custom-call | flops 268435456 | bytes 1048576 | tf_op jit(solution)/shard_map/own_part/pallas_call | solution.py:37
  59.2 2.2 %own_part.2 = (f32[256,256]{1,0:T(8,128)S(1)}, f32[256,256]{1,0:T(8,128)S(1)}) custom-call(s32[6]{0:T(128)S(1)} %pad_add_fusion.place.refs_0_, bf16[256,256]{1,0:T(8,128)(2,1)S(1)} %get-tuple-element.58.refs_1_, bf16[256,256]{1,0:T(8,128)(2,1)S(1)} %get-tuple-element.59.refs_2_, bf16[256,256]{1,0:T(8,128)(2,1)S(1)} %get-tuple-element.60.refs_3_, ...), custom_call_target="tpu_custom_call" | custom-call | flops 268435456 | bytes 1048576 | tf_op jit(solution)/shard_map/own_part/pallas_call | solution.py:37
  61.4 4.9 %collective-permute-done.25.refs_4_ = bf16[272,256]{1,0:T(8,128)(2,1)S(1)} collective-permute-done((bf16[272,256]{1,0:T(8,128)(2,1)S(1)}, bf16[272,256]{1,0:T(8,128)(2,1)S(1)}, u32[]{:S(2)}, u32[]{:S(2)}) %collective-permute-start.25) | collective-permute-done | bytes 139296 | tf_op jit(solution)/shard_map/ppermute | solution.py:562
  66.2 1.0 combine.2
  67.3 1.2 collective-permute-done.34.other
  69.1 0.9 collective-permute-start.35
  70.0 1.2 collective-permute-start.36
  71.2 1.4 collective-permute-start.37
  72.6 2.8 %collective-permute-start.21 = (bf16[256,256]{1,0:T(8,128)(2,1)S(1)}, bf16[256,256]{1,0:T(8,128)(2,1)S(1)}, u32[]{:S(2)}, u32[]{:S(2)}) collective-permute-start(bf16[256,256]{1,0:T(8,128)(2,1)S(1)} %get-tuple-element.58.refs_1_), channel_id=1, source_target_pairs={{0,8},{8,0},{16,24},{24,16},{1,9},{9,1},{17,25},{25,17},{2,10},{10... | collective-permute-start | bytes 393224 | tf_op jit(solution)/shard_map/ppermute | solution.py:562
  75.5 2.3 %collective-permute-start.23 = (bf16[256,256]{1,0:T(8,128)(2,1)S(1)}, bf16[256,256]{1,0:T(8,128)(2,1)S(1)}, u32[]{:S(2)}, u32[]{:S(2)}) collective-permute-start(bf16[256,256]{1,0:T(8,128)(2,1)S(1)} %get-tuple-element.58.refs_1_), channel_id=1, source_target_pairs={{0,24},{8,16},{16,8},{24,0},{1,25},{9,17},{17,9},{25,1},{2,26},{10... | collective-permute-start | bytes 393224 | tf_op jit(solution)/shard_map/ppermute | solution.py:562
  78.4 0.9 finish.3
  79.3 2.4 %collective-permute-start.38 = (bf16[32,2048]{1,0:T(8,128)(2,1)S(1)}, bf16[32,2048]{1,0:T(8,128)(2,1)S(1)}, u32[]{:S(2)}, u32[]{:S(2)}) collective-permute-start(bf16[32,2048]{1,0:T(8,128)(2,1)S(1)} %get-tuple-element.88.refs_0_), channel_id=1, source_target_pairs={{0,8},{8,0},{16,24},{24,16},{1,9},{9,1},{17,25},{25,17},{2,10},{10... | collective-permute-start | bytes 393224 | tf_op jit(solution)/shard_map/ppermute | solution.py:562
  81.7 2.4 %collective-permute-start.40 = (bf16[32,2048]{1,0:T(8,128)(2,1)S(1)}, bf16[32,2048]{1,0:T(8,128)(2,1)S(1)}, u32[]{:S(2)}, u32[]{:S(2)}) collective-permute-start(bf16[32,2048]{1,0:T(8,128)(2,1)S(1)} %get-tuple-element.88.refs_0_), channel_id=1, source_target_pairs={{0,24},{8,16},{16,8},{24,0},{1,25},{9,17},{17,9},{25,1},{2,26},{10... | collective-permute-start | bytes 393224 | tf_op jit(solution)/shard_map/ppermute | solution.py:562
  84.1 4.3 %collective-permute-done.22.refs_2_ = bf16[256,256]{1,0:T(8,128)(2,1)S(1)} collective-permute-done((bf16[256,256]{1,0:T(8,128)(2,1)S(1)}, bf16[256,256]{1,0:T(8,128)(2,1)S(1)}, u32[]{:S(2)}, u32[]{:S(2)}) %collective-permute-start.22) | collective-permute-done | bytes 131104 | tf_op jit(solution)/shard_map/ppermute | solution.py:562
  88.4 3.8 %away_parts.1 = (bf16[272,256]{1,0:T(8,128)(2,1)S(1)}, bf16[272,256]{1,0:T(8,128)(2,1)S(1)}, bf16[272,256]{1,0:T(8,128)(2,1)S(1)}) custom-call(s32[6]{0:T(128)S(1)} %pad_add_fusion.place.refs_0_, bf16[256,256]{1,0:T(8,128)(2,1)S(1)} %collective-permute-done.21.refs_1_, bf16[256,256]{1,0:T(8,128)(2,1)S(1)} %collective-permute-done.22.refs_2_, ...), custom_call_target="tpu_custom_call" | custom-call | flops 268435456 | bytes 1048576 | tf_op jit(solution)/shard_map/away_parts/pallas_call | solution.py:37
  92.2 6.4 %collective-permute-done.39.refs_2_ = bf16[32,2048]{1,0:T(8,128)(2,1)S(1)} collective-permute-done((bf16[32,2048]{1,0:T(8,128)(2,1)S(1)}, bf16[32,2048]{1,0:T(8,128)(2,1)S(1)}, u32[]{:S(2)}, u32[]{:S(2)}) %collective-permute-start.39) | collective-permute-done | bytes 131104 | tf_op jit(solution)/shard_map/ppermute | solution.py:562
  99.0 1.4 collective-permute-start.43
  100.4 2.1 %collective-permute-start.27 = (bf16[272,256]{1,0:T(8,128)(2,1)S(1)}, bf16[272,256]{1,0:T(8,128)(2,1)S(1)}, u32[]{:S(2)}, u32[]{:S(2)}) collective-permute-start(bf16[272,256]{1,0:T(8,128)(2,1)S(1)} %get-tuple-element.71.refs_4_), channel_id=1, source_target_pairs={{0,8},{8,0},{16,24},{24,16},{1,9},{9,1},{17,25},{25,17},{2,10},{10... | collective-permute-start | bytes 417800 | tf_op jit(solution)/shard_map/ppermute | solution.py:562
  103.0 1.8 %collective-permute-start.29 = (bf16[272,256]{1,0:T(8,128)(2,1)S(1)}, bf16[272,256]{1,0:T(8,128)(2,1)S(1)}, u32[]{:S(2)}, u32[]{:S(2)}) collective-permute-start(bf16[272,256]{1,0:T(8,128)(2,1)S(1)} %get-tuple-element.73), channel_id=1, source_target_pairs={{0,24},{8,16},{16,8},{24,0},{1,25},{9,17},{17,9},{25,1},{2,26},{10... | collective-permute-start | bytes 417800 | tf_op jit(solution)/shard_map/ppermute | solution.py:562
  104.9 4.4 %largest_logits.4.refs_2_.refs_0_ = f32[8,256]{1,0:T(8,128)S(1)} custom-call(s32[6]{0:T(128)S(1)} %pad_add_fusion.place.refs_0_, bf16[128,2048]{1,0:T(8,128)(2,1)S(1)} %stack.10.refs_1_, bf16[128,2048]{1,0:T(8,128)(2,1)S(1)} %collective-permute-done.41.refs_2_, bf16[3136,2048]{1,0:T(8,128)(2,1)S(1)} %bitcast.14), custom_call_target="tpu_custom_call" | custom-call | flops 3288334336 | bytes 12845056 | tf_op jit(solution)/shard_map/largest_logits/pallas_call | solution.py:37
  109.3 6.6 %collective-permute-done.28.refs_4_ = bf16[272,256]{1,0:T(8,128)(2,1)S(1)} collective-permute-done((bf16[272,256]{1,0:T(8,128)(2,1)S(1)}, bf16[272,256]{1,0:T(8,128)(2,1)S(1)}, u32[]{:S(2)}, u32[]{:S(2)}) %collective-permute-start.28) | collective-permute-done | bytes 139296 | tf_op jit(solution)/shard_map/ppermute | solution.py:562
  116.6 1.4 collective-permute-start.46
  118.0 1.0 collective-permute-start.47
  119.0 4.4 %largest_logits.5.refs_4_.refs_1_ = f32[8,256]{1,0:T(8,128)S(1)} custom-call(s32[6]{0:T(128)S(1)} %pad_add_fusion.place.refs_0_, bf16[128,2048]{1,0:T(8,128)(2,1)S(1)} %get-tuple-element.89.refs_1_, bf16[128,2048]{1,0:T(8,128)(2,1)S(1)} %collective-permute-done.44.refs_2_, bf16[3136,2048]{1,0:T(8,128)(2,1)S(1)} %bitcast.14), custom_call_target="tpu_custom_call" | custom-call | flops 3288334336 | bytes 12845056 | tf_op jit(solution)/shard_map/largest_logits/pallas_call | solution.py:37
  123.4 4.4 %largest_logits.6.refs_2_ = f32[8,256]{1,0:T(8,128)S(1)} custom-call(s32[6]{0:T(128)S(1)} %pad_add_fusion.place.refs_0_, bf16[128,2048]{1,0:T(8,128)(2,1)S(1)} %get-tuple-element.90.refs_1_, bf16[128,2048]{1,0:T(8,128)(2,1)S(1)} %collective-permute-done.45.refs_2_, bf16[3136,2048]{1,0:T(8,128)(2,1)S(1)} %bitcast.14, f32[8,256]{1,0:T(8,128)S(1)} %largest_logits.5.refs_4_.refs_1_), custom_call_target="tpu_custom_call" | custom-call | flops 3288334336 | bytes 12845056 | tf_op jit(solution)/shard_map/largest_logits/pallas_call | solution.py:37
  128.0 1.9 %collective-permute-done.48.refs_2_ = bf16[128,2048]{1,0:T(8,128)(2,1)S(1)} collective-permute-done((bf16[128,2048]{1,0:T(8,128)(2,1)S(1)}, bf16[128,2048]{1,0:T(8,128)(2,1)S(1)}, u32[]{:S(2)}, u32[]{:S(2)}) %collective-permute-start.48) | collective-permute-done | bytes 524320 | tf_op jit(solution)/shard_map/ppermute | solution.py:559
  129.9 4.4 %largest_logits.7.refs_3_ = f32[8,256]{1,0:T(8,128)S(1)} custom-call(s32[6]{0:T(128)S(1)} %pad_add_fusion.place.refs_0_, bf16[128,2048]{1,0:T(8,128)(2,1)S(1)} %stack.11.refs_1_, bf16[128,2048]{1,0:T(8,128)(2,1)S(1)} %collective-permute-done.48.refs_2_, bf16[3136,2048]{1,0:T(8,128)(2,1)S(1)} %bitcast.14), custom_call_target="tpu_custom_call" | custom-call | flops 3288334336 | bytes 12845056 | tf_op jit(solution)/shard_map/largest_logits/pallas_call | solution.py:37
  135.1 1.0 collective-permute-done.49
  136.6 3.2 %collective-permute-done.50 = f32[8,256]{1,0:T(8,128)S(1)} collective-permute-done((f32[8,256]{1,0:T(8,128)S(1)}, f32[8,256]{1,0:T(8,128)S(1)}, u32[]{:S(2)}, u32[]{:S(2)}) %collective-permute-start.50) | collective-permute-done | bytes 8224 | tf_op jit(solution)/shard_map/ppermute | solution.py:636
  139.9 1.0 collective-permute-start.51
  140.9 1.0 combine.3
  142.1 1.5 collective-permute-done.51
  143.7 2.5 %collective-permute-start.52 = (f32[8,256]{1,0:T(8,128)S(1)}, f32[8,256]{1,0:T(8,128)S(1)}, u32[]{:S(2)}, u32[]{:S(2)}) collective-permute-start(f32[8,256]{1,0:T(8,128)S(1)} %add_select_fusion.2), channel_id=1, source_target_pairs={{0,8},{8,0},{16,24},{24,16},{1,9},{9,1},{17,25},{25,17},{2,10},{10... | collective-permute-start | bytes 24584 | tf_op jit(solution)/shard_map/ppermute | solution.py:636
  147.0 1.0 collective-permute-start.32
  148.1 2.1 %collective-permute-start.33 = (bf16[32,2048]{1,0:T(8,128)(2,1)S(1)}, bf16[32,2048]{1,0:T(8,128)(2,1)S(1)}, u32[]{:S(2)}, u32[]{:S(2)}) collective-permute-start(bf16[32,2048]{1,0:T(8,128)(2,1)S(1)} %get-tuple-element.79), channel_id=1, source_target_pairs={{0,6},{1,7},{2,4},{3,5},{4,2},{5,3},{6,0},{7,1},{8,14},{9,15},{10,... | collective-permute-start | bytes 393224 | tf_op jit(solution)/shard_map/ppermute | solution.py:559
  150.2 1.9 %collective-permute-done.31.refs_1_ = bf16[32,2048]{1,0:T(8,128)(2,1)S(1)} collective-permute-done((bf16[32,2048]{1,0:T(8,128)(2,1)S(1)}, bf16[32,2048]{1,0:T(8,128)(2,1)S(1)}, u32[]{:S(2)}, u32[]{:S(2)}) %collective-permute-start.31) | collective-permute-done | bytes 131104 | tf_op jit(solution)/shard_map/ppermute | solution.py:559
  152.6 1.4 collective-permute-done.33.refs_3_
  154.0 0.9 finish.2
  (113 shorter events, 11.6 us)
Async XLA Ops:
  0.6 68.0 %copy-start = (bf16[256,2048]{1,0:T(8,128)(2,1)S(1)}, bf16[256,2048]{1,0:T(8,128)(2,1)}, u32[]{:S(2)}) copy-start(bf16[256,2048]{1,0:T(8,128)(2,1)} %w_keep.3) | copy-start | bytes 3145732
  0.6 77.8 %copy-start.7 = (f32[2048]{0:T(1024)S(1)}, f32[2048]{0:T(1024)}, u32[]{:S(2)}) copy-start(f32[2048]{0:T(1024)} %param.24) | copy-start | bytes 24580
  0.7 77.8 %copy-start.8 = (f32[2048]{0:T(1024)S(1)}, f32[2048]{0:T(1024)}, u32[]{:S(2)}) copy-start(f32[2048]{0:T(1024)} %param.25) | copy-start | bytes 24580
  0.7 22.5 %collective-permute-start.7 = (bf16[256,2048]{1,0:T(8,128)(2,1)}, bf16[256,2048]{1,0:T(8,128)(2,1)S(1)}, u32[]{:S(2)}, u32[]{:S(2)}) collective-permute-start(bf16[256,2048]{1,0:T(8,128)(2,1)} %w_keep.3), channel_id=1, source_target_pairs={{0,1},{1,0},{2,3},{3,2},{4,5},{5,4},{6,7},{7,6},{8,9},{9,8},{10,11... | collective-permute-start | bytes 3145736 | tf_op jit(solution)/shard_map/ppermute | solution.py:559
  1.2 16.0 %collective-permute-start = (bf16[256,256]{1,0:T(8,128)(2,1)}, bf16[256,256]{1,0:T(8,128)(2,1)S(1)}, u32[]{:S(2)}, u32[]{:S(2)}) collective-permute-start(bf16[256,256]{1,0:T(8,128)(2,1)} %refs_1_.2), channel_id=1, source_target_pairs={{0,2},{1,3},{2,0},{3,1},{4,6},{5,7},{6,4},{7,5},{8,10},{9,11},{10,... | collective-permute-start | bytes 393224 | tf_op jit(solution)/shard_map/ppermute | solution.py:559
  3.7 14.0 %collective-permute-start.1 = (bf16[256,256]{1,0:T(8,128)(2,1)}, bf16[256,256]{1,0:T(8,128)(2,1)S(1)}, u32[]{:S(2)}, u32[]{:S(2)}) collective-permute-start(bf16[256,256]{1,0:T(8,128)(2,1)} %refs_1_.2), channel_id=1, source_target_pairs={{0,4},{1,5},{2,6},{3,7},{4,0},{5,1},{6,2},{7,3},{8,12},{9,13},{10,... | collective-permute-start | bytes 393224 | tf_op jit(solution)/shard_map/ppermute | solution.py:559
  5.3 12.5 %collective-permute-start.2 = (bf16[256,256]{1,0:T(8,128)(2,1)}, bf16[256,256]{1,0:T(8,128)(2,1)S(1)}, u32[]{:S(2)}, u32[]{:S(2)}) collective-permute-start(bf16[256,256]{1,0:T(8,128)(2,1)} %refs_1_.2), channel_id=1, source_target_pairs={{0,6},{1,7},{2,4},{3,5},{4,2},{5,3},{6,0},{7,1},{8,14},{9,15},{10,... | collective-permute-start | bytes 393224 | tf_op jit(solution)/shard_map/ppermute | solution.py:559
  5.3 13.0 %collective-permute-start.3 = (bf16[256,256]{1,0:T(8,128)(2,1)}, bf16[256,256]{1,0:T(8,128)(2,1)S(1)}, u32[]{:S(2)}, u32[]{:S(2)}) collective-permute-start(bf16[256,256]{1,0:T(8,128)(2,1)} %refs_1_.2), channel_id=1, source_target_pairs={{0,1},{1,0},{2,3},{3,2},{4,5},{5,4},{6,7},{7,6},{8,9},{9,8},{10,11... | collective-permute-start | bytes 393224 | tf_op jit(solution)/shard_map/ppermute | solution.py:559
  7.3 97.6 %slice-start = ((s8[12845056]{0:T(1024)(128)(4,1)}), s8[262144]{0:T(1024)(128)(4,1)S(1)}, s32[]{:S(2)}) async-start(s8[12845056]{0:T(1024)(128)(4,1)} %bitcast.13), calls=%async_computation | async-start | bytes 524288
  17.1 3.2 %collective-permute-start.4 = (bf16[256,256]{1,0:T(8,128)(2,1)S(1)}, bf16[256,256]{1,0:T(8,128)(2,1)S(1)}, u32[]{:S(2)}, u32[]{:S(2)}) collective-permute-start(bf16[256,256]{1,0:T(8,128)(2,1)S(1)} %collective-permute-done.refs_2_), channel_id=1, source_target_pairs={{0,1},{1,0},{2,3},{3,2},{4,5},{5,4},{6,7},{7,6},{8,9},{9,8},{10,11... | collective-permute-start | bytes 393224 | tf_op jit(solution)/shard_map/ppermute | solution.py:559
  17.7 5.3 %collective-permute-start.5 = (bf16[256,256]{1,0:T(8,128)(2,1)S(1)}, bf16[256,256]{1,0:T(8,128)(2,1)S(1)}, u32[]{:S(2)}, u32[]{:S(2)}) collective-permute-start(bf16[256,256]{1,0:T(8,128)(2,1)S(1)} %collective-permute-done.1.refs_3_), channel_id=1, source_target_pairs={{0,1},{1,0},{2,3},{3,2},{4,5},{5,4},{6,7},{7,6},{8,9},{9,8},{10,11... | collective-permute-start | bytes 393224 | tf_op jit(solution)/shard_map/ppermute | solution.py:559
  17.8 5.3 %collective-permute-start.6 = (bf16[256,256]{1,0:T(8,128)(2,1)S(1)}, bf16[256,256]{1,0:T(8,128)(2,1)S(1)}, u32[]{:S(2)}, u32[]{:S(2)}) collective-permute-start(bf16[256,256]{1,0:T(8,128)(2,1)S(1)} %collective-permute-done.2.refs_4_), channel_id=1, source_target_pairs={{0,1},{1,0},{2,3},{3,2},{4,5},{5,4},{6,7},{7,6},{8,9},{9,8},{10,11... | collective-permute-start | bytes 393224 | tf_op jit(solution)/shard_map/ppermute | solution.py:559
  18.3 17.9 %collective-permute-start.11 = (bf16[256,256]{1,0:T(8,128)(2,1)S(1)}, bf16[256,256]{1,0:T(8,128)(2,1)S(1)}, u32[]{:S(2)}, u32[]{:S(2)}) collective-permute-start(bf16[256,256]{1,0:T(8,128)(2,1)S(1)} %get-tuple-element.96.refs_13_), channel_id=1, source_target_pairs={{0,8},{8,0},{16,24},{24,16},{1,9},{9,1},{17,25},{25,17},{2,10},{10... | collective-permute-start | bytes 393224 | tf_op jit(solution)/shard_map/ppermute | solution.py:562
  20.4 15.8 %collective-permute-start.12 = (bf16[256,256]{1,0:T(8,128)(2,1)S(1)}, bf16[256,256]{1,0:T(8,128)(2,1)S(1)}, u32[]{:S(2)}, u32[]{:S(2)}) collective-permute-start(bf16[256,256]{1,0:T(8,128)(2,1)S(1)} %get-tuple-element.94), channel_id=1, source_target_pairs={{0,16},{8,24},{16,0},{24,8},{1,17},{9,25},{17,1},{25,9},{2,18},{10... | collective-permute-start | bytes 393224 | tf_op jit(solution)/shard_map/ppermute | solution.py:562
  23.0 81.9 %slice-start.1 = ((s8[12845056]{0:T(1024)(128)(4,1)}), s8[4194304]{0:T(1024)(128)(4,1)S(1)}, s32[]{:S(2)}) async-start(s8[12845056]{0:T(1024)(128)(4,1)} %bitcast.13), calls=%async_computation.1 | async-start | bytes 8388608
  23.0 13.2 %collective-permute-start.13 = (bf16[256,256]{1,0:T(8,128)(2,1)S(1)}, bf16[256,256]{1,0:T(8,128)(2,1)S(1)}, u32[]{:S(2)}, u32[]{:S(2)}) collective-permute-start(bf16[256,256]{1,0:T(8,128)(2,1)S(1)} %get-tuple-element.93), channel_id=1, source_target_pairs={{0,24},{8,16},{16,8},{24,0},{1,25},{9,17},{17,9},{25,1},{2,26},{10... | collective-permute-start | bytes 393224 | tf_op jit(solution)/shard_map/ppermute | solution.py:562
  23.1 1.4 copy-start.1
  24.5 1.3 copy-start.2
  25.8 1.2 copy-start.3
  29.7 6.5 %collective-permute-start.8 = (bf16[256,256]{1,0:T(8,128)(2,1)S(1)}, bf16[256,256]{1,0:T(8,128)(2,1)S(1)}, u32[]{:S(2)}, u32[]{:S(2)}) collective-permute-start(bf16[256,256]{1,0:T(8,128)(2,1)S(1)} %get-tuple-element.49.refs_1_), channel_id=1, source_target_pairs={{0,8},{8,0},{16,24},{24,16},{1,9},{9,1},{17,25},{25,17},{2,10},{10... | collective-permute-start | bytes 393224 | tf_op jit(solution)/shard_map/ppermute | solution.py:562
  33.4 7.8 %collective-permute-start.10 = (bf16[256,256]{1,0:T(8,128)(2,1)S(1)}, bf16[256,256]{1,0:T(8,128)(2,1)S(1)}, u32[]{:S(2)}, u32[]{:S(2)}) collective-permute-start(bf16[256,256]{1,0:T(8,128)(2,1)S(1)} %get-tuple-element.49.refs_1_), channel_id=1, source_target_pairs={{0,24},{8,16},{16,8},{24,0},{1,25},{9,17},{17,9},{25,1},{2,26},{10... | collective-permute-start | bytes 393224 | tf_op jit(solution)/shard_map/ppermute | solution.py:562
  36.9 6.1 %collective-permute-start.14 = (bf16[256,256]{1,0:T(8,128)(2,1)S(1)}, bf16[256,256]{1,0:T(8,128)(2,1)S(1)}, u32[]{:S(2)}, u32[]{:S(2)}) collective-permute-start(bf16[256,256]{1,0:T(8,128)(2,1)S(1)} %choose.1.refs_6_), channel_id=1, source_target_pairs={{0,2},{1,3},{2,0},{3,1},{4,6},{5,7},{6,4},{7,5},{8,10},{9,11},{10,... | collective-permute-start | bytes 393224 | tf_op jit(solution)/shard_map/ppermute | solution.py:559
  38.5 7.7 %collective-permute-start.15 = (bf16[256,256]{1,0:T(8,128)(2,1)S(1)}, bf16[256,256]{1,0:T(8,128)(2,1)S(1)}, u32[]{:S(2)}, u32[]{:S(2)}) collective-permute-start(bf16[256,256]{1,0:T(8,128)(2,1)S(1)} %choose.1.refs_6_), channel_id=1, source_target_pairs={{0,4},{1,5},{2,6},{3,7},{4,0},{5,1},{6,2},{7,3},{8,12},{9,13},{10,... | collective-permute-start | bytes 393224 | tf_op jit(solution)/shard_map/ppermute | solution.py:559
  40.0 6.1 %collective-permute-start.16 = (bf16[256,256]{1,0:T(8,128)(2,1)S(1)}, bf16[256,256]{1,0:T(8,128)(2,1)S(1)}, u32[]{:S(2)}, u32[]{:S(2)}) collective-permute-start(bf16[256,256]{1,0:T(8,128)(2,1)S(1)} %choose.1.refs_6_), channel_id=1, source_target_pairs={{0,6},{1,7},{2,4},{3,5},{4,2},{5,3},{6,0},{7,1},{8,14},{9,15},{10,... | collective-permute-start | bytes 393224 | tf_op jit(solution)/shard_map/ppermute | solution.py:559
  40.5 7.3 %collective-permute-start.9 = (bf16[256,256]{1,0:T(8,128)(2,1)S(1)}, bf16[256,256]{1,0:T(8,128)(2,1)S(1)}, u32[]{:S(2)}, u32[]{:S(2)}) collective-permute-start(bf16[256,256]{1,0:T(8,128)(2,1)S(1)} %get-tuple-element.49.refs_1_), channel_id=1, source_target_pairs={{0,16},{8,24},{16,0},{24,8},{1,17},{9,25},{17,1},{25,9},{2,18},{10... | collective-permute-start | bytes 393224 | tf_op jit(solution)/shard_map/ppermute | solution.py:562
  41.2 6.5 %collective-permute-start.17 = (bf16[256,256]{1,0:T(8,128)(2,1)S(1)}, bf16[256,256]{1,0:T(8,128)(2,1)S(1)}, u32[]{:S(2)}, u32[]{:S(2)}) collective-permute-start(bf16[256,256]{1,0:T(8,128)(2,1)S(1)} %choose.1.refs_6_), channel_id=1, source_target_pairs={{0,1},{1,0},{2,3},{3,2},{4,5},{5,4},{6,7},{7,6},{8,9},{9,8},{10,11... | collective-permute-start | bytes 393224 | tf_op jit(solution)/shard_map/ppermute | solution.py:559
  43.0 4.7 %collective-permute-start.18 = (bf16[256,256]{1,0:T(8,128)(2,1)S(1)}, bf16[256,256]{1,0:T(8,128)(2,1)S(1)}, u32[]{:S(2)}, u32[]{:S(2)}) collective-permute-start(bf16[256,256]{1,0:T(8,128)(2,1)S(1)} %collective-permute-done.14.refs_7_), channel_id=1, source_target_pairs={{0,1},{1,0},{2,3},{3,2},{4,5},{5,4},{6,7},{7,6},{8,9},{9,8},{10,11... | collective-permute-start | bytes 393224 | tf_op jit(solution)/shard_map/ppermute | solution.py:559
  46.1 1.6 %collective-permute-start.19 = (bf16[256,256]{1,0:T(8,128)(2,1)S(1)}, bf16[256,256]{1,0:T(8,128)(2,1)S(1)}, u32[]{:S(2)}, u32[]{:S(2)}) collective-permute-start(bf16[256,256]{1,0:T(8,128)(2,1)S(1)} %collective-permute-done.15.refs_8_), channel_id=1, source_target_pairs={{0,1},{1,0},{2,3},{3,2},{4,5},{5,4},{6,7},{7,6},{8,9},{9,8},{10,11... | collective-permute-start | bytes 393224 | tf_op jit(solution)/shard_map/ppermute | solution.py:559
  46.1 1.6 %collective-permute-start.20 = (bf16[256,256]{1,0:T(8,128)(2,1)S(1)}, bf16[256,256]{1,0:T(8,128)(2,1)S(1)}, u32[]{:S(2)}, u32[]{:S(2)}) collective-permute-start(bf16[256,256]{1,0:T(8,128)(2,1)S(1)} %collective-permute-done.16.refs_9_), channel_id=1, source_target_pairs={{0,1},{1,0},{2,3},{3,2},{4,5},{5,4},{6,7},{7,6},{8,9},{9,8},{10,11... | collective-permute-start | bytes 393224 | tf_op jit(solution)/shard_map/ppermute | solution.py:559
  47.8 57.1 %slice-start.2 = ((s8[12845056]{0:T(1024)(128)(4,1)}), s8[4194304]{0:T(1024)(128)(4,1)S(1)}, s32[]{:S(2)}) async-start(s8[12845056]{0:T(1024)(128)(4,1)} %bitcast.13), calls=%async_computation.2 | async-start | bytes 8388608
  52.7 8.7 %collective-permute-start.24 = (bf16[272,256]{1,0:T(8,128)(2,1)S(1)}, bf16[272,256]{1,0:T(8,128)(2,1)S(1)}, u32[]{:S(2)}, u32[]{:S(2)}) collective-permute-start(bf16[272,256]{1,0:T(8,128)(2,1)S(1)} %get-tuple-element.67), channel_id=1, source_target_pairs={{0,8},{8,0},{16,24},{24,16},{1,9},{9,1},{17,25},{25,17},{2,10},{10... | collective-permute-start | bytes 417800 | tf_op jit(solution)/shard_map/ppermute | solution.py:562
  52.7 13.5 %collective-permute-start.25 = (bf16[272,256]{1,0:T(8,128)(2,1)S(1)}, bf16[272,256]{1,0:T(8,128)(2,1)S(1)}, u32[]{:S(2)}, u32[]{:S(2)}) collective-permute-start(bf16[272,256]{1,0:T(8,128)(2,1)S(1)} %get-tuple-element.68), channel_id=1, source_target_pairs={{0,16},{8,24},{16,0},{24,8},{1,17},{9,25},{17,1},{25,9},{2,18},{10... | collective-permute-start | bytes 417800 | tf_op jit(solution)/shard_map/ppermute | solution.py:562
  54.2 12.0 %collective-permute-start.26 = (bf16[272,256]{1,0:T(8,128)(2,1)S(1)}, bf16[272,256]{1,0:T(8,128)(2,1)S(1)}, u32[]{:S(2)}, u32[]{:S(2)}) collective-permute-start(bf16[272,256]{1,0:T(8,128)(2,1)S(1)} %get-tuple-element.69), channel_id=1, source_target_pairs={{0,24},{8,16},{16,8},{24,0},{1,25},{9,17},{17,9},{25,1},{2,26},{10... | collective-permute-start | bytes 417800 | tf_op jit(solution)/shard_map/ppermute | solution.py:562
  59.1 45.7 %slice-start.3 = ((s8[12845056]{0:T(1024)(128)(4,1)}), s8[4194304]{0:T(1024)(128)(4,1)S(1)}, s32[]{:S(2)}) async-start(s8[12845056]{0:T(1024)(128)(4,1)} %bitcast.13), calls=%async_computation.3 | async-start | bytes 8388608
  67.3 1.3 collective-permute-start.34
  69.1 6.4 %collective-permute-start.35 = (bf16[32,2048]{1,0:T(8,128)(2,1)S(1)}, bf16[32,2048]{1,0:T(8,128)(2,1)S(1)}, u32[]{:S(2)}, u32[]{:S(2)}) collective-permute-start(bf16[32,2048]{1,0:T(8,128)(2,1)S(1)} %get-tuple-element.83), channel_id=1, source_target_pairs={{0,2},{1,3},{2,0},{3,1},{4,6},{5,7},{6,4},{7,5},{8,10},{9,11},{10,... | collective-permute-start | bytes 393224 | tf_op jit(solution)/shard_map/ppermute | solution.py:559
  70.0 7.8 %collective-permute-start.36 = (bf16[32,2048]{1,0:T(8,128)(2,1)S(1)}, bf16[32,2048]{1,0:T(8,128)(2,1)S(1)}, u32[]{:S(2)}, u32[]{:S(2)}) collective-permute-start(bf16[32,2048]{1,0:T(8,128)(2,1)S(1)} %get-tuple-element.84), channel_id=1, source_target_pairs={{0,4},{1,5},{2,6},{3,7},{4,0},{5,1},{6,2},{7,3},{8,12},{9,13},{10,... | collective-permute-start | bytes 393224 | tf_op jit(solution)/shard_map/ppermute | solution.py:559
  71.2 7.2 %collective-permute-start.37 = (bf16[32,2048]{1,0:T(8,128)(2,1)S(1)}, bf16[32,2048]{1,0:T(8,128)(2,1)S(1)}, u32[]{:S(2)}, u32[]{:S(2)}) collective-permute-start(bf16[32,2048]{1,0:T(8,128)(2,1)S(1)} %get-tuple-element.85), channel_id=1, source_target_pairs={{0,6},{1,7},{2,4},{3,5},{4,2},{5,3},{6,0},{7,1},{8,14},{9,15},{10,... | collective-permute-start | bytes 393224 | tf_op jit(solution)/shard_map/ppermute | solution.py:559
  72.6 9.1 %collective-permute-start.21 = (bf16[256,256]{1,0:T(8,128)(2,1)S(1)}, bf16[256,256]{1,0:T(8,128)(2,1)S(1)}, u32[]{:S(2)}, u32[]{:S(2)}) collective-permute-start(bf16[256,256]{1,0:T(8,128)(2,1)S(1)} %get-tuple-element.58.refs_1_), channel_id=1, source_target_pairs={{0,8},{8,0},{16,24},{24,16},{1,9},{9,1},{17,25},{25,17},{2,10},{10... | collective-permute-start | bytes 393224 | tf_op jit(solution)/shard_map/ppermute | solution.py:562
  75.4 13.0 %collective-permute-start.22 = (bf16[256,256]{1,0:T(8,128)(2,1)S(1)}, bf16[256,256]{1,0:T(8,128)(2,1)S(1)}, u32[]{:S(2)}, u32[]{:S(2)}) collective-permute-start(bf16[256,256]{1,0:T(8,128)(2,1)S(1)} %get-tuple-element.58.refs_1_), channel_id=1, source_target_pairs={{0,16},{8,24},{16,0},{24,8},{1,17},{9,25},{17,1},{25,9},{2,18},{10... | collective-permute-start | bytes 393224 | tf_op jit(solution)/shard_map/ppermute | solution.py:562
  75.5 12.9 %collective-permute-start.23 = (bf16[256,256]{1,0:T(8,128)(2,1)S(1)}, bf16[256,256]{1,0:T(8,128)(2,1)S(1)}, u32[]{:S(2)}, u32[]{:S(2)}) collective-permute-start(bf16[256,256]{1,0:T(8,128)(2,1)S(1)} %get-tuple-element.58.refs_1_), channel_id=1, source_target_pairs={{0,24},{8,16},{16,8},{24,0},{1,25},{9,17},{17,9},{25,1},{2,26},{10... | collective-permute-start | bytes 393224 | tf_op jit(solution)/shard_map/ppermute | solution.py:562
  79.3 12.9 %collective-permute-start.38 = (bf16[32,2048]{1,0:T(8,128)(2,1)S(1)}, bf16[32,2048]{1,0:T(8,128)(2,1)S(1)}, u32[]{:S(2)}, u32[]{:S(2)}) collective-permute-start(bf16[32,2048]{1,0:T(8,128)(2,1)S(1)} %get-tuple-element.88.refs_0_), channel_id=1, source_target_pairs={{0,8},{8,0},{16,24},{24,16},{1,9},{9,1},{17,25},{25,17},{2,10},{10... | collective-permute-start | bytes 393224 | tf_op jit(solution)/shard_map/ppermute | solution.py:562
  81.7 16.8 %collective-permute-start.39 = (bf16[32,2048]{1,0:T(8,128)(2,1)S(1)}, bf16[32,2048]{1,0:T(8,128)(2,1)S(1)}, u32[]{:S(2)}, u32[]{:S(2)}) collective-permute-start(bf16[32,2048]{1,0:T(8,128)(2,1)S(1)} %get-tuple-element.88.refs_0_), channel_id=1, source_target_pairs={{0,16},{8,24},{16,0},{24,8},{1,17},{9,25},{17,1},{25,9},{2,18},{10... | collective-permute-start | bytes 393224 | tf_op jit(solution)/shard_map/ppermute | solution.py:562
  81.7 16.8 %collective-permute-start.40 = (bf16[32,2048]{1,0:T(8,128)(2,1)S(1)}, bf16[32,2048]{1,0:T(8,128)(2,1)S(1)}, u32[]{:S(2)}, u32[]{:S(2)}) collective-permute-start(bf16[32,2048]{1,0:T(8,128)(2,1)S(1)} %get-tuple-element.88.refs_0_), channel_id=1, source_target_pairs={{0,24},{8,16},{16,8},{24,0},{1,25},{9,17},{17,9},{25,1},{2,26},{10... | collective-permute-start | bytes 393224 | tf_op jit(solution)/shard_map/ppermute | solution.py:562
  98.6 4.5 %collective-permute-start.41 = (bf16[128,2048]{1,0:T(8,128)(2,1)S(1)}, bf16[128,2048]{1,0:T(8,128)(2,1)S(1)}, u32[]{:S(2)}, u32[]{:S(2)}) collective-permute-start(bf16[128,2048]{1,0:T(8,128)(2,1)S(1)} %stack.10.refs_1_), channel_id=1, source_target_pairs={{0,1},{1,0},{2,3},{3,2},{4,5},{5,4},{6,7},{7,6},{8,9},{9,8},{10,11... | collective-permute-start | bytes 1572872 | tf_op jit(solution)/shard_map/ppermute | solution.py:559
  98.7 17.3 %collective-permute-start.42 = (bf16[128,2048]{1,0:T(8,128)(2,1)S(1)}, bf16[128,2048]{1,0:T(8,128)(2,1)S(1)}, u32[]{:S(2)}, u32[]{:S(2)}) collective-permute-start(bf16[128,2048]{1,0:T(8,128)(2,1)S(1)} %stack.10.refs_1_), channel_id=1, source_target_pairs={{0,2},{1,3},{2,0},{3,1},{4,6},{5,7},{6,4},{7,5},{8,10},{9,11},{10,... | collective-permute-start | bytes 1572872 | tf_op jit(solution)/shard_map/ppermute | solution.py:559
  99.0 16.9 %collective-permute-start.43 = (bf16[128,2048]{1,0:T(8,128)(2,1)S(1)}, bf16[128,2048]{1,0:T(8,128)(2,1)S(1)}, u32[]{:S(2)}, u32[]{:S(2)}) collective-permute-start(bf16[128,2048]{1,0:T(8,128)(2,1)S(1)} %stack.10.refs_1_), channel_id=1, source_target_pairs={{0,4},{1,5},{2,6},{3,7},{4,0},{5,1},{6,2},{7,3},{8,12},{9,13},{10,... | collective-permute-start | bytes 1572872 | tf_op jit(solution)/shard_map/ppermute | solution.py:559
  100.4 8.9 %collective-permute-start.27 = (bf16[272,256]{1,0:T(8,128)(2,1)S(1)}, bf16[272,256]{1,0:T(8,128)(2,1)S(1)}, u32[]{:S(2)}, u32[]{:S(2)}) collective-permute-start(bf16[272,256]{1,0:T(8,128)(2,1)S(1)} %get-tuple-element.71.refs_4_), channel_id=1, source_target_pairs={{0,8},{8,0},{16,24},{24,16},{1,9},{9,1},{17,25},{25,17},{2,10},{10... | collective-permute-start | bytes 417800 | tf_op jit(solution)/shard_map/ppermute | solution.py:562
  102.5 13.4 %collective-permute-start.28 = (bf16[272,256]{1,0:T(8,128)(2,1)S(1)}, bf16[272,256]{1,0:T(8,128)(2,1)S(1)}, u32[]{:S(2)}, u32[]{:S(2)}) collective-permute-start(bf16[272,256]{1,0:T(8,128)(2,1)S(1)} %get-tuple-element.72), channel_id=1, source_target_pairs={{0,16},{8,24},{16,0},{24,8},{1,17},{9,25},{17,1},{25,9},{2,18},{10... | collective-permute-start | bytes 417800 | tf_op jit(solution)/shard_map/ppermute | solution.py:562
  103.0 12.9 %collective-permute-start.29 = (bf16[272,256]{1,0:T(8,128)(2,1)S(1)}, bf16[272,256]{1,0:T(8,128)(2,1)S(1)}, u32[]{:S(2)}, u32[]{:S(2)}) collective-permute-start(bf16[272,256]{1,0:T(8,128)(2,1)S(1)} %get-tuple-element.73), channel_id=1, source_target_pairs={{0,24},{8,16},{16,8},{24,0},{1,25},{9,17},{17,9},{25,1},{2,26},{10... | collective-permute-start | bytes 417800 | tf_op jit(solution)/shard_map/ppermute | solution.py:562
  116.0 3.0 %collective-permute-start.44 = (bf16[128,2048]{1,0:T(8,128)(2,1)S(1)}, bf16[128,2048]{1,0:T(8,128)(2,1)S(1)}, u32[]{:S(2)}, u32[]{:S(2)}) collective-permute-start(bf16[128,2048]{1,0:T(8,128)(2,1)S(1)} %get-tuple-element.89.refs_1_), channel_id=1, source_target_pairs={{0,1},{1,0},{2,3},{3,2},{4,5},{5,4},{6,7},{7,6},{8,9},{9,8},{10,11... | collective-permute-start | bytes 1572872 | tf_op jit(solution)/shard_map/ppermute | solution.py:559
  116.1 7.3 %collective-permute-start.45 = (bf16[128,2048]{1,0:T(8,128)(2,1)S(1)}, bf16[128,2048]{1,0:T(8,128)(2,1)S(1)}, u32[]{:S(2)}, u32[]{:S(2)}) collective-permute-start(bf16[128,2048]{1,0:T(8,128)(2,1)S(1)} %get-tuple-element.90.refs_1_), channel_id=1, source_target_pairs={{0,1},{1,0},{2,3},{3,2},{4,5},{5,4},{6,7},{7,6},{8,9},{9,8},{10,11... | collective-permute-start | bytes 1572872 | tf_op jit(solution)/shard_map/ppermute | solution.py:559
  116.6 11.3 %collective-permute-start.46 = (bf16[64,2048]{1,0:T(8,128)(2,1)S(1)}, bf16[64,2048]{1,0:T(8,128)(2,1)S(1)}, u32[]{:S(2)}, u32[]{:S(2)}) collective-permute-start(bf16[64,2048]{1,0:T(8,128)(2,1)S(1)} %get-tuple-element.91), channel_id=1, source_target_pairs={{0,2},{1,3},{2,0},{3,1},{4,6},{5,7},{6,4},{7,5},{8,10},{9,11},{10,... | collective-permute-start | bytes 786440 | tf_op jit(solution)/shard_map/ppermute | solution.py:559
  118.0 9.9 %collective-permute-start.47 = (bf16[64,2048]{1,0:T(8,128)(2,1)S(1)}, bf16[64,2048]{1,0:T(8,128)(2,1)S(1)}, u32[]{:S(2)}, u32[]{:S(2)}) collective-permute-start(bf16[64,2048]{1,0:T(8,128)(2,1)S(1)} %get-tuple-element.92), channel_id=1, source_target_pairs={{0,4},{1,5},{2,6},{3,7},{4,0},{5,1},{6,2},{7,3},{8,12},{9,13},{10,... | collective-permute-start | bytes 786440 | tf_op jit(solution)/shard_map/ppermute | solution.py:559
  127.9 2.0 %collective-permute-start.48 = (bf16[128,2048]{1,0:T(8,128)(2,1)S(1)}, bf16[128,2048]{1,0:T(8,128)(2,1)S(1)}, u32[]{:S(2)}, u32[]{:S(2)}) collective-permute-start(bf16[128,2048]{1,0:T(8,128)(2,1)S(1)} %stack.11.refs_1_), channel_id=1, source_target_pairs={{0,1},{1,0},{2,3},{3,2},{4,5},{5,4},{6,7},{7,6},{8,9},{9,8},{10,11... | collective-permute-start | bytes 1572872 | tf_op jit(solution)/shard_map/ppermute | solution.py:559
  134.9 1.2 collective-permute-start.49
  136.2 3.7 %collective-permute-start.50 = (f32[8,256]{1,0:T(8,128)S(1)}, f32[8,256]{1,0:T(8,128)S(1)}, u32[]{:S(2)}, u32[]{:S(2)}) collective-permute-start(f32[8,256]{1,0:T(8,128)S(1)} %add_select_fusion.4), channel_id=1, source_target_pairs={{0,2},{1,3},{2,0},{3,1},{4,6},{5,7},{6,4},{7,5},{8,10},{9,11},{10,... | collective-permute-start | bytes 24584 | tf_op jit(solution)/shard_map/ppermute | solution.py:636
  139.9 3.7 %collective-permute-start.51 = (f32[8,256]{1,0:T(8,128)S(1)}, f32[8,256]{1,0:T(8,128)S(1)}, u32[]{:S(2)}, u32[]{:S(2)}) collective-permute-start(f32[8,256]{1,0:T(8,128)S(1)} %add_select_fusion.3), channel_id=1, source_target_pairs={{0,4},{1,5},{2,6},{3,7},{4,0},{5,1},{6,2},{7,3},{8,12},{9,13},{10,... | collective-permute-start | bytes 24584 | tf_op jit(solution)/shard_map/ppermute | solution.py:636
  142.0 4.2 %collective-permute-start.30 = (bf16[128,256]{1,0:T(8,128)(2,1)S(1)}, bf16[128,256]{1,0:T(8,128)(2,1)S(1)}, u32[]{:S(2)}, u32[]{:S(2)}) collective-permute-start(bf16[128,256]{1,0:T(8,128)(2,1)S(1)} %get-tuple-element.75), channel_id=1, source_target_pairs={{0,1},{1,0},{2,3},{3,2},{4,5},{5,4},{6,7},{7,6},{8,9},{9,8},{10,11... | collective-permute-start | bytes 196616 | tf_op jit(solution)/shard_map/ppermute | solution.py:559
  143.7 6.5 %collective-permute-start.52 = (f32[8,256]{1,0:T(8,128)S(1)}, f32[8,256]{1,0:T(8,128)S(1)}, u32[]{:S(2)}, u32[]{:S(2)}) collective-permute-start(f32[8,256]{1,0:T(8,128)S(1)} %add_select_fusion.2), channel_id=1, source_target_pairs={{0,8},{8,0},{16,24},{24,16},{1,9},{9,1},{17,25},{25,17},{2,10},{10... | collective-permute-start | bytes 24584 | tf_op jit(solution)/shard_map/ppermute | solution.py:636
  146.6 5.6 %collective-permute-start.31 = (bf16[32,2048]{1,0:T(8,128)(2,1)S(1)}, bf16[32,2048]{1,0:T(8,128)(2,1)S(1)}, u32[]{:S(2)}, u32[]{:S(2)}) collective-permute-start(bf16[32,2048]{1,0:T(8,128)(2,1)S(1)} %get-tuple-element.77), channel_id=1, source_target_pairs={{0,2},{1,3},{2,0},{3,1},{4,6},{5,7},{6,4},{7,5},{8,10},{9,11},{10,... | collective-permute-start | bytes 393224 | tf_op jit(solution)/shard_map/ppermute | solution.py:559
  147.0 5.6 %collective-permute-start.32 = (bf16[32,2048]{1,0:T(8,128)(2,1)S(1)}, bf16[32,2048]{1,0:T(8,128)(2,1)S(1)}, u32[]{:S(2)}, u32[]{:S(2)}) collective-permute-start(bf16[32,2048]{1,0:T(8,128)(2,1)S(1)} %get-tuple-element.78), channel_id=1, source_target_pairs={{0,4},{1,5},{2,6},{3,7},{4,0},{5,1},{6,2},{7,3},{8,12},{9,13},{10,... | collective-permute-start | bytes 393224 | tf_op jit(solution)/shard_map/ppermute | solution.py:559
  148.1 5.9 %collective-permute-start.33 = (bf16[32,2048]{1,0:T(8,128)(2,1)S(1)}, bf16[32,2048]{1,0:T(8,128)(2,1)S(1)}, u32[]{:S(2)}, u32[]{:S(2)}) collective-permute-start(bf16[32,2048]{1,0:T(8,128)(2,1)S(1)} %get-tuple-element.79), channel_id=1, source_target_pairs={{0,6},{1,7},{2,4},{3,5},{4,2},{5,3},{6,0},{7,1},{8,14},{9,15},{10,... | collective-permute-start | bytes 393224 | tf_op jit(solution)/shard_map/ppermute | solution.py:559
  150.2 4.7 %collective-permute-start.53 = (f32[8,256]{1,0:T(8,128)S(1)}, f32[8,256]{1,0:T(8,128)S(1)}, u32[]{:S(2)}, u32[]{:S(2)}) collective-permute-start(f32[8,256]{1,0:T(8,128)S(1)} %add_select_fusion.1), channel_id=1, source_target_pairs={{0,16},{8,24},{16,0},{24,8},{1,17},{9,25},{17,1},{25,9},{2,18},{10... | collective-permute-start | bytes 24584 | tf_op jit(solution)/shard_map/ppermute | solution.py:636
  (5 other events, 4.4 us)

commit v5 on v4

--- a/solution.py
+++ b/solution.py
@@ -603,7 +603,7 @@
     messages = exchange(messages)
     queries = exchange([query] * len(tok_masks))
     own_two = own_part(tok_count, place, query, key, value, cache_keys, cache_values)
-    keep = join(own, messages, [own_two[0]])
+    keep = join(own, messages, [own_two[0], queries[0]])
     parts = away_parts(tok_count, tok_masks, place, queries, cache_keys, cache_values, [keep[0]])
     _, normed, square = finish_layer(False, out_layer(*keep), residual)
 

time: 157 us -> 155 us (0.987)
  starting transfers between devices: 54 us -> 52.4 us
  transfers between devices with their start and end apart: 54 -> 54, of which waited for: 17 -> 16; matrix products, arithmetic and copies ran while one was open for 7% -> 7% of each run, Pallas kernels for 18% -> 18%
where the time goes in v5:
time: 155 us
  starting transfers between devices  52.4 us (34%)
  waiting for transfers between devices  41.7 us (27%)
  Pallas kernels  39.2 us (25%)
  local copies, waits for them, and re-layouts  18.9 us (12%)
  other arithmetic  1.63 us (1%)
    pallas_call x17, Pallas kernels, call(): return pl.pallas_call(body, in_specs=specs, **rest)(*operands, *after)  37 us
    ppermute x18, starting transfers between devices, by_tok(): return lax.ppermute(value, 'tok', xor_pairs(tok_count, mask))  26.6 us
    ppermute x18, waiting for transfers between devices, by_tok(): return lax.ppermute(value, 'tok', xor_pairs(tok_count, mask))  22.9 us
    ppermute x31, starting transfers between devices, by_head(): return lax.ppermute(value, 'head', xor_pairs(head_count, mask))  21.7 us
    ppermute x31, waiting for transfers between devices, by_head(): return lax.ppermute(value, 'head', xor_pairs(head_count, mask))  13 us
    gather x1, local copies, waits for them, and re-layouts, shards(): embed.at[ids].get(mode='promise_in_bounds')  9.81 us
    unnamed x30, local copies, waits for them, and re-layouts  8.26 us
    ppermute x5, waiting for transfers between devices, shards(): other = lax.ppermute(best, axis, xor_pairs(size, mask))  5.84 us
  transfers between devices with their start and end apart: 54, of which 16 were waited for; matrix products, arithmetic and copies ran while one was open for 7% of the time, Pallas kernels for 18%

profile of v5, /device:TPU:0, one launch (start us, length us, event | category | flops | bytes accessed | tf_op | source)
XLA Modules:
  0.0 154.9 jit_solution(9306112745896697945)
XLA Ops:
  1.2 2.6 %collective-permute-start = (bf16[256,256]{1,0:T(8,128)(2,1)}, bf16[256,256]{1,0:T(8,128)(2,1)S(1)}, u32[]{:S(2)}, u32[]{:S(2)}) collective-permute-start(bf16[256,256]{1,0:T(8,128)(2,1)} %refs_1_.2), channel_id=1, source_target_pairs={{0,2},{1,3},{2,0},{3,1},{4,6},{5,7},{6,4},{7,5},{8,10},{9,11},{10,... | collective-permute-start | bytes 393224 | tf_op jit(solution)/shard_map/ppermute | solution.py:559
  3.7 1.5 collective-permute-start.1
  5.3 0.7 pad_add_fusion.place.refs_0_
  6.0 0.7 copy-done.9
  7.3 9.8 %gather_fusion = bf16[1024,256]{1,0:T(8,128)(2,1)S(1)} fusion(bf16[25088,256]{1,0:T(8,128)(2,1)} %param.26, s32[1024]{0:T(1024)S(1)} %broadcast_clamp_fusion), kind=kCustom, calls=%fused_computation | custom fusion | bytes 1052672 | tf_op jit(solution)/shard_map/gather | solution.py:587
  18.3 2.1 %collective-permute-start.11 = (bf16[256,256]{1,0:T(8,128)(2,1)S(1)}, bf16[256,256]{1,0:T(8,128)(2,1)S(1)}, u32[]{:S(2)}, u32[]{:S(2)}) collective-permute-start(bf16[256,256]{1,0:T(8,128)(2,1)S(1)} %get-tuple-element.96.refs_13_), channel_id=1, source_target_pairs={{0,8},{8,0},{16,24},{24,16},{1,9},{9,1},{17,25},{25,17},{2,10},{10... | collective-permute-start | bytes 393224 | tf_op jit(solution)/shard_map/ppermute | solution.py:562
  20.4 2.6 %collective-permute-start.12 = (bf16[256,256]{1,0:T(8,128)(2,1)S(1)}, bf16[256,256]{1,0:T(8,128)(2,1)S(1)}, u32[]{:S(2)}, u32[]{:S(2)}) collective-permute-start(bf16[256,256]{1,0:T(8,128)(2,1)S(1)} %get-tuple-element.94), channel_id=1, source_target_pairs={{0,16},{8,24},{16,0},{24,8},{1,17},{9,25},{17,1},{25,9},{2,18},{10... | collective-permute-start | bytes 393224 | tf_op jit(solution)/shard_map/ppermute | solution.py:562
  23.1 1.4 copy-done.1
  24.5 1.3 copy-done.2
  25.8 1.2 copy-done.3
  27.0 0.9 copy-done.6
  27.9 1.8 %project.1 = (bf16[256,256]{1,0:T(8,128)(2,1)S(1)}, bf16[256,256]{1,0:T(8,128)(2,1)S(1)}, bf16[256,256]{1,0:T(8,128)(2,1)S(1)}, bf16[32,2048]{1,0:T(8,128)(2,1)S...) custom-call(s32[6]{0:T(128)S(1)} %pad_add_fusion.place.refs_0_, ...), custom_call_target="tpu_custom_call" | custom-call | flops 805306368 | bytes 4194304 | tf_op jit(solution)/shard_map/project/pallas_call | solution.py:37
  29.7 0.9 collective-permute-start.8
  30.6 1.0 copy-done.4
  31.6 1.0 copy-done.5
  33.4 2.8 %collective-permute-start.10 = (bf16[256,256]{1,0:T(8,128)(2,1)S(1)}, bf16[256,256]{1,0:T(8,128)(2,1)S(1)}, u32[]{:S(2)}, u32[]{:S(2)}) collective-permute-start(bf16[256,256]{1,0:T(8,128)(2,1)S(1)} %get-tuple-element.49.refs_1_), channel_id=1, source_target_pairs={{0,24},{8,16},{16,8},{24,0},{1,25},{9,17},{17,9},{25,1},{2,26},{10... | collective-permute-start | bytes 393224 | tf_op jit(solution)/shard_map/ppermute | solution.py:562
  36.2 0.7 choose.1.refs_6_
  36.9 1.6 %collective-permute-start.14 = (bf16[256,256]{1,0:T(8,128)(2,1)S(1)}, bf16[256,256]{1,0:T(8,128)(2,1)S(1)}, u32[]{:S(2)}, u32[]{:S(2)}) collective-permute-start(bf16[256,256]{1,0:T(8,128)(2,1)S(1)} %choose.1.refs_6_), channel_id=1, source_target_pairs={{0,2},{1,3},{2,0},{3,1},{4,6},{5,7},{6,4},{7,5},{8,10},{9,11},{10,... | collective-permute-start | bytes 393224 | tf_op jit(solution)/shard_map/ppermute | solution.py:559
  38.5 1.5 collective-permute-start.15
  40.5 0.8 collective-permute-start.9
  41.2 1.8 %collective-permute-done.14.refs_7_ = bf16[256,256]{1,0:T(8,128)(2,1)S(1)} collective-permute-done((bf16[256,256]{1,0:T(8,128)(2,1)S(1)}, bf16[256,256]{1,0:T(8,128)(2,1)S(1)}, u32[]{:S(2)}, u32[]{:S(2)}) %collective-permute-start.14) | collective-permute-done | bytes 131104 | tf_op jit(solution)/shard_map/ppermute | solution.py:559
  43.1 3.1 %collective-permute-done.15.refs_8_ = bf16[256,256]{1,0:T(8,128)(2,1)S(1)} collective-permute-done((bf16[256,256]{1,0:T(8,128)(2,1)S(1)}, bf16[256,256]{1,0:T(8,128)(2,1)S(1)}, u32[]{:S(2)}, u32[]{:S(2)}) %collective-permute-start.15) | collective-permute-done | bytes 131104 | tf_op jit(solution)/shard_map/ppermute | solution.py:559
  46.7 1.1 collective-permute-done.9.refs_2_
  47.8 4.9 %second_stage.1 = (bf16[272,256]{1,0:T(8,128)(2,1)S(1)}, bf16[272,256]{1,0:T(8,128)(2,1)S(1)}, bf16[272,256]{1,0:T(8,128)(2,1)S(1)}, bf16[256,256]{1,0:T(8,128)(...) custom-call(s32[6]{0:T(128)S(1)} %pad_add_fusion.place.refs_0_, ...), custom_call_target="tpu_custom_call" | custom-call | flops 1073741824 | bytes 4194304 | tf_op jit(solution)/shard_map/second_stage/pallas_call | solution.py:37
  52.7 1.5 collective-permute-start.25
  54.2 2.9 %collective-permute-start.26 = (bf16[272,256]{1,0:T(8,128)(2,1)S(1)}, bf16[272,256]{1,0:T(8,128)(2,1)S(1)}, u32[]{:S(2)}, u32[]{:S(2)}) collective-permute-start(bf16[272,256]{1,0:T(8,128)(2,1)S(1)} %get-tuple-element.69), channel_id=1, source_target_pairs={{0,24},{8,16},{16,8},{24,0},{1,25},{9,17},{17,9},{25,1},{2,26},{10... | collective-permute-start | bytes 417800 | tf_op jit(solution)/shard_map/ppermute | solution.py:562
  57.1 2.0 %own_part.3 = (f32[256,256]{1,0:T(8,128)S(1)}, f32[256,256]{1,0:T(8,128)S(1)}) custom-call(s32[6]{0:T(128)S(1)} %pad_add_fusion.place.refs_0_, bf16[256,256]{1,0:T(8,128)(2,1)S(1)} %get-tuple-element.49.refs_1_, bf16[256,256]{1,0:T(8,128)(2,1)S(1)} %get-tuple-element.63.refs_2_, bf16[256,256]{1,0:T(8,128)(2,1)S(1)} %get-tuple-element.64.refs_3_, ...), custom_call_target="tpu_custom_call" | custom-call | flops 268435456 | bytes 1048576 | tf_op jit(solution)/shard_map/own_part/pallas_call | solution.py:37
  59.2 2.2 %own_part.2 = (f32[256,256]{1,0:T(8,128)S(1)}, f32[256,256]{1,0:T(8,128)S(1)}) custom-call(s32[6]{0:T(128)S(1)} %pad_add_fusion.place.refs_0_, bf16[256,256]{1,0:T(8,128)(2,1)S(1)} %get-tuple-element.58.refs_1_, bf16[256,256]{1,0:T(8,128)(2,1)S(1)} %get-tuple-element.59.refs_2_, bf16[256,256]{1,0:T(8,128)(2,1)S(1)} %get-tuple-element.60.refs_3_, ...), custom_call_target="tpu_custom_call" | custom-call | flops 268435456 | bytes 1048576 | tf_op jit(solution)/shard_map/own_part/pallas_call | solution.py:37
  61.4 5.9 %collective-permute-done.21.refs_7_.refs_1_ = bf16[256,256]{1,0:T(8,128)(2,1)S(1)} collective-permute-done((bf16[256,256]{1,0:T(8,128)(2,1)S(1)}, bf16[256,256]{1,0:T(8,128)(2,1)S(1)}, u32[]{:S(2)}, u32[]{:S(2)}) %collective-permute-start.21) | collective-permute-done | bytes 131104 | tf_op jit(solution)/shard_map/ppermute | solution.py:562
  67.3 1.0 combine.2
  68.4 1.2 collective-permute-done.34.other
  70.3 1.2 collective-permute-start.36
  71.5 2.1 %collective-permute-start.37 = (bf16[32,2048]{1,0:T(8,128)(2,1)S(1)}, bf16[32,2048]{1,0:T(8,128)(2,1)S(1)}, u32[]{:S(2)}, u32[]{:S(2)}) collective-permute-start(bf16[32,2048]{1,0:T(8,128)(2,1)S(1)} %get-tuple-element.85), channel_id=1, source_target_pairs={{0,6},{1,7},{2,4},{3,5},{4,2},{5,3},{6,0},{7,1},{8,14},{9,15},{10,... | collective-permute-start | bytes 393224 | tf_op jit(solution)/shard_map/ppermute | solution.py:559
  73.7 1.7 %collective-permute-start.22 = (bf16[256,256]{1,0:T(8,128)(2,1)S(1)}, bf16[256,256]{1,0:T(8,128)(2,1)S(1)}, u32[]{:S(2)}, u32[]{:S(2)}) collective-permute-start(bf16[256,256]{1,0:T(8,128)(2,1)S(1)} %get-tuple-element.58.refs_1_), channel_id=1, source_target_pairs={{0,16},{8,24},{16,0},{24,8},{1,17},{9,25},{17,1},{25,9},{2,18},{10... | collective-permute-start | bytes 393224 | tf_op jit(solution)/shard_map/ppermute | solution.py:562
  75.4 2.4 %collective-permute-start.23 = (bf16[256,256]{1,0:T(8,128)(2,1)S(1)}, bf16[256,256]{1,0:T(8,128)(2,1)S(1)}, u32[]{:S(2)}, u32[]{:S(2)}) collective-permute-start(bf16[256,256]{1,0:T(8,128)(2,1)S(1)} %get-tuple-element.58.refs_1_), channel_id=1, source_target_pairs={{0,24},{8,16},{16,8},{24,0},{1,25},{9,17},{17,9},{25,1},{2,26},{10... | collective-permute-start | bytes 393224 | tf_op jit(solution)/shard_map/ppermute | solution.py:562
  77.8 1.2 collective-permute-done.37.refs_3_
  79.0 0.9 finish.3
  79.9 1.9 %collective-permute-start.38 = (bf16[32,2048]{1,0:T(8,128)(2,1)S(1)}, bf16[32,2048]{1,0:T(8,128)(2,1)S(1)}, u32[]{:S(2)}, u32[]{:S(2)}) collective-permute-start(bf16[32,2048]{1,0:T(8,128)(2,1)S(1)} %get-tuple-element.88.refs_0_), channel_id=1, source_target_pairs={{0,8},{8,0},{16,24},{24,16},{1,9},{9,1},{17,25},{25,17},{2,10},{10... | collective-permute-start | bytes 393224 | tf_op jit(solution)/shard_map/ppermute | solution.py:562
  81.7 2.6 %collective-permute-start.40 = (bf16[32,2048]{1,0:T(8,128)(2,1)S(1)}, bf16[32,2048]{1,0:T(8,128)(2,1)S(1)}, u32[]{:S(2)}, u32[]{:S(2)}) collective-permute-start(bf16[32,2048]{1,0:T(8,128)(2,1)S(1)} %get-tuple-element.88.refs_0_), channel_id=1, source_target_pairs={{0,24},{8,16},{16,8},{24,0},{1,25},{9,17},{17,9},{25,1},{2,26},{10... | collective-permute-start | bytes 393224 | tf_op jit(solution)/shard_map/ppermute | solution.py:562
  84.3 7.6 %collective-permute-done.22.refs_2_ = bf16[256,256]{1,0:T(8,128)(2,1)S(1)} collective-permute-done((bf16[256,256]{1,0:T(8,128)(2,1)S(1)}, bf16[256,256]{1,0:T(8,128)(2,1)S(1)}, u32[]{:S(2)}, u32[]{:S(2)}) %collective-permute-start.22) | collective-permute-done | bytes 131104 | tf_op jit(solution)/shard_map/ppermute | solution.py:562
  91.9 3.8 %away_parts.1 = (bf16[272,256]{1,0:T(8,128)(2,1)S(1)}, bf16[272,256]{1,0:T(8,128)(2,1)S(1)}, bf16[272,256]{1,0:T(8,128)(2,1)S(1)}) custom-call(s32[6]{0:T(128)S(1)} %pad_add_fusion.place.refs_0_, bf16[256,256]{1,0:T(8,128)(2,1)S(1)} %collective-permute-done.21.refs_7_.refs_1_, bf16[256,256]{1,0:T(8,128)(2,1)S(1)} %collective-permute-done.22.refs_2_, ...), custom_call_target="tpu_custom_call" | custom-call | flops 268435456 | bytes 1048576 | tf_op jit(solution)/shard_map/away_parts/pallas_call | solution.py:37
  95.7 1.9 %collective-permute-done.39.refs_2_ = bf16[32,2048]{1,0:T(8,128)(2,1)S(1)} collective-permute-done((bf16[32,2048]{1,0:T(8,128)(2,1)S(1)}, bf16[32,2048]{1,0:T(8,128)(2,1)S(1)}, u32[]{:S(2)}, u32[]{:S(2)}) %collective-permute-start.39) | collective-permute-done | bytes 131104 | tf_op jit(solution)/shard_map/ppermute | solution.py:562
  98.1 1.0 collective-permute-start.43
  99.1 2.0 %collective-permute-start.27 = (bf16[272,256]{1,0:T(8,128)(2,1)S(1)}, bf16[272,256]{1,0:T(8,128)(2,1)S(1)}, u32[]{:S(2)}, u32[]{:S(2)}) collective-permute-start(bf16[272,256]{1,0:T(8,128)(2,1)S(1)} %get-tuple-element.71.refs_4_), channel_id=1, source_target_pairs={{0,8},{8,0},{16,24},{24,16},{1,9},{9,1},{17,25},{25,17},{2,10},{10... | collective-permute-start | bytes 417800 | tf_op jit(solution)/shard_map/ppermute | solution.py:562
  101.4 2.1 %collective-permute-start.29 = (bf16[272,256]{1,0:T(8,128)(2,1)S(1)}, bf16[272,256]{1,0:T(8,128)(2,1)S(1)}, u32[]{:S(2)}, u32[]{:S(2)}) collective-permute-start(bf16[272,256]{1,0:T(8,128)(2,1)S(1)} %get-tuple-element.73), channel_id=1, source_target_pairs={{0,24},{8,16},{16,8},{24,0},{1,25},{9,17},{17,9},{25,1},{2,26},{10... | collective-permute-start | bytes 417800 | tf_op jit(solution)/shard_map/ppermute | solution.py:562
  103.5 4.4 %largest_logits.4.refs_2_.refs_0_ = f32[8,256]{1,0:T(8,128)S(1)} custom-call(s32[6]{0:T(128)S(1)} %pad_add_fusion.place.refs_0_, bf16[128,2048]{1,0:T(8,128)(2,1)S(1)} %stack.10.refs_1_, bf16[128,2048]{1,0:T(8,128)(2,1)S(1)} %collective-permute-done.41.refs_2_, bf16[3136,2048]{1,0:T(8,128)(2,1)S(1)} %bitcast.14), custom_call_target="tpu_custom_call" | custom-call | flops 3288334336 | bytes 12845056 | tf_op jit(solution)/shard_map/largest_logits/pallas_call | solution.py:37
  107.9 6.4 %collective-permute-done.28.refs_4_ = bf16[272,256]{1,0:T(8,128)(2,1)S(1)} collective-permute-done((bf16[272,256]{1,0:T(8,128)(2,1)S(1)}, bf16[272,256]{1,0:T(8,128)(2,1)S(1)}, u32[]{:S(2)}, u32[]{:S(2)}) %collective-permute-start.28) | collective-permute-done | bytes 139296 | tf_op jit(solution)/shard_map/ppermute | solution.py:562
  115.0 1.6 %collective-permute-start.46 = (bf16[64,2048]{1,0:T(8,128)(2,1)S(1)}, bf16[64,2048]{1,0:T(8,128)(2,1)S(1)}, u32[]{:S(2)}, u32[]{:S(2)}) collective-permute-start(bf16[64,2048]{1,0:T(8,128)(2,1)S(1)} %get-tuple-element.91), channel_id=1, source_target_pairs={{0,2},{1,3},{2,0},{3,1},{4,6},{5,7},{6,4},{7,5},{8,10},{9,11},{10,... | collective-permute-start | bytes 786440 | tf_op jit(solution)/shard_map/ppermute | solution.py:559
  116.6 1.0 collective-permute-start.47
  117.6 4.4 %largest_logits.5.refs_4_.refs_1_ = f32[8,256]{1,0:T(8,128)S(1)} custom-call(s32[6]{0:T(128)S(1)} %pad_add_fusion.place.refs_0_, bf16[128,2048]{1,0:T(8,128)(2,1)S(1)} %get-tuple-element.89.refs_1_, bf16[128,2048]{1,0:T(8,128)(2,1)S(1)} %collective-permute-done.44.refs_2_, bf16[3136,2048]{1,0:T(8,128)(2,1)S(1)} %bitcast.14), custom_call_target="tpu_custom_call" | custom-call | flops 3288334336 | bytes 12845056 | tf_op jit(solution)/shard_map/largest_logits/pallas_call | solution.py:37
  122.1 4.4 %largest_logits.6.refs_2_ = f32[8,256]{1,0:T(8,128)S(1)} custom-call(s32[6]{0:T(128)S(1)} %pad_add_fusion.place.refs_0_, bf16[128,2048]{1,0:T(8,128)(2,1)S(1)} %get-tuple-element.90.refs_1_, bf16[128,2048]{1,0:T(8,128)(2,1)S(1)} %collective-permute-done.45.refs_2_, bf16[3136,2048]{1,0:T(8,128)(2,1)S(1)} %bitcast.14, f32[8,256]{1,0:T(8,128)S(1)} %largest_logits.5.refs_4_.refs_1_), custom_call_target="tpu_custom_call" | custom-call | flops 3288334336 | bytes 12845056 | tf_op jit(solution)/shard_map/largest_logits/pallas_call | solution.py:37
  126.6 1.9 %collective-permute-done.48.refs_2_ = bf16[128,2048]{1,0:T(8,128)(2,1)S(1)} collective-permute-done((bf16[128,2048]{1,0:T(8,128)(2,1)S(1)}, bf16[128,2048]{1,0:T(8,128)(2,1)S(1)}, u32[]{:S(2)}, u32[]{:S(2)}) %collective-permute-start.48) | collective-permute-done | bytes 524320 | tf_op jit(solution)/shard_map/ppermute | solution.py:559
  128.5 4.4 %largest_logits.7.refs_3_ = f32[8,256]{1,0:T(8,128)S(1)} custom-call(s32[6]{0:T(128)S(1)} %pad_add_fusion.place.refs_0_, bf16[128,2048]{1,0:T(8,128)(2,1)S(1)} %stack.11.refs_1_, bf16[128,2048]{1,0:T(8,128)(2,1)S(1)} %collective-permute-done.48.refs_2_, bf16[3136,2048]{1,0:T(8,128)(2,1)S(1)} %bitcast.14), custom_call_target="tpu_custom_call" | custom-call | flops 3288334336 | bytes 12845056 | tf_op jit(solution)/shard_map/largest_logits/pallas_call | solution.py:37
  133.7 1.0 collective-permute-done.49
  135.2 3.3 %collective-permute-done.50 = f32[8,256]{1,0:T(8,128)S(1)} collective-permute-done((f32[8,256]{1,0:T(8,128)S(1)}, f32[8,256]{1,0:T(8,128)S(1)}, u32[]{:S(2)}, u32[]{:S(2)}) %collective-permute-start.50) | collective-permute-done | bytes 8224 | tf_op jit(solution)/shard_map/ppermute | solution.py:636
  138.6 1.0 collective-permute-start.51
  139.6 1.0 combine.3
  140.7 1.5 collective-permute-done.51
  142.3 2.4 %collective-permute-start.52 = (f32[8,256]{1,0:T(8,128)S(1)}, f32[8,256]{1,0:T(8,128)S(1)}, u32[]{:S(2)}, u32[]{:S(2)}) collective-permute-start(f32[8,256]{1,0:T(8,128)S(1)} %add_select_fusion.2), channel_id=1, source_target_pairs={{0,8},{8,0},{16,24},{24,16},{1,9},{9,1},{17,25},{25,17},{2,10},{10... | collective-permute-start | bytes 24584 | tf_op jit(solution)/shard_map/ppermute | solution.py:636
  145.6 1.0 collective-permute-start.32
  146.7 2.1 %collective-permute-start.33 = (bf16[32,2048]{1,0:T(8,128)(2,1)S(1)}, bf16[32,2048]{1,0:T(8,128)(2,1)S(1)}, u32[]{:S(2)}, u32[]{:S(2)}) collective-permute-start(bf16[32,2048]{1,0:T(8,128)(2,1)S(1)} %get-tuple-element.79), channel_id=1, source_target_pairs={{0,6},{1,7},{2,4},{3,5},{4,2},{5,3},{6,0},{7,1},{8,14},{9,15},{10,... | collective-permute-start | bytes 393224 | tf_op jit(solution)/shard_map/ppermute | solution.py:559
  148.9 1.9 %collective-permute-done.31.refs_1_ = bf16[32,2048]{1,0:T(8,128)(2,1)S(1)} collective-permute-done((bf16[32,2048]{1,0:T(8,128)(2,1)S(1)}, bf16[32,2048]{1,0:T(8,128)(2,1)S(1)}, u32[]{:S(2)}, u32[]{:S(2)}) %collective-permute-start.31) | collective-permute-done | bytes 131104 | tf_op jit(solution)/shard_map/ppermute | solution.py:559
  151.2 1.4 collective-permute-done.33.refs_3_
  152.6 0.9 finish.2
  (113 shorter events, 11.0 us)
Async XLA Ops:
  0.6 69.0 %copy-start = (bf16[256,2048]{1,0:T(8,128)(2,1)S(1)}, bf16[256,2048]{1,0:T(8,128)(2,1)}, u32[]{:S(2)}) copy-start(bf16[256,2048]{1,0:T(8,128)(2,1)} %w_keep.3) | copy-start | bytes 3145732
  0.6 78.3 %copy-start.7 = (f32[2048]{0:T(1024)S(1)}, f32[2048]{0:T(1024)}, u32[]{:S(2)}) copy-start(f32[2048]{0:T(1024)} %param.24) | copy-start | bytes 24580
  0.7 78.3 %copy-start.8 = (f32[2048]{0:T(1024)S(1)}, f32[2048]{0:T(1024)}, u32[]{:S(2)}) copy-start(f32[2048]{0:T(1024)} %param.25) | copy-start | bytes 24580
  0.7 22.5 %collective-permute-start.7 = (bf16[256,2048]{1,0:T(8,128)(2,1)}, bf16[256,2048]{1,0:T(8,128)(2,1)S(1)}, u32[]{:S(2)}, u32[]{:S(2)}) collective-permute-start(bf16[256,2048]{1,0:T(8,128)(2,1)} %w_keep.3), channel_id=1, source_target_pairs={{0,1},{1,0},{2,3},{3,2},{4,5},{5,4},{6,7},{7,6},{8,9},{9,8},{10,11... | collective-permute-start | bytes 3145736 | tf_op jit(solution)/shard_map/ppermute | solution.py:559
  1.2 16.0 %collective-permute-start = (bf16[256,256]{1,0:T(8,128)(2,1)}, bf16[256,256]{1,0:T(8,128)(2,1)S(1)}, u32[]{:S(2)}, u32[]{:S(2)}) collective-permute-start(bf16[256,256]{1,0:T(8,128)(2,1)} %refs_1_.2), channel_id=1, source_target_pairs={{0,2},{1,3},{2,0},{3,1},{4,6},{5,7},{6,4},{7,5},{8,10},{9,11},{10,... | collective-permute-start | bytes 393224 | tf_op jit(solution)/shard_map/ppermute | solution.py:559
  3.7 14.0 %collective-permute-start.1 = (bf16[256,256]{1,0:T(8,128)(2,1)}, bf16[256,256]{1,0:T(8,128)(2,1)S(1)}, u32[]{:S(2)}, u32[]{:S(2)}) collective-permute-start(bf16[256,256]{1,0:T(8,128)(2,1)} %refs_1_.2), channel_id=1, source_target_pairs={{0,4},{1,5},{2,6},{3,7},{4,0},{5,1},{6,2},{7,3},{8,12},{9,13},{10,... | collective-permute-start | bytes 393224 | tf_op jit(solution)/shard_map/ppermute | solution.py:559
  5.3 12.5 %collective-permute-start.2 = (bf16[256,256]{1,0:T(8,128)(2,1)}, bf16[256,256]{1,0:T(8,128)(2,1)S(1)}, u32[]{:S(2)}, u32[]{:S(2)}) collective-permute-start(bf16[256,256]{1,0:T(8,128)(2,1)} %refs_1_.2), channel_id=1, source_target_pairs={{0,6},{1,7},{2,4},{3,5},{4,2},{5,3},{6,0},{7,1},{8,14},{9,15},{10,... | collective-permute-start | bytes 393224 | tf_op jit(solution)/shard_map/ppermute | solution.py:559
  5.3 13.0 %collective-permute-start.3 = (bf16[256,256]{1,0:T(8,128)(2,1)}, bf16[256,256]{1,0:T(8,128)(2,1)S(1)}, u32[]{:S(2)}, u32[]{:S(2)}) collective-permute-start(bf16[256,256]{1,0:T(8,128)(2,1)} %refs_1_.2), channel_id=1, source_target_pairs={{0,1},{1,0},{2,3},{3,2},{4,5},{5,4},{6,7},{7,6},{8,9},{9,8},{10,11... | collective-permute-start | bytes 393224 | tf_op jit(solution)/shard_map/ppermute | solution.py:559
  7.3 96.2 %slice-start = ((s8[12845056]{0:T(1024)(128)(4,1)}), s8[262144]{0:T(1024)(128)(4,1)S(1)}, s32[]{:S(2)}) async-start(s8[12845056]{0:T(1024)(128)(4,1)} %bitcast.13), calls=%async_computation | async-start | bytes 524288
  17.1 3.2 %collective-permute-start.4 = (bf16[256,256]{1,0:T(8,128)(2,1)S(1)}, bf16[256,256]{1,0:T(8,128)(2,1)S(1)}, u32[]{:S(2)}, u32[]{:S(2)}) collective-permute-start(bf16[256,256]{1,0:T(8,128)(2,1)S(1)} %collective-permute-done.refs_2_), channel_id=1, source_target_pairs={{0,1},{1,0},{2,3},{3,2},{4,5},{5,4},{6,7},{7,6},{8,9},{9,8},{10,11... | collective-permute-start | bytes 393224 | tf_op jit(solution)/shard_map/ppermute | solution.py:559
  17.7 5.3 %collective-permute-start.5 = (bf16[256,256]{1,0:T(8,128)(2,1)S(1)}, bf16[256,256]{1,0:T(8,128)(2,1)S(1)}, u32[]{:S(2)}, u32[]{:S(2)}) collective-permute-start(bf16[256,256]{1,0:T(8,128)(2,1)S(1)} %collective-permute-done.1.refs_3_), channel_id=1, source_target_pairs={{0,1},{1,0},{2,3},{3,2},{4,5},{5,4},{6,7},{7,6},{8,9},{9,8},{10,11... | collective-permute-start | bytes 393224 | tf_op jit(solution)/shard_map/ppermute | solution.py:559
  17.8 5.3 %collective-permute-start.6 = (bf16[256,256]{1,0:T(8,128)(2,1)S(1)}, bf16[256,256]{1,0:T(8,128)(2,1)S(1)}, u32[]{:S(2)}, u32[]{:S(2)}) collective-permute-start(bf16[256,256]{1,0:T(8,128)(2,1)S(1)} %collective-permute-done.2.refs_4_), channel_id=1, source_target_pairs={{0,1},{1,0},{2,3},{3,2},{4,5},{5,4},{6,7},{7,6},{8,9},{9,8},{10,11... | collective-permute-start | bytes 393224 | tf_op jit(solution)/shard_map/ppermute | solution.py:559
  18.3 17.9 %collective-permute-start.11 = (bf16[256,256]{1,0:T(8,128)(2,1)S(1)}, bf16[256,256]{1,0:T(8,128)(2,1)S(1)}, u32[]{:S(2)}, u32[]{:S(2)}) collective-permute-start(bf16[256,256]{1,0:T(8,128)(2,1)S(1)} %get-tuple-element.96.refs_13_), channel_id=1, source_target_pairs={{0,8},{8,0},{16,24},{24,16},{1,9},{9,1},{17,25},{25,17},{2,10},{10... | collective-permute-start | bytes 393224 | tf_op jit(solution)/shard_map/ppermute | solution.py:562
  20.4 15.8 %collective-permute-start.12 = (bf16[256,256]{1,0:T(8,128)(2,1)S(1)}, bf16[256,256]{1,0:T(8,128)(2,1)S(1)}, u32[]{:S(2)}, u32[]{:S(2)}) collective-permute-start(bf16[256,256]{1,0:T(8,128)(2,1)S(1)} %get-tuple-element.94), channel_id=1, source_target_pairs={{0,16},{8,24},{16,0},{24,8},{1,17},{9,25},{17,1},{25,9},{2,18},{10... | collective-permute-start | bytes 393224 | tf_op jit(solution)/shard_map/ppermute | solution.py:562
  23.0 80.5 %slice-start.1 = ((s8[12845056]{0:T(1024)(128)(4,1)}), s8[4194304]{0:T(1024)(128)(4,1)S(1)}, s32[]{:S(2)}) async-start(s8[12845056]{0:T(1024)(128)(4,1)} %bitcast.13), calls=%async_computation.1 | async-start | bytes 8388608
  23.0 13.2 %collective-permute-start.13 = (bf16[256,256]{1,0:T(8,128)(2,1)S(1)}, bf16[256,256]{1,0:T(8,128)(2,1)S(1)}, u32[]{:S(2)}, u32[]{:S(2)}) collective-permute-start(bf16[256,256]{1,0:T(8,128)(2,1)S(1)} %get-tuple-element.93), channel_id=1, source_target_pairs={{0,24},{8,16},{16,8},{24,0},{1,25},{9,17},{17,9},{25,1},{2,26},{10... | collective-permute-start | bytes 393224 | tf_op jit(solution)/shard_map/ppermute | solution.py:562
  23.1 1.4 copy-start.1
  24.5 1.3 copy-start.2
  25.8 1.2 copy-start.3
  29.7 6.5 %collective-permute-start.8 = (bf16[256,256]{1,0:T(8,128)(2,1)S(1)}, bf16[256,256]{1,0:T(8,128)(2,1)S(1)}, u32[]{:S(2)}, u32[]{:S(2)}) collective-permute-start(bf16[256,256]{1,0:T(8,128)(2,1)S(1)} %get-tuple-element.49.refs_1_), channel_id=1, source_target_pairs={{0,8},{8,0},{16,24},{24,16},{1,9},{9,1},{17,25},{25,17},{2,10},{10... | collective-permute-start | bytes 393224 | tf_op jit(solution)/shard_map/ppermute | solution.py:562
  33.4 7.8 %collective-permute-start.10 = (bf16[256,256]{1,0:T(8,128)(2,1)S(1)}, bf16[256,256]{1,0:T(8,128)(2,1)S(1)}, u32[]{:S(2)}, u32[]{:S(2)}) collective-permute-start(bf16[256,256]{1,0:T(8,128)(2,1)S(1)} %get-tuple-element.49.refs_1_), channel_id=1, source_target_pairs={{0,24},{8,16},{16,8},{24,0},{1,25},{9,17},{17,9},{25,1},{2,26},{10... | collective-permute-start | bytes 393224 | tf_op jit(solution)/shard_map/ppermute | solution.py:562
  36.9 6.1 %collective-permute-start.14 = (bf16[256,256]{1,0:T(8,128)(2,1)S(1)}, bf16[256,256]{1,0:T(8,128)(2,1)S(1)}, u32[]{:S(2)}, u32[]{:S(2)}) collective-permute-start(bf16[256,256]{1,0:T(8,128)(2,1)S(1)} %choose.1.refs_6_), channel_id=1, source_target_pairs={{0,2},{1,3},{2,0},{3,1},{4,6},{5,7},{6,4},{7,5},{8,10},{9,11},{10,... | collective-permute-start | bytes 393224 | tf_op jit(solution)/shard_map/ppermute | solution.py:559
  38.5 7.7 %collective-permute-start.15 = (bf16[256,256]{1,0:T(8,128)(2,1)S(1)}, bf16[256,256]{1,0:T(8,128)(2,1)S(1)}, u32[]{:S(2)}, u32[]{:S(2)}) collective-permute-start(bf16[256,256]{1,0:T(8,128)(2,1)S(1)} %choose.1.refs_6_), channel_id=1, source_target_pairs={{0,4},{1,5},{2,6},{3,7},{4,0},{5,1},{6,2},{7,3},{8,12},{9,13},{10,... | collective-permute-start | bytes 393224 | tf_op jit(solution)/shard_map/ppermute | solution.py:559
  40.0 6.1 %collective-permute-start.16 = (bf16[256,256]{1,0:T(8,128)(2,1)S(1)}, bf16[256,256]{1,0:T(8,128)(2,1)S(1)}, u32[]{:S(2)}, u32[]{:S(2)}) collective-permute-start(bf16[256,256]{1,0:T(8,128)(2,1)S(1)} %choose.1.refs_6_), channel_id=1, source_target_pairs={{0,6},{1,7},{2,4},{3,5},{4,2},{5,3},{6,0},{7,1},{8,14},{9,15},{10,... | collective-permute-start | bytes 393224 | tf_op jit(solution)/shard_map/ppermute | solution.py:559
  40.5 7.3 %collective-permute-start.9 = (bf16[256,256]{1,0:T(8,128)(2,1)S(1)}, bf16[256,256]{1,0:T(8,128)(2,1)S(1)}, u32[]{:S(2)}, u32[]{:S(2)}) collective-permute-start(bf16[256,256]{1,0:T(8,128)(2,1)S(1)} %get-tuple-element.49.refs_1_), channel_id=1, source_target_pairs={{0,16},{8,24},{16,0},{24,8},{1,17},{9,25},{17,1},{25,9},{2,18},{10... | collective-permute-start | bytes 393224 | tf_op jit(solution)/shard_map/ppermute | solution.py:562
  41.2 6.5 %collective-permute-start.17 = (bf16[256,256]{1,0:T(8,128)(2,1)S(1)}, bf16[256,256]{1,0:T(8,128)(2,1)S(1)}, u32[]{:S(2)}, u32[]{:S(2)}) collective-permute-start(bf16[256,256]{1,0:T(8,128)(2,1)S(1)} %choose.1.refs_6_), channel_id=1, source_target_pairs={{0,1},{1,0},{2,3},{3,2},{4,5},{5,4},{6,7},{7,6},{8,9},{9,8},{10,11... | collective-permute-start | bytes 393224 | tf_op jit(solution)/shard_map/ppermute | solution.py:559
  43.0 4.7 %collective-permute-start.18 = (bf16[256,256]{1,0:T(8,128)(2,1)S(1)}, bf16[256,256]{1,0:T(8,128)(2,1)S(1)}, u32[]{:S(2)}, u32[]{:S(2)}) collective-permute-start(bf16[256,256]{1,0:T(8,128)(2,1)S(1)} %collective-permute-done.14.refs_7_), channel_id=1, source_target_pairs={{0,1},{1,0},{2,3},{3,2},{4,5},{5,4},{6,7},{7,6},{8,9},{9,8},{10,11... | collective-permute-start | bytes 393224 | tf_op jit(solution)/shard_map/ppermute | solution.py:559
  46.1 1.6 %collective-permute-start.19 = (bf16[256,256]{1,0:T(8,128)(2,1)S(1)}, bf16[256,256]{1,0:T(8,128)(2,1)S(1)}, u32[]{:S(2)}, u32[]{:S(2)}) collective-permute-start(bf16[256,256]{1,0:T(8,128)(2,1)S(1)} %collective-permute-done.15.refs_8_), channel_id=1, source_target_pairs={{0,1},{1,0},{2,3},{3,2},{4,5},{5,4},{6,7},{7,6},{8,9},{9,8},{10,11... | collective-permute-start | bytes 393224 | tf_op jit(solution)/shard_map/ppermute | solution.py:559
  46.1 1.6 %collective-permute-start.20 = (bf16[256,256]{1,0:T(8,128)(2,1)S(1)}, bf16[256,256]{1,0:T(8,128)(2,1)S(1)}, u32[]{:S(2)}, u32[]{:S(2)}) collective-permute-start(bf16[256,256]{1,0:T(8,128)(2,1)S(1)} %collective-permute-done.16.refs_9_), channel_id=1, source_target_pairs={{0,1},{1,0},{2,3},{3,2},{4,5},{5,4},{6,7},{7,6},{8,9},{9,8},{10,11... | collective-permute-start | bytes 393224 | tf_op jit(solution)/shard_map/ppermute | solution.py:559
  47.8 55.7 %slice-start.2 = ((s8[12845056]{0:T(1024)(128)(4,1)}), s8[4194304]{0:T(1024)(128)(4,1)S(1)}, s32[]{:S(2)}) async-start(s8[12845056]{0:T(1024)(128)(4,1)} %bitcast.13), calls=%async_computation.2 | async-start | bytes 8388608
  52.7 14.6 %collective-permute-start.24 = (bf16[272,256]{1,0:T(8,128)(2,1)S(1)}, bf16[272,256]{1,0:T(8,128)(2,1)S(1)}, u32[]{:S(2)}, u32[]{:S(2)}) collective-permute-start(bf16[272,256]{1,0:T(8,128)(2,1)S(1)} %get-tuple-element.67), channel_id=1, source_target_pairs={{0,8},{8,0},{16,24},{24,16},{1,9},{9,1},{17,25},{25,17},{2,10},{10... | collective-permute-start | bytes 417800 | tf_op jit(solution)/shard_map/ppermute | solution.py:562
  52.7 14.5 %collective-permute-start.25 = (bf16[272,256]{1,0:T(8,128)(2,1)S(1)}, bf16[272,256]{1,0:T(8,128)(2,1)S(1)}, u32[]{:S(2)}, u32[]{:S(2)}) collective-permute-start(bf16[272,256]{1,0:T(8,128)(2,1)S(1)} %get-tuple-element.68), channel_id=1, source_target_pairs={{0,16},{8,24},{16,0},{24,8},{1,17},{9,25},{17,1},{25,9},{2,18},{10... | collective-permute-start | bytes 417800 | tf_op jit(solution)/shard_map/ppermute | solution.py:562
  54.2 13.0 %collective-permute-start.26 = (bf16[272,256]{1,0:T(8,128)(2,1)S(1)}, bf16[272,256]{1,0:T(8,128)(2,1)S(1)}, u32[]{:S(2)}, u32[]{:S(2)}) collective-permute-start(bf16[272,256]{1,0:T(8,128)(2,1)S(1)} %get-tuple-element.69), channel_id=1, source_target_pairs={{0,24},{8,16},{16,8},{24,0},{1,25},{9,17},{17,9},{25,1},{2,26},{10... | collective-permute-start | bytes 417800 | tf_op jit(solution)/shard_map/ppermute | solution.py:562
  57.1 10.1 %collective-permute-start.21 = (bf16[256,256]{1,0:T(8,128)(2,1)S(1)}, bf16[256,256]{1,0:T(8,128)(2,1)S(1)}, u32[]{:S(2)}, u32[]{:S(2)}) collective-permute-start(bf16[256,256]{1,0:T(8,128)(2,1)S(1)} %get-tuple-element.58.refs_1_), channel_id=1, source_target_pairs={{0,8},{8,0},{16,24},{24,16},{1,9},{9,1},{17,25},{25,17},{2,10},{10... | collective-permute-start | bytes 393224 | tf_op jit(solution)/shard_map/ppermute | solution.py:562
  59.1 44.3 %slice-start.3 = ((s8[12845056]{0:T(1024)(128)(4,1)}), s8[4194304]{0:T(1024)(128)(4,1)S(1)}, s32[]{:S(2)}) async-start(s8[12845056]{0:T(1024)(128)(4,1)} %bitcast.13), calls=%async_computation.3 | async-start | bytes 8388608
  68.3 1.3 collective-permute-start.34
  70.1 7.7 %collective-permute-start.35 = (bf16[32,2048]{1,0:T(8,128)(2,1)S(1)}, bf16[32,2048]{1,0:T(8,128)(2,1)S(1)}, u32[]{:S(2)}, u32[]{:S(2)}) collective-permute-start(bf16[32,2048]{1,0:T(8,128)(2,1)S(1)} %get-tuple-element.83), channel_id=1, source_target_pairs={{0,2},{1,3},{2,0},{3,1},{4,6},{5,7},{6,4},{7,5},{8,10},{9,11},{10,... | collective-permute-start | bytes 393224 | tf_op jit(solution)/shard_map/ppermute | solution.py:559
  70.3 7.5 %collective-permute-start.36 = (bf16[32,2048]{1,0:T(8,128)(2,1)S(1)}, bf16[32,2048]{1,0:T(8,128)(2,1)S(1)}, u32[]{:S(2)}, u32[]{:S(2)}) collective-permute-start(bf16[32,2048]{1,0:T(8,128)(2,1)S(1)} %get-tuple-element.84), channel_id=1, source_target_pairs={{0,4},{1,5},{2,6},{3,7},{4,0},{5,1},{6,2},{7,3},{8,12},{9,13},{10,... | collective-permute-start | bytes 393224 | tf_op jit(solution)/shard_map/ppermute | solution.py:559
  71.5 7.5 %collective-permute-start.37 = (bf16[32,2048]{1,0:T(8,128)(2,1)S(1)}, bf16[32,2048]{1,0:T(8,128)(2,1)S(1)}, u32[]{:S(2)}, u32[]{:S(2)}) collective-permute-start(bf16[32,2048]{1,0:T(8,128)(2,1)S(1)} %get-tuple-element.85), channel_id=1, source_target_pairs={{0,6},{1,7},{2,4},{3,5},{4,2},{5,3},{6,0},{7,1},{8,14},{9,15},{10,... | collective-permute-start | bytes 393224 | tf_op jit(solution)/shard_map/ppermute | solution.py:559
  73.7 18.3 %collective-permute-start.22 = (bf16[256,256]{1,0:T(8,128)(2,1)S(1)}, bf16[256,256]{1,0:T(8,128)(2,1)S(1)}, u32[]{:S(2)}, u32[]{:S(2)}) collective-permute-start(bf16[256,256]{1,0:T(8,128)(2,1)S(1)} %get-tuple-element.58.refs_1_), channel_id=1, source_target_pairs={{0,16},{8,24},{16,0},{24,8},{1,17},{9,25},{17,1},{25,9},{2,18},{10... | collective-permute-start | bytes 393224 | tf_op jit(solution)/shard_map/ppermute | solution.py:562
  75.4 16.6 %collective-permute-start.23 = (bf16[256,256]{1,0:T(8,128)(2,1)S(1)}, bf16[256,256]{1,0:T(8,128)(2,1)S(1)}, u32[]{:S(2)}, u32[]{:S(2)}) collective-permute-start(bf16[256,256]{1,0:T(8,128)(2,1)S(1)} %get-tuple-element.58.refs_1_), channel_id=1, source_target_pairs={{0,24},{8,16},{16,8},{24,0},{1,25},{9,17},{17,9},{25,1},{2,26},{10... | collective-permute-start | bytes 393224 | tf_op jit(solution)/shard_map/ppermute | solution.py:562
  79.9 15.8 %collective-permute-start.38 = (bf16[32,2048]{1,0:T(8,128)(2,1)S(1)}, bf16[32,2048]{1,0:T(8,128)(2,1)S(1)}, u32[]{:S(2)}, u32[]{:S(2)}) collective-permute-start(bf16[32,2048]{1,0:T(8,128)(2,1)S(1)} %get-tuple-element.88.refs_0_), channel_id=1, source_target_pairs={{0,8},{8,0},{16,24},{24,16},{1,9},{9,1},{17,25},{25,17},{2,10},{10... | collective-permute-start | bytes 393224 | tf_op jit(solution)/shard_map/ppermute | solution.py:562
  81.7 15.8 %collective-permute-start.39 = (bf16[32,2048]{1,0:T(8,128)(2,1)S(1)}, bf16[32,2048]{1,0:T(8,128)(2,1)S(1)}, u32[]{:S(2)}, u32[]{:S(2)}) collective-permute-start(bf16[32,2048]{1,0:T(8,128)(2,1)S(1)} %get-tuple-element.88.refs_0_), channel_id=1, source_target_pairs={{0,16},{8,24},{16,0},{24,8},{1,17},{9,25},{17,1},{25,9},{2,18},{10... | collective-permute-start | bytes 393224 | tf_op jit(solution)/shard_map/ppermute | solution.py:562
  81.7 15.8 %collective-permute-start.40 = (bf16[32,2048]{1,0:T(8,128)(2,1)S(1)}, bf16[32,2048]{1,0:T(8,128)(2,1)S(1)}, u32[]{:S(2)}, u32[]{:S(2)}) collective-permute-start(bf16[32,2048]{1,0:T(8,128)(2,1)S(1)} %get-tuple-element.88.refs_0_), channel_id=1, source_target_pairs={{0,24},{8,16},{16,8},{24,0},{1,25},{9,17},{17,9},{25,1},{2,26},{10... | collective-permute-start | bytes 393224 | tf_op jit(solution)/shard_map/ppermute | solution.py:562
  97.6 3.8 %collective-permute-start.41 = (bf16[128,2048]{1,0:T(8,128)(2,1)S(1)}, bf16[128,2048]{1,0:T(8,128)(2,1)S(1)}, u32[]{:S(2)}, u32[]{:S(2)}) collective-permute-start(bf16[128,2048]{1,0:T(8,128)(2,1)S(1)} %stack.10.refs_1_), channel_id=1, source_target_pairs={{0,1},{1,0},{2,3},{3,2},{4,5},{5,4},{6,7},{7,6},{8,9},{9,8},{10,11... | collective-permute-start | bytes 1572872 | tf_op jit(solution)/shard_map/ppermute | solution.py:559
  97.7 16.7 %collective-permute-start.42 = (bf16[128,2048]{1,0:T(8,128)(2,1)S(1)}, bf16[128,2048]{1,0:T(8,128)(2,1)S(1)}, u32[]{:S(2)}, u32[]{:S(2)}) collective-permute-start(bf16[128,2048]{1,0:T(8,128)(2,1)S(1)} %stack.10.refs_1_), channel_id=1, source_target_pairs={{0,2},{1,3},{2,0},{3,1},{4,6},{5,7},{6,4},{7,5},{8,10},{9,11},{10,... | collective-permute-start | bytes 1572872 | tf_op jit(solution)/shard_map/ppermute | solution.py:559
  98.1 16.2 %collective-permute-start.43 = (bf16[128,2048]{1,0:T(8,128)(2,1)S(1)}, bf16[128,2048]{1,0:T(8,128)(2,1)S(1)}, u32[]{:S(2)}, u32[]{:S(2)}) collective-permute-start(bf16[128,2048]{1,0:T(8,128)(2,1)S(1)} %stack.10.refs_1_), channel_id=1, source_target_pairs={{0,4},{1,5},{2,6},{3,7},{4,0},{5,1},{6,2},{7,3},{8,12},{9,13},{10,... | collective-permute-start | bytes 1572872 | tf_op jit(solution)/shard_map/ppermute | solution.py:559
  99.1 8.9 %collective-permute-start.27 = (bf16[272,256]{1,0:T(8,128)(2,1)S(1)}, bf16[272,256]{1,0:T(8,128)(2,1)S(1)}, u32[]{:S(2)}, u32[]{:S(2)}) collective-permute-start(bf16[272,256]{1,0:T(8,128)(2,1)S(1)} %get-tuple-element.71.refs_4_), channel_id=1, source_target_pairs={{0,8},{8,0},{16,24},{24,16},{1,9},{9,1},{17,25},{25,17},{2,10},{10... | collective-permute-start | bytes 417800 | tf_op jit(solution)/shard_map/ppermute | solution.py:562
  101.1 13.3 %collective-permute-start.28 = (bf16[272,256]{1,0:T(8,128)(2,1)S(1)}, bf16[272,256]{1,0:T(8,128)(2,1)S(1)}, u32[]{:S(2)}, u32[]{:S(2)}) collective-permute-start(bf16[272,256]{1,0:T(8,128)(2,1)S(1)} %get-tuple-element.72), channel_id=1, source_target_pairs={{0,16},{8,24},{16,0},{24,8},{1,17},{9,25},{17,1},{25,9},{2,18},{10... | collective-permute-start | bytes 417800 | tf_op jit(solution)/shard_map/ppermute | solution.py:562
  101.4 12.9 %collective-permute-start.29 = (bf16[272,256]{1,0:T(8,128)(2,1)S(1)}, bf16[272,256]{1,0:T(8,128)(2,1)S(1)}, u32[]{:S(2)}, u32[]{:S(2)}) collective-permute-start(bf16[272,256]{1,0:T(8,128)(2,1)S(1)} %get-tuple-element.73), channel_id=1, source_target_pairs={{0,24},{8,16},{16,8},{24,0},{1,25},{9,17},{17,9},{25,1},{2,26},{10... | collective-permute-start | bytes 417800 | tf_op jit(solution)/shard_map/ppermute | solution.py:562
  114.5 3.2 %collective-permute-start.44 = (bf16[128,2048]{1,0:T(8,128)(2,1)S(1)}, bf16[128,2048]{1,0:T(8,128)(2,1)S(1)}, u32[]{:S(2)}, u32[]{:S(2)}) collective-permute-start(bf16[128,2048]{1,0:T(8,128)(2,1)S(1)} %get-tuple-element.89.refs_1_), channel_id=1, source_target_pairs={{0,1},{1,0},{2,3},{3,2},{4,5},{5,4},{6,7},{7,6},{8,9},{9,8},{10,11... | collective-permute-start | bytes 1572872 | tf_op jit(solution)/shard_map/ppermute | solution.py:559
  114.5 7.5 %collective-permute-start.45 = (bf16[128,2048]{1,0:T(8,128)(2,1)S(1)}, bf16[128,2048]{1,0:T(8,128)(2,1)S(1)}, u32[]{:S(2)}, u32[]{:S(2)}) collective-permute-start(bf16[128,2048]{1,0:T(8,128)(2,1)S(1)} %get-tuple-element.90.refs_1_), channel_id=1, source_target_pairs={{0,1},{1,0},{2,3},{3,2},{4,5},{5,4},{6,7},{7,6},{8,9},{9,8},{10,11... | collective-permute-start | bytes 1572872 | tf_op jit(solution)/shard_map/ppermute | solution.py:559
  115.0 11.5 %collective-permute-start.46 = (bf16[64,2048]{1,0:T(8,128)(2,1)S(1)}, bf16[64,2048]{1,0:T(8,128)(2,1)S(1)}, u32[]{:S(2)}, u32[]{:S(2)}) collective-permute-start(bf16[64,2048]{1,0:T(8,128)(2,1)S(1)} %get-tuple-element.91), channel_id=1, source_target_pairs={{0,2},{1,3},{2,0},{3,1},{4,6},{5,7},{6,4},{7,5},{8,10},{9,11},{10,... | collective-permute-start | bytes 786440 | tf_op jit(solution)/shard_map/ppermute | solution.py:559
  116.6 9.9 %collective-permute-start.47 = (bf16[64,2048]{1,0:T(8,128)(2,1)S(1)}, bf16[64,2048]{1,0:T(8,128)(2,1)S(1)}, u32[]{:S(2)}, u32[]{:S(2)}) collective-permute-start(bf16[64,2048]{1,0:T(8,128)(2,1)S(1)} %get-tuple-element.92), channel_id=1, source_target_pairs={{0,4},{1,5},{2,6},{3,7},{4,0},{5,1},{6,2},{7,3},{8,12},{9,13},{10,... | collective-permute-start | bytes 786440 | tf_op jit(solution)/shard_map/ppermute | solution.py:559
  126.6 2.0 %collective-permute-start.48 = (bf16[128,2048]{1,0:T(8,128)(2,1)S(1)}, bf16[128,2048]{1,0:T(8,128)(2,1)S(1)}, u32[]{:S(2)}, u32[]{:S(2)}) collective-permute-start(bf16[128,2048]{1,0:T(8,128)(2,1)S(1)} %stack.11.refs_1_), channel_id=1, source_target_pairs={{0,1},{1,0},{2,3},{3,2},{4,5},{5,4},{6,7},{7,6},{8,9},{9,8},{10,11... | collective-permute-start | bytes 1572872 | tf_op jit(solution)/shard_map/ppermute | solution.py:559
  133.6 1.2 collective-permute-start.49
  134.8 3.7 %collective-permute-start.50 = (f32[8,256]{1,0:T(8,128)S(1)}, f32[8,256]{1,0:T(8,128)S(1)}, u32[]{:S(2)}, u32[]{:S(2)}) collective-permute-start(f32[8,256]{1,0:T(8,128)S(1)} %add_select_fusion.4), channel_id=1, source_target_pairs={{0,2},{1,3},{2,0},{3,1},{4,6},{5,7},{6,4},{7,5},{8,10},{9,11},{10,... | collective-permute-start | bytes 24584 | tf_op jit(solution)/shard_map/ppermute | solution.py:636
  138.6 3.7 %collective-permute-start.51 = (f32[8,256]{1,0:T(8,128)S(1)}, f32[8,256]{1,0:T(8,128)S(1)}, u32[]{:S(2)}, u32[]{:S(2)}) collective-permute-start(f32[8,256]{1,0:T(8,128)S(1)} %add_select_fusion.3), channel_id=1, source_target_pairs={{0,4},{1,5},{2,6},{3,7},{4,0},{5,1},{6,2},{7,3},{8,12},{9,13},{10,... | collective-permute-start | bytes 24584 | tf_op jit(solution)/shard_map/ppermute | solution.py:636
  140.6 4.1 %collective-permute-start.30 = (bf16[128,256]{1,0:T(8,128)(2,1)S(1)}, bf16[128,256]{1,0:T(8,128)(2,1)S(1)}, u32[]{:S(2)}, u32[]{:S(2)}) collective-permute-start(bf16[128,256]{1,0:T(8,128)(2,1)S(1)} %get-tuple-element.75), channel_id=1, source_target_pairs={{0,1},{1,0},{2,3},{3,2},{4,5},{5,4},{6,7},{7,6},{8,9},{9,8},{10,11... | collective-permute-start | bytes 196616 | tf_op jit(solution)/shard_map/ppermute | solution.py:559
  142.3 6.5 %collective-permute-start.52 = (f32[8,256]{1,0:T(8,128)S(1)}, f32[8,256]{1,0:T(8,128)S(1)}, u32[]{:S(2)}, u32[]{:S(2)}) collective-permute-start(f32[8,256]{1,0:T(8,128)S(1)} %add_select_fusion.2), channel_id=1, source_target_pairs={{0,8},{8,0},{16,24},{24,16},{1,9},{9,1},{17,25},{25,17},{2,10},{10... | collective-permute-start | bytes 24584 | tf_op jit(solution)/shard_map/ppermute | solution.py:636
  145.2 5.6 %collective-permute-start.31 = (bf16[32,2048]{1,0:T(8,128)(2,1)S(1)}, bf16[32,2048]{1,0:T(8,128)(2,1)S(1)}, u32[]{:S(2)}, u32[]{:S(2)}) collective-permute-start(bf16[32,2048]{1,0:T(8,128)(2,1)S(1)} %get-tuple-element.77), channel_id=1, source_target_pairs={{0,2},{1,3},{2,0},{3,1},{4,6},{5,7},{6,4},{7,5},{8,10},{9,11},{10,... | collective-permute-start | bytes 393224 | tf_op jit(solution)/shard_map/ppermute | solution.py:559
  145.6 5.6 %collective-permute-start.32 = (bf16[32,2048]{1,0:T(8,128)(2,1)S(1)}, bf16[32,2048]{1,0:T(8,128)(2,1)S(1)}, u32[]{:S(2)}, u32[]{:S(2)}) collective-permute-start(bf16[32,2048]{1,0:T(8,128)(2,1)S(1)} %get-tuple-element.78), channel_id=1, source_target_pairs={{0,4},{1,5},{2,6},{3,7},{4,0},{5,1},{6,2},{7,3},{8,12},{9,13},{10,... | collective-permute-start | bytes 393224 | tf_op jit(solution)/shard_map/ppermute | solution.py:559
  146.7 6.0 %collective-permute-start.33 = (bf16[32,2048]{1,0:T(8,128)(2,1)S(1)}, bf16[32,2048]{1,0:T(8,128)(2,1)S(1)}, u32[]{:S(2)}, u32[]{:S(2)}) collective-permute-start(bf16[32,2048]{1,0:T(8,128)(2,1)S(1)} %get-tuple-element.79), channel_id=1, source_target_pairs={{0,6},{1,7},{2,4},{3,5},{4,2},{5,3},{6,0},{7,1},{8,14},{9,15},{10,... | collective-permute-start | bytes 393224 | tf_op jit(solution)/shard_map/ppermute | solution.py:559
  148.8 4.7 %collective-permute-start.53 = (f32[8,256]{1,0:T(8,128)S(1)}, f32[8,256]{1,0:T(8,128)S(1)}, u32[]{:S(2)}, u32[]{:S(2)}) collective-permute-start(f32[8,256]{1,0:T(8,128)S(1)} %add_select_fusion.1), channel_id=1, source_target_pairs={{0,16},{8,24},{16,0},{24,8},{1,17},{9,25},{17,1},{25,9},{2,18},{10... | collective-permute-start | bytes 24584 | tf_op jit(solution)/shard_map/ppermute | solution.py:636
  (5 other events, 4.4 us)
